TPU v7x, 256 devices: a whole 4x4x8 slice. The times are simulated.
256 devices in a mesh: fsdp: 16 (over z, core), dp: 4 (over y), ctx: 4 (over x).
Axes of the slice: x: 4, y: 4, z: 8, core: 2. Of those that a mesh axis runs over, the one named last changes fastest.
Arguments:
- weights: bfloat16 [4, 512, 8192], P(None, None, 'fsdp'), may hold values from -0.119628906 to 0.119628906
- momentum: bfloat16 [4, 512, 8192], P(None, None, 'fsdp'), may hold values from -400 to 400, as said below
- gradient: bfloat16 [4, 512, 8192], P(None, None, 'fsdp'), may hold values from -400 to 400, as said below
- logit_max: float32 [4, 4, 61, 32], P('dp', 'ctx'), may hold values from 0.2 to 600, as said below
- layer_of: int32 [4], replicated, may hold values from 0 to 60
Outputs:
- new_weights: bfloat16 [4, 512, 8192], P(None, None, 'fsdp')
- new_momentum: bfloat16 [4, 512, 8192], P(None, None, 'fsdp')
Inputs may be any that keep to these rules, and one draw needn't show every extreme that they name: `momentum`: entries of order one to some hundred, rows and columns of different scales. `gradient`: entries of order one to some hundred, rows and columns of different scales. `logit_max`: positive.
All inputs are finite; a program needn't handle non-finite values.
Results may differ from a plain program's by a relative error of at most 0.0062.
Values may be sent and summed in bfloat16 or wider, within the bound.
No kernel may reach another device: no remote copies, remote signals or barrier semaphores. Data moves between devices by JAX's collectives and lax.ppermute only.
A program may use at most 64 MiB of HBM per device.

v0:
```python
import math

import jax
import jax.numpy as jnp
from jax import lax
from jax.sharding import PartitionSpec as P

HEADS = 32
KNOPE = 128
VDIM = 128
LAYERS = 61
ITERS = 5


quintic_a = 3.4445
quintic_b = -4.775
quintic_c = 2.0315
momentum_decay = 0.95
step_size = 0.1
clip_limit = 100.0
norm_eps = 1e-07
rms_factor = 0.2


def gram_of(column_block):
    return lax.dot_general(
        column_block, column_block, (((1,), (1,)), ((), ())), preferred_element_type=jnp.float32
    )


def newton_gram(gram_now):
    highest = lax.Precision.HIGHEST
    identity = jnp.eye(gram_now.shape[0], dtype=jnp.float32)
    factors = identity
    for iteration in range(ITERS):
        square = jnp.dot(gram_now, gram_now, precision=highest)
        factor = quintic_a * identity + quintic_b * gram_now + quintic_c * square
        left_side = jnp.dot(factor, gram_now, precision=highest)
        gram_now = jnp.dot(left_side, factor, precision=highest)
        if iteration == 0:
            factors = factor
        else:
            factors = jnp.dot(factor, factors, precision=highest)
    return factors


def on_device(weights, momentum, gradient, logit_max, layer_of):
    new_momentum = (
        momentum_decay * momentum.astype(jnp.float32) + gradient.astype(jnp.float32)
    ).astype(jnp.bfloat16)
    matrix_count = weights.shape[0]
    rows_count = weights.shape[1]
    shard_cols = weights.shape[2]
    dp_count = lax.axis_size("dp")
    ctx_count = lax.axis_size("ctx")
    quarter = shard_cols // dp_count
    matrix_index = lax.axis_index("ctx")
    shard_index = lax.axis_index("fsdp")
    offset = lax.axis_index("dp") * quarter
    own_rows = lax.dynamic_index_in_dim(new_momentum, matrix_index, 0, keepdims=False)
    own_piece = lax.dynamic_slice_in_dim(own_rows, offset, quarter, 1)
    layer_match = jnp.arange(LAYERS, dtype=jnp.int32)[None, :] == layer_of[:, None]
    peaks = lax.pmax(logit_max[0, 0], ("dp", "ctx"))
    chosen = jnp.sum(jnp.where(layer_match[:, :, None], peaks[None, :, :], 0.0), axis=1)
    matrix_match = jnp.arange(matrix_count, dtype=jnp.int32) == matrix_index
    head_peak = jnp.sum(jnp.where(matrix_match[:, None], chosen, 0.0), axis=0)
    partial_gram = gram_of(lax.all_gather(own_piece, "fsdp", axis=1, tiled=True))
    gram_now = lax.psum(partial_gram, "dp")
    norm_value = jnp.sqrt(jnp.trace(gram_now)) + norm_eps
    factors = newton_gram(gram_now / (norm_value * norm_value))
    scaled = (own_piece.astype(jnp.float32) / norm_value).astype(jnp.bfloat16)
    orthogonal = jnp.dot(factors.astype(jnp.bfloat16), scaled, preferred_element_type=jnp.float32)
    total_cols = shard_cols * lax.axis_size("fsdp")
    update = rms_factor * math.sqrt(max(rows_count, total_cols)) * orthogonal
    columns = shard_index * shard_cols + offset + jnp.arange(quarter, dtype=jnp.int32)
    head_ids = columns // (KNOPE + VDIM)
    key_column = columns % (KNOPE + VDIM) < KNOPE
    head_scale = jnp.sqrt(jnp.minimum(1.0, clip_limit / head_peak))
    head_match = head_ids[:, None] == jnp.arange(HEADS, dtype=jnp.int32)[None, :]
    per_column = jnp.sum(jnp.where(head_match, head_scale[None, :], 0.0), axis=1)
    column_scale = jnp.where(key_column, per_column, 1.0)
    own_weights = lax.dynamic_index_in_dim(weights, matrix_index, 0, keepdims=False)
    weight_piece = lax.dynamic_slice_in_dim(own_weights, offset, quarter, 1)
    fresh_piece = (
        (weight_piece.astype(jnp.float32) - step_size * update) * column_scale[None, :]
    ).astype(jnp.bfloat16)
    gathered_all = lax.all_gather(fresh_piece[None], ("dp", "ctx"), axis=0, tiled=True)
    arranged = gathered_all.reshape(dp_count, ctx_count, rows_count, quarter)
    new_weights = jnp.transpose(arranged, (1, 2, 0, 3)).reshape(
        ctx_count, rows_count, dp_count * quarter
    )
    return (new_weights, new_momentum)


def solution(mesh):
    in_specs = (
        P(None, None, "fsdp"),
        P(None, None, "fsdp"),
        P(None, None, "fsdp"),
        P("dp", "ctx", None, None),
        P(),
    )
    out_specs = (P(None, None, "fsdp"), P(None, None, "fsdp"))
    return jax.shard_map(
        on_device, mesh=mesh, in_specs=in_specs, out_specs=out_specs, check_vma=False
    )
```

profile of v0, /device:TPU:1, one launch (start us, length us, event | category | flops | bytes accessed | tf_op | source)
XLA Modules:
  0.0 227.9 jit_solution(16672405036660512969)
XLA Ops:
  7.2 2.8 %add_convert_fusion = bf16[4,512,512]{2,1,0:T(8,128)(2,1)S(1)} fusion(bf16[4,512,512]{2,1,0:T(8,128)(2,1)} %param.7, bf16[4,512,512]{2,1,0:T(8,128)(2,1)} %param.6), kind=kLoop, calls=%fused_computation | loop fusion | flops 5242880 | bytes 6291456 | tf_op jit(solution)/shard_map/convert_element_type | solution.py:50
  11.1 45.2 %all-gather.5.cloned.1.call-done = bf16[1,512,2048]{2,1,0:T(8,128)(2,1)} async-done(((bf16[1,512,128]{2,1,0:T(8,128)(2,1)}), bf16[1,512,2048]{2,1,0:T(8,128)(2,1)}) %all-gather.5.cloned.1.call-update) | async-done | bytes 2097168 | tf_op jit(solution)/shard_map/all_gather | solution.py:67
  56.3 4.5 %fusion = f32[512,512]{1,0:T(8,128)} fusion(bf16[1,512,2048]{2,1,0:T(8,128)(2,1)} %all-gather.5.cloned.1.call-done), kind=kOutput, calls=%fused_computation.7 | convolution fusion | flops 1073741824 | bytes 3145728 | tf_op jit(solution)/shard_map/dot_general | solution.py:26
  60.9 60.8 %pmax.7 = f32[61,32]{0,1:T(8,128)S(1)} all-reduce(f32[61,32]{0,1:T(8,128)S(1)} %bitcast.51), channel_id=1, replica_groups=mesh['fsdp'=16,'dp'=4,'ctx'=4] {'dp','ctx'}, use_global_device_ids=true, to_apply=%region_2.3 | all-reduce | flops 1952 | bytes 15616 | tf_op jit(solution)/shard_map/pmax | solution.py:63
  122.2 1.9 select_reduce_fusion
  124.8 4.1 %fusion.6 = f32[512,512]{1,0:T(8,128)S(1)} fusion(f32[512,512]{1,0:T(8,128)} %all-reduce.2.cloned.1.call-done, f32[]{:T(128)S(6)} %mul.80), kind=kOutput, calls=%fused_computation.18 | convolution fusion | flops 1612709888 | bytes 2097156 | tf_op jit(solution)/shard_map/dot_general | solution.py:36
  128.9 1.9 fusion.10
  130.7 1.8 fusion.14
  132.6 1.9 fusion.5
  134.5 1.8 fusion.21
  136.3 1.8 fusion.15
  138.2 2.1 fusion.16
  140.3 1.9 fusion.4
  142.2 1.8 fusion.17
  145.9 1.8 fusion.18
  147.8 1.9 fusion.3
  149.7 1.8 fusion.19
  151.5 2.1 fusion.23
  153.7 1.8 fusion.20
  155.5 1.9 fusion.2
  157.4 1.8 convolution_convert_fusion
  159.3 2.0 fusion.9
  161.3 56.8 %all-gather.7.cloned.1.call-done = bf16[8192,128]{1,0:T(8,128)(2,1)} async-done(((bf16[512,128]{1,0:T(8,128)(2,1)}), bf16[8192,128]{1,0:T(8,128)(2,1)}) %all-gather.7.cloned.1.call-update) | async-done | bytes 2097168 | tf_op jit(solution)/shard_map/all_gather | solution.py:87
  218.1 3.3 %copy.12 = bf16[4,4,64,8,128]{4,3,0,2,1:T(8,128)(2,1)} copy(bf16[4,4,64,8,128]{4,3,2,1,0:T(8,128)(2,1)} %bitcast.49) | data formatting | bytes 4194304 | tf_op jit(solution)/shard_map/reshape | solution.py:89
  (25 shorter events, 3.4 us)
Async XLA Ops:
  7.2 49.2 %all-gather.5.cloned.1.call-start = ((), (), s32[]{:S(2)}) async-start(), calls=%async_computation.1 | async-start | bytes 2228224 | tf_op jit(solution)/shard_map/all_gather | solution.py:67
  10.1 149.2 %copy-start = (bf16[4,512,512]{2,1,0:T(8,128)(2,1)}, bf16[4,512,512]{2,1,0:T(8,128)(2,1)S(1)}, u32[]{:S(2)}) copy-start(bf16[4,512,512]{2,1,0:T(8,128)(2,1)S(1)} %add_convert_fusion) | copy-start | bytes 6291460
  11.0 111.1 %all-reduce.2.cloned.1.call-start = ((), (), s32[]{:S(2)}) async-start(), calls=%async_computation | async-start | bytes 2097152 | tf_op jit(solution)/shard_map/psum | solution.py:68
  11.1 49.8 %copy-start.2 = (f32[1,1,61,32]{2,3,1,0:T(8,128)S(1)}, f32[1,1,61,32]{2,3,1,0:T(8,128)}, u32[]{:S(2)}) copy-start(f32[1,1,61,32]{2,3,1,0:T(8,128)} %param.8) | copy-start | bytes 23428
  11.1 110.6 %copy-start.3 = (s32[4]{0:T(128)S(1)}, s32[4]{0:T(128)}, u32[]{:S(2)}) copy-start(s32[4]{0:T(128)} %param.9) | copy-start | bytes 52
  60.8 157.3 %all-gather.7.cloned.1.call-start = ((), (), s32[]{:S(2)}) async-start(), calls=%async_computation.2 | async-start | bytes 2228224 | tf_op jit(solution)/shard_map/all_gather | solution.py:87
  124.8 4.1 %copy-start.1 = (f32[512,512]{1,0:T(8,128)S(1)}, f32[512,512]{1,0:T(8,128)}, u32[]{:S(2)}) copy-start(f32[512,512]{1,0:T(8,128)} %all-reduce.2.cloned.1.call-done) | copy-start | bytes 3145732
Sparse Core Ops, SparseCore 0:
  11.1 45.1 all-gather.4
  60.9 48.7 all-reduce.1
  161.4 56.6 all-gather.6
where the time goes:
time: 228 us
  waiting for transfers between devices  102 us (45%)
  blocking collectives  60.8 us (27%)
  matrix products  40.8 us (18%)
  between operations  14.7 us (6%)
  other arithmetic  5.15 us (2%)
  local copies, waits for them, and re-layouts  4.21 us (2%)
    pmax x1, blocking collectives, on_device(): peaks = lax.pmax(logit_max[0, 0], ('dp', 'ctx'))  60.8 us
    all_gather x1, waiting for transfers between devices, on_device(): lax.all_gather(fresh_piece[None], ('dp', 'ctx'), axis=0, tiled=True)  56.8 us
    all_gather x1, waiting for transfers between devices, on_device(): lax.all_gather(own_piece, 'fsdp', axis=1, tiled=True)  45.2 us
    dot_general x5, matrix products, newton_gram(): square = jnp.dot(gram_now, gram_now, precision=highest)  11.6 us
    dot_general x4, matrix products, newton_gram(): factors = jnp.dot(factor, factors, precision=highest)  7.67 us
    dot_general x4, matrix products, newton_gram(): gram_now = jnp.dot(left_side, factor, precision=highest)  7.63 us
    dot_general x4, matrix products, newton_gram(): left_side = jnp.dot(factor, gram_now, precision=highest)  7.41 us
  transfers between devices with their start and end apart: 3, of which 2 were waited for; matrix products, arithmetic and copies ran while one was open for 0% of the time, Pallas kernels for 0%

commit v1 on v0

v1 whole, which is shorter than its diff:
```python
import functools
import math

import jax
import jax.numpy as jnp
from jax import lax
from jax.experimental import pallas as pl
from jax.experimental.pallas import tpu as pltpu
from jax.sharding import PartitionSpec as P

KNOPE = 128
VDIM = 128
ITERS = 5

quintic_a = 3.4445
quintic_b = -4.775
quintic_c = 2.0315
momentum_decay = 0.95
step_size = 0.1
clip_limit = 100.0
norm_eps = 1e-07
rms_factor = 0.2

BLOCK = 128
BLOCKS = 4
PART = 160
TAIL = 8
HALF = 640
END = 16
UPPER = [(row, column) for row in range(BLOCKS) for column in range(row, BLOCKS)]


def decayed(momentum, gradient):
    return (momentum_decay * momentum.astype(jnp.float32) + gradient.astype(jnp.float32)).astype(jnp.bfloat16)


def aligned(index, to):
    return pl.multiple_of(index * to, to)


def partial_gram_kernel(momentum_ref, gradient_ref, keep_ref, send_ref, momentum, gradient, fresh, packed, arrived):
    matrix, dp_at, core = lax.axis_index("ctx"), lax.axis_index("dp"), lax.rem(lax.axis_index("fsdp"), 2)
    copies = []
    for at in (0, 2, 1):
        rows = pl.ds(aligned(lax.rem(dp_at + at, BLOCKS), BLOCK), BLOCK)
        pair = [
            pltpu.make_async_copy(source.at[matrix, rows], target.at[at], arrived.at[side, at])
            for side, (source, target) in enumerate(((momentum_ref, momentum), (gradient_ref, gradient)))
        ]
        for copy in pair:
            copy.start()
        copies.append((at, pair))
    for at, pair in copies:
        for copy in pair:
            copy.wait()
        fresh[at * BLOCK : (at + 1) * BLOCK, :] = decayed(momentum[at], gradient[at])

    def gram(left, right):
        return lax.dot_general(left, right, (((1,), (1,)), ((), ())), preferred_element_type=jnp.float32)

    early = dp_at < BLOCKS // 2
    far_rows = jnp.where(early, 0, 5)
    far_columns = jnp.where(early, 2, 0)
    packed[2 * BLOCK :, :] = gram(
        fresh[pl.ds(aligned(far_rows, BLOCK // 2), BLOCK // 2), :], fresh[pl.ds(aligned(far_columns, BLOCK), BLOCK), :]
    )
    packed[0:BLOCK, :] = gram(fresh[0:BLOCK, :], fresh[0:BLOCK, :])
    packed[BLOCK : 2 * BLOCK, :] = gram(fresh[0:BLOCK, :], fresh[BLOCK : 2 * BLOCK, :])
    keep_ref[...] = packed[pl.ds(aligned(core, PART), PART), :]
    send_ref[...] = packed[pl.ds(aligned(1 - core, PART), PART), :]


def partial_gram(momentum, gradient):
    rank, cols = momentum.shape[1:]
    shape = jax.ShapeDtypeStruct((PART, BLOCK), jnp.float32)
    blocks = pltpu.VMEM((3, BLOCK, cols), jnp.bfloat16)
    return pl.pallas_call(
        partial_gram_kernel,
        out_shape=(shape, shape),
        in_specs=[pl.BlockSpec(memory_space=pl.ANY)] * 2,
        out_specs=(pl.BlockSpec(memory_space=pltpu.VMEM),) * 2,
        scratch_shapes=[
            blocks,
            blocks,
            pltpu.VMEM((3 * BLOCK, cols), jnp.bfloat16),
            pltpu.VMEM((2 * PART, BLOCK), jnp.float32),
            pltpu.SemaphoreType.DMA((2, 3)),
        ],
        compiler_params=pltpu.CompilerParams(vmem_limit_bytes=62 * 2**20),
        cost_estimate=pl.CostEstimate(flops=4 * PART * BLOCK * cols, bytes_accessed=3 * rank * cols, transcendentals=0),
    )(momentum, gradient)


def split_in_two(value):
    high = value.astype(jnp.bfloat16)
    return high, (value - high.astype(jnp.float32)).astype(jnp.bfloat16)


def split_in_three(value):
    high = value.astype(jnp.bfloat16)
    rest = value - high.astype(jnp.float32)
    middle = rest.astype(jnp.bfloat16)
    return high, middle, (rest - middle.astype(jnp.float32)).astype(jnp.bfloat16)


def newton_kernel(*refs):
    (own, near, cross, far), rest = [refs[2 * at : 2 * at + 2] for at in range(BLOCKS)], refs[2 * BLOCKS :]
    first_ref, second_ref, peaks_ref, packed, stacks, a_now, pairs_q, pair_a, pair_b, pair_p = rest
    rank = pair_a.shape[1]
    mid = rank // 2
    dp_at, core = lax.axis_index("dp"), lax.rem(lax.axis_index("fsdp"), 2)
    for turn, pair in ((0, own), (1 + 2 * core, near), (3 - 2 * core, cross), (2, far)):
        for side, piece in enumerate(pair):
            half = core + side - 2 * core * side
            stacks[dp_at ^ turn, pl.ds(aligned(half, PART), PART), :] = piece[0:PART, :]
    peaks = jnp.maximum(jnp.maximum(own[0][PART:, :], near[0][PART:, :]), jnp.maximum(cross[0][PART:, :], far[0][PART:, :]))
    peaks_ref[...] = peaks

    def own_block(block):
        return stacks[block, 0:BLOCK, :]

    def beside(block):
        return stacks[block, BLOCK : 2 * BLOCK, :]

    eye = lax.broadcasted_iota(jnp.int32, (BLOCK, BLOCK), 0) == lax.broadcasted_iota(jnp.int32, (BLOCK, BLOCK), 1)
    diagonal = (own_block(0) + own_block(1)) + (own_block(2) + own_block(3))
    norm = jnp.sqrt(jnp.full((1, 1), jnp.sum(jnp.where(eye, diagonal, 0.0)), jnp.float32)) + norm_eps
    inverse = 1.0 / (norm * norm)

    def place(row, column, value):
        a_now[row * BLOCK : (row + 1) * BLOCK, column * BLOCK : (column + 1) * BLOCK] = value

    for block in range(BLOCKS):
        place(block, block, own_block(block) * inverse)
        after = (block + 1) % BLOCKS
        place(block, after, beside(block) * inverse)
        place(after, block, beside(block).T * inverse)
    for block in range(2):
        far_block = jnp.concatenate([stacks[block, 2 * BLOCK :, :], stacks[block + 2, 2 * BLOCK :, :]], axis=0) * inverse
        place(block, block + 2, far_block)
        place(block + 2, block, far_block.T)

    strips = [slice(0, mid), slice(mid, rank)]
    rows_at = lax.broadcasted_iota(jnp.int32, (rank, mid), 0)
    columns_at = lax.broadcasted_iota(jnp.int32, (rank, mid), 1)
    shifts = [jnp.where(rows_at == columns_at + strip.start, quintic_a, 0.0) for strip in strips]
    dot = functools.partial(jnp.dot, preferred_element_type=jnp.float32)

    def keep(pair, strip, value):
        pair[0, :, strip], pair[1, :, strip] = split_in_two(value)

    def product(left, right, strip):
        return dot(left[0], right[0, :, strip]) + (dot(left[0], right[1, :, strip]) + dot(left[1], right[0, :, strip]))

    for strip in strips:
        keep(pair_a, strip, a_now[:, strip])
    for iteration in range(ITERS):
        pair_q = pairs_q.at[iteration % 2]
        for strip, shift in zip(strips, shifts):
            square = product(pair_a, pair_a, strip)
            keep(pair_q, strip, shift + quintic_b * a_now[:, strip] + quintic_c * square)
        if iteration == ITERS - 1:
            break
        for strip in strips:
            keep(pair_b, strip, product(pair_q, pair_a, strip))
        if iteration == 0:
            pair_p[...] = pair_q[...]
        else:
            keep(pair_p, strips[0], product(pair_q, pair_p, strips[0]))
        for strip in strips:
            a_now[:, strip] = product(pair_q, pair_b, strip)
            keep(pair_a, strip, a_now[:, strip])
        if iteration > 0:
            keep(pair_p, strips[1], product(pair_q, pair_p, strips[1]))
    for strip in strips:
        a_now[:, strip] = product(pair_q, pair_p, strip)
    for at, (row, column) in enumerate(UPPER):
        block = a_now[row * BLOCK : (row + 1) * BLOCK, column * BLOCK : (column + 1) * BLOCK]
        at_row = at % (HALF // BLOCK) * BLOCK
        packed[at // (HALF // BLOCK), at_row : at_row + BLOCK, :] = block.astype(jnp.bfloat16)
    line = lax.broadcasted_iota(jnp.int32, (END, BLOCK), 0)
    spread = jnp.zeros((END, BLOCK), jnp.float32)
    for at, term in enumerate(split_in_three(norm)):
        spread = jnp.where(line == at, term.astype(jnp.float32), spread)
    for half in range(2):
        packed[half, HALF:, :] = spread.astype(jnp.bfloat16)
    first_ref[...] = packed[core]
    second_ref[...] = packed[1 - core]


def newton(parts, rank):
    whole = pl.BlockSpec(memory_space=pltpu.VMEM)
    pair = pltpu.VMEM((2, rank, rank), jnp.bfloat16)
    piece = jax.ShapeDtypeStruct((HALF + END, BLOCK), jnp.bfloat16)
    return pl.pallas_call(
        newton_kernel,
        out_shape=(piece, piece, jax.ShapeDtypeStruct((TAIL, BLOCK), jnp.float32)),
        in_specs=[whole] * len(parts),
        out_specs=(whole,) * 3,
        scratch_shapes=[
            pltpu.VMEM((2, HALF + END, BLOCK), jnp.bfloat16),
            pltpu.VMEM((BLOCKS, 2 * PART, BLOCK), jnp.float32),
            pltpu.VMEM((rank, rank), jnp.float32),
            pltpu.VMEM((2, 2, rank, rank), jnp.bfloat16),
            pair,
            pair,
            pair,
        ],
        compiler_params=pltpu.CompilerParams(vmem_limit_bytes=40 * 2**20),
        cost_estimate=pl.CostEstimate(flops=17 * 6 * rank**3, bytes_accessed=6 * rank * rank, transcendentals=0),
    )(*parts)


def last_kernel(update_scale, masks, weights_ref, momentum_ref, peaks_ref, first_ref, second_ref, *refs):
    out_ref, packed, factors, weights, momentum, fresh, arrived, left = refs[-8:]
    rank, cols = fresh.shape
    shard = lax.axis_index("fsdp")
    core = lax.rem(shard, 2)
    matrix = lax.axis_index("ctx") ^ (masks[0] + (masks[1] - masks[0]) * core)
    loads = [
        pltpu.make_async_copy(source.at[matrix], target, arrived.at[at])
        for at, (source, target) in enumerate(((momentum_ref, momentum), (weights_ref, weights)))
    ]
    for load in loads:
        load.start()
    packed[core] = first_ref[...]
    packed[1 - core] = second_ref[...]
    for at, (row, column) in enumerate(UPPER):
        at_row = at % (HALF // BLOCK) * BLOCK
        block = packed[at // (HALF // BLOCK), at_row : at_row + BLOCK, :]
        factors[row * BLOCK : (row + 1) * BLOCK, column * BLOCK : (column + 1) * BLOCK] = block
        if row != column:
            factors[column * BLOCK : (column + 1) * BLOCK, row * BLOCK : (row + 1) * BLOCK] = block.T
    end = first_ref[HALF:, :].astype(jnp.float32)
    norm = (end[0:1, 0:1] + end[1:2, 0:1]) + end[2:3, 0:1]
    heads = cols // (KNOPE + VDIM)
    column = lax.broadcasted_iota(jnp.int32, (1, cols), 1)
    lane = lax.broadcasted_iota(jnp.int32, (1, BLOCK), 1)
    column_peaks = jnp.full((1, cols), clip_limit, jnp.float32)
    for head in range(heads):
        place = matrix * (BLOCK // BLOCKS) + shard * heads + head
        peak = jnp.max(jnp.where(lane == place, peaks_ref[0:1, :], 0.0), axis=1, keepdims=True)
        first = head * (KNOPE + VDIM)
        column_peaks = jnp.where((column >= first) & (column < first + KNOPE), peak, column_peaks)
    scale = jnp.sqrt(jnp.minimum(1.0, clip_limit / column_peaks))
    loads[0].wait()
    momentum[...] = (momentum[...].astype(jnp.float32) / norm).astype(jnp.bfloat16)
    loads[1].wait()
    stores = []
    for at in range(BLOCKS):
        rows = slice(at * BLOCK, (at + 1) * BLOCK)
        orthogonal = jnp.dot(factors[rows, :], momentum[...], preferred_element_type=jnp.float32)
        value = (weights[rows, :].astype(jnp.float32) - step_size * (update_scale * orthogonal)) * scale
        fresh[rows, :] = value.astype(jnp.bfloat16)
        stores.append(pltpu.make_async_copy(fresh.at[rows], out_ref.at[matrix, rows], left.at[at]))
        stores[-1].start()
    for store in stores:
        store.wait()


def last_product(update_scale, masks, weights, momentum, peaks, pair, before):
    rank, cols = weights.shape[1:]
    whole, outside = pl.BlockSpec(memory_space=pltpu.VMEM), pl.BlockSpec(memory_space=pl.ANY)
    earlier = [] if before is None else [before]
    square, block = pltpu.VMEM((rank, rank), jnp.bfloat16), pltpu.VMEM((rank, cols), jnp.bfloat16)
    return pl.pallas_call(
        functools.partial(last_kernel, update_scale, masks),
        out_shape=jax.ShapeDtypeStruct(weights.shape, jnp.bfloat16),
        in_specs=[outside] * 2 + [whole] * 3 + [outside] * len(earlier),
        out_specs=outside,
        scratch_shapes=[
            pltpu.VMEM((2, HALF + END, BLOCK), jnp.bfloat16),
            square,
            block,
            block,
            block,
            pltpu.SemaphoreType.DMA((2,)),
            pltpu.SemaphoreType.DMA((BLOCKS,)),
        ],
        input_output_aliases={5: 0} if earlier else {},
        compiler_params=pltpu.CompilerParams(vmem_limit_bytes=24 * 2**20),
        cost_estimate=pl.CostEstimate(flops=2 * rank * rank * cols, bytes_accessed=6 * rank * cols, transcendentals=0),
    )(weights, momentum, peaks, *pair, *earlier)


def crossed(value, axis, mask):
    return lax.ppermute(value, axis, [(at, at ^ mask) for at in range(lax.axis_size(axis))])


def along_z(value, masks):
    pairs = [(at, (at // 2 ^ masks[at % 2]) * 2 + at % 2) for at in range(lax.axis_size("fsdp"))]
    return lax.ppermute(value, "fsdp", pairs)


def by_core(value, axis, masks):
    count = lax.axis_size(axis)
    pairs = [
        (shard * count + at, shard * count + (at ^ masks[shard % 2]))
        for shard in range(lax.axis_size("fsdp"))
        for at in range(count)
    ]
    return lax.ppermute(value, ("fsdp", axis), pairs)


def swapped(value):
    return crossed(value, "fsdp", 1)


def gather_halves(axis, half):
    near, cross = by_core(half, axis, (1, 3)), by_core(half, axis, (3, 1))
    far = by_core(near, axis, (3, 1))
    return (half, swapped(half)), (near, swapped(cross)), (cross, swapped(near)), (far, swapped(far))


def on_device(weights, momentum, gradient, logit_max, layer_of):
    rank, cols = weights.shape[1:]
    fsdp = lax.axis_size("fsdp")
    layers = logit_max.shape[2]

    keep, send = partial_gram(momentum, gradient)
    total = keep + swapped(send)

    layer_match = jnp.arange(layers, dtype=jnp.int32)[None, :] == layer_of[:, None]
    peaks = jnp.max(jnp.where(layer_match[:, :, None], logit_max[0, 0][None], 0.0), axis=1)
    peaks = jnp.broadcast_to(peaks.reshape(1, BLOCK), (TAIL, BLOCK))
    total = total + along_z(total, (1, 7))
    total = total + along_z(total, (3, 1))
    peaks = jnp.maximum(peaks, crossed(peaks, "ctx", 1))
    total, peaks = lax.optimization_barrier((total, peaks))
    total = total + along_z(total, (7, 3))
    peaks = jnp.maximum(peaks, crossed(peaks, "ctx", 3))
    new_momentum = decayed(momentum, gradient)
    total, new_momentum = lax.optimization_barrier((total, new_momentum))

    parts = gather_halves("dp", jnp.concatenate([total, peaks], axis=0))

    first, second, peaks = newton([piece for pair in parts for piece in pair], rank)
    update_scale = rms_factor * math.sqrt(max(rank, cols * fsdp))
    last = functools.partial(last_product, update_scale)
    near = tuple(by_core(piece, "ctx", (1, 3)) for piece in (first, second))
    new_weights = last((0, 0), weights, new_momentum, peaks, (first, second), None)
    near_first, new_weights = lax.optimization_barrier((near[0], new_weights))
    far = by_core(near_first, "ctx", (3, 1))
    cross = swapped(near[1]), swapped(near_first)
    new_weights = last((1, 3), weights, new_momentum, peaks, (near_first, near[1]), new_weights)
    far, new_weights = lax.optimization_barrier((far, new_weights))
    far = far, swapped(far)
    new_weights = last((3, 1), weights, new_momentum, peaks, cross, new_weights)
    new_weights = last((2, 2), weights, new_momentum, peaks, far, new_weights)
    return (new_weights, new_momentum)


def solution(mesh):
    in_specs = (
        P(None, None, "fsdp"),
        P(None, None, "fsdp"),
        P(None, None, "fsdp"),
        P("dp", "ctx", None, None),
        P(),
    )
    out_specs = (P(None, None, "fsdp"), P(None, None, "fsdp"))
    return jax.shard_map(
        on_device, mesh=mesh, in_specs=in_specs, out_specs=out_specs, check_vma=False
    )
```

time: 228 us -> 72.5 us (0.32)
  waiting for transfers between devices: 102 us -> 12.6 us
  blocking collectives: 60.8 us -> 0 us
  matrix products: 40.8 us -> 0 us
  starting transfers between devices: 0.12 us -> 31.4 us
  Pallas kernels: 0 us -> 23.3 us
  between operations: 14.7 us -> 0.96 us
  local copies, waits for them, and re-layouts: 4.21 us -> 0.11 us
    all_gather x2 -> x0, waiting for transfers between devices: 102 us -> none  [the longest x1 56.8 us: on_device(): lax.all_gather(fresh_piece[None], ('dp', 'ctx'), axis=0, tiled=True)]
    pmax x1 -> x0, blocking collectives: 60.8 us -> none  [on_device(): peaks = lax.pmax(logit_max[0, 0], ('dp', 'ctx'))]
    dot_general x19 -> x0, matrix products: 40.8 us -> none  [the longest x5 11.6 us: newton_gram(): square = jnp.dot(gram_now, gram_now, precision=highest)]
    ppermute x0 -> x19, starting transfers between devices: none -> 31.4 us  [the longest x10 19.8 us: crossed(): lax.ppermute(value, axis, [(at, at ^ mask) for at in range(lax.axis_size(...]
    pallas_call x0 -> x6, Pallas kernels: none -> 23.3 us  [the longest x1 14.7 us: newton(): pl.pallas_call(newton_kernel, out_shape=(piece, piece, jax.ShapeDtypeStru...]
    ppermute x0 -> x19, waiting for transfers between devices: none -> 12.6 us  [the longest x3 5.84 us: along_z(): return lax.ppermute(value, 'fsdp', pairs)]
    reshape x1 -> x0, local copies, waits for them, and re-layouts: 3.29 us -> none  [on_device(): jnp.transpose(arranged, (1, 2, 0, 3))]
  transfers between devices with their start and end apart: 3 -> 19, of which waited for: 2 -> 9; matrix products, arithmetic and copies ran while one was open for 0% -> 4% of each run, Pallas kernels for 0% -> 7%
where the time goes in v1:
time: 72.5 us; the launch traced here: 72.4 us
  starting transfers between devices  31.4 us (43%)
  Pallas kernels  23.3 us (32%)
  waiting for transfers between devices  12.6 us (17%)
  other arithmetic  3.97 us (5%)
  between operations  0.96 us (1%)
    ppermute x10, starting transfers between devices, crossed(): lax.ppermute(value, axis, [(at, at ^ mask) for at in range(lax.axis_size(...  19.8 us
    pallas_call x1, Pallas kernels, newton(): pl.pallas_call(newton_kernel, out_shape=(piece, piece, jax.ShapeDtypeStru...  14.7 us
    pallas_call x4, Pallas kernels, last_product(): pl.pallas_call(functools.partial(last_kernel, update_scale, masks), out_s...  6.35 us
    ppermute x3, starting transfers between devices, along_z(): return lax.ppermute(value, 'fsdp', pairs)  6.04 us
    ppermute x3, waiting for transfers between devices, along_z(): return lax.ppermute(value, 'fsdp', pairs)  5.84 us
    ppermute x6, starting transfers between devices, by_core(): return lax.ppermute(value, ('fsdp', axis), pairs)  5.6 us
    ppermute x6, waiting for transfers between devices, by_core(): return lax.ppermute(value, ('fsdp', axis), pairs)  4.75 us
    convert_element_type x1, other arithmetic, decayed(): (momentum_decay * momentum.astype(jnp.float32) + gradient.astype(jnp.floa...  2.85 us
  transfers between devices with their start and end apart: 19, of which 9 were waited for; matrix products, arithmetic and copies ran while one was open for 4% of the time, Pallas kernels for 7%

profile of v1, /device:TPU:1, one launch (start us, length us, event | category | flops | bytes accessed | tf_op | source)
XLA Modules:
  0.0 72.4 jit_solution(17872088040361871451)
XLA Ops:
  0.6 2.3 %shard_map.68 = (f32[160,128]{1,0:T(8,128)}, f32[160,128]{1,0:T(8,128)}) custom-call(bf16[4,512,512]{2,1,0:T(8,128)(2,1)} %momentum_ref.1, bf16[4,512,512]{2,1,0:T(8,128)(2,1)} %gradient_ref.1), custom_call_target="tpu_custom_call" | custom-call | flops 41943040 | bytes 786432 | tf_op jit(solution)/shard_map/pallas_call | solution.py:77
  2.9 3.3 %collective-permute-start = (f32[160,128]{1,0:T(8,128)}, f32[160,128]{1,0:T(8,128)S(1)}, u32[]{:S(2)}, u32[]{:S(2)}) collective-permute-start(f32[160,128]{1,0:T(8,128)} %get-tuple-element.16), channel_id=1, source_target_pairs={{0,16},{16,0},{32,48},{48,32},{64,80},{80,64},{96,112},{112,96},{1... | collective-permute-start | bytes 245768 | tf_op jit(solution)/shard_map/ppermute | solution.py:287
  6.3 1.1 %collective-permute-done = f32[160,128]{1,0:T(8,128)S(1)} collective-permute-done((f32[160,128]{1,0:T(8,128)}, f32[160,128]{1,0:T(8,128)S(1)}, u32[]{:S(2)}, u32[]{:S(2)}) %collective-permute-start) | collective-permute-done | bytes 81952 | tf_op jit(solution)/shard_map/ppermute | solution.py:287
  8.3 3.9 %collective-permute-start.1 = (f32[160,128]{1,0:T(8,128)S(1)}, f32[160,128]{1,0:T(8,128)S(1)}, u32[]{:S(2)}, u32[]{:S(2)}) collective-permute-start(f32[160,128]{1,0:T(8,128)S(1)} %add.15), channel_id=1, source_target_pairs={{0,32},{16,240},{32,0},{48,208},{64,96},{80,176},{96,64},{112,144}... | collective-permute-start | bytes 245768 | tf_op jit(solution)/shard_map/ppermute | solution.py:292
  12.4 1.2 %collective-permute-start.3 = (f32[8,128]{1,0:T(8,128)S(1)}, f32[8,128]{1,0:T(8,128)S(1)}, u32[]{:S(2)}, u32[]{:S(2)}) collective-permute-start(f32[8,128]{1,0:T(8,128)S(1)} %broadcast_in_dim.37), channel_id=1, source_target_pairs={{0,1},{1,0},{2,3},{3,2},{4,5},{5,4},{6,7},{7,6},{8,9},{9,8},{10,11... | collective-permute-start | bytes 12296 | tf_op jit(solution)/shard_map/ppermute | solution.py:287
  13.6 1.3 %collective-permute-done.1 = f32[160,128]{1,0:T(8,128)S(1)} collective-permute-done((f32[160,128]{1,0:T(8,128)S(1)}, f32[160,128]{1,0:T(8,128)S(1)}, u32[]{:S(2)}, u32[]{:S(2)}) %collective-permute-start.1) | collective-permute-done | bytes 81952 | tf_op jit(solution)/shard_map/ppermute | solution.py:292
  15.9 3.5 %collective-permute-done.2 = f32[160,128]{1,0:T(8,128)S(1)} collective-permute-done((f32[160,128]{1,0:T(8,128)S(1)}, f32[160,128]{1,0:T(8,128)S(1)}, u32[]{:S(2)}, u32[]{:S(2)}) %collective-permute-start.2) | collective-permute-done | bytes 81952 | tf_op jit(solution)/shard_map/ppermute | solution.py:292
  19.4 1.9 %collective-permute-start.5 = (f32[8,128]{1,0:T(8,128)S(1)}, f32[8,128]{1,0:T(8,128)S(1)}, u32[]{:S(2)}, u32[]{:S(2)}) collective-permute-start(f32[8,128]{1,0:T(8,128)S(1)} %broadcast_maximum_fusion), channel_id=1, source_target_pairs={{0,3},{1,2},{2,1},{3,0},{4,7},{5,6},{6,5},{7,4},{8,11},{9,10},{10,... | collective-permute-start | bytes 12296 | tf_op jit(solution)/shard_map/ppermute | solution.py:287
  21.3 1.2 %collective-permute-start.4 = (f32[160,128]{1,0:T(8,128)S(1)}, f32[160,128]{1,0:T(8,128)S(1)}, u32[]{:S(2)}, u32[]{:S(2)}) collective-permute-start(f32[160,128]{1,0:T(8,128)S(1)} %add.17), channel_id=1, source_target_pairs={{0,224},{16,112},{32,192},{48,80},{64,160},{80,48},{96,128},{112,1... | collective-permute-start | bytes 245768 | tf_op jit(solution)/shard_map/ppermute | solution.py:292
  22.5 2.8 %add_convert_fusion.momentum_ref = bf16[4,512,512]{2,1,0:T(8,128)(2,1)S(1)} fusion(bf16[4,512,512]{2,1,0:T(8,128)(2,1)} %gradient_ref.1, bf16[4,512,512]{2,1,0:T(8,128)(2,1)} %momentum_ref.1), kind=kLoop, calls=%fused_computation | loop fusion | flops 5242880 | bytes 6291456 | tf_op jit(solution)/shard_map/convert_element_type | solution.py:34
  25.4 1.0 %collective-permute-done.4 = f32[160,128]{1,0:T(8,128)S(1)} collective-permute-done((f32[160,128]{1,0:T(8,128)S(1)}, f32[160,128]{1,0:T(8,128)S(1)}, u32[]{:S(2)}, u32[]{:S(2)}) %collective-permute-start.4) | collective-permute-done | bytes 81952 | tf_op jit(solution)/shard_map/ppermute | solution.py:292
  26.5 2.8 %collective-permute-start.7 = (f32[168,128]{1,0:T(8,128)S(1)}, f32[168,128]{1,0:T(8,128)S(1)}, u32[]{:S(2)}, u32[]{:S(2)}) collective-permute-start(f32[168,128]{1,0:T(8,128)S(1)} %pad_maximum_fusion.refs_0_), channel_id=1, source_target_pairs={{0,4},{4,0},{8,12},{12,8},{16,28},{20,24},{24,20},{28,16},{32,36},... | collective-permute-start | bytes 258056 | tf_op jit(solution)/shard_map/ppermute | solution.py:302
  29.3 1.9 %collective-permute-done.7.refs_2_ = f32[168,128]{1,0:T(8,128)S(1)} collective-permute-done((f32[168,128]{1,0:T(8,128)S(1)}, f32[168,128]{1,0:T(8,128)S(1)}, u32[]{:S(2)}, u32[]{:S(2)}) %collective-permute-start.7) | collective-permute-done | bytes 86048 | tf_op jit(solution)/shard_map/ppermute | solution.py:302
  31.2 7.2 %collective-permute-start.6 = (f32[168,128]{1,0:T(8,128)S(1)}, f32[168,128]{1,0:T(8,128)S(1)}, u32[]{:S(2)}, u32[]{:S(2)}) collective-permute-start(f32[168,128]{1,0:T(8,128)S(1)} %pad_maximum_fusion.refs_0_), channel_id=1, source_target_pairs={{0,16},{16,0},{32,48},{48,32},{64,80},{80,64},{96,112},{112,96},{1... | collective-permute-start | bytes 258056 | tf_op jit(solution)/shard_map/ppermute | solution.py:287
  38.9 2.1 %collective-permute-start.12 = (f32[168,128]{1,0:T(8,128)S(1)}, f32[168,128]{1,0:T(8,128)S(1)}, u32[]{:S(2)}, u32[]{:S(2)}) collective-permute-start(f32[168,128]{1,0:T(8,128)S(1)} %collective-permute-done.11.refs_6_), channel_id=1, source_target_pairs={{0,16},{16,0},{32,48},{48,32},{64,80},{80,64},{96,112},{112,96},{1... | collective-permute-start | bytes 258056 | tf_op jit(solution)/shard_map/ppermute | solution.py:287
  41.9 14.7 %shard_map.69 = (bf16[656,128]{1,0:T(8,128)(2,1)S(1)}, bf16[656,128]{1,0:T(8,128)(2,1)S(1)}, f32[8,128]{1,0:T(8,128)S(1)}) custom-call(f32[168,128]{1,0:T(8,128)S(1)} %pad_maximum_fusion.refs_0_, f32[168,128]{1,0:T(8,128)S(1)} %collective-permute-done.6.refs_1_, f32[168,128]{1,0:T(8,128)S(1)} %collective-permute-done.7.refs_2_, ...), custom_call_target="tpu_custom_call" | custom-call | flops 13690208256 | bytes 1572864 | tf_op jit(solution)/shard_map/pallas_call | solution.py:195
  56.8 2.6 %collective-permute-start.15 = (bf16[656,128]{1,0:T(8,128)(2,1)S(1)}, bf16[656,128]{1,0:T(8,128)(2,1)S(1)}, u32[]{:S(2)}, u32[]{:S(2)}) collective-permute-start(bf16[656,128]{1,0:T(8,128)(2,1)S(1)} %get-tuple-element.23.second_ref), channel_id=1, source_target_pairs={{0,1},{1,0},{2,3},{3,2},{16,19},{17,18},{18,17},{19,16},{32,33},{3... | collective-permute-start | bytes 503816 | tf_op jit(solution)/shard_map/ppermute | solution.py:302
  59.4 1.6 %shard_map.70.refs_0_ = bf16[4,512,512]{2,1,0:T(8,128)(2,1)} custom-call(bf16[4,512,512]{2,1,0:T(8,128)(2,1)S(1)} %copy-done.1, bf16[4,512,512]{2,1,0:T(8,128)(2,1)S(1)} %add_convert_fusion.momentum_ref, f32[8,128]{1,0:T(8,128)S(1)} %get-tuple-element.21.peaks_ref, bf16[656,128]{1,0:T(8,128)(2,1)S(1)} %get-tuple-element.22.first_ref, ...), custom_call_target="tpu_custom_call" | custom-call | flops 268435456 | bytes 1572864 | tf_op jit(solution)/shard_map/pallas_call | solution.py:266
  61.0 1.1 %collective-permute-done.13.first_ref = bf16[656,128]{1,0:T(8,128)(2,1)S(1)} collective-permute-done((bf16[656,128]{1,0:T(8,128)(2,1)S(1)}, bf16[656,128]{1,0:T(8,128)(2,1)S(1)}, u32[]{:S(2)}, u32[]{:S(2)}) %collective-permute-start.13) | collective-permute-done | bytes 167968 | tf_op jit(solution)/shard_map/ppermute | solution.py:302
  62.7 1.2 %collective-permute-done.15.second_ref = bf16[656,128]{1,0:T(8,128)(2,1)S(1)} collective-permute-done((bf16[656,128]{1,0:T(8,128)(2,1)S(1)}, bf16[656,128]{1,0:T(8,128)(2,1)S(1)}, u32[]{:S(2)}, u32[]{:S(2)}) %collective-permute-start.15) | collective-permute-done | bytes 167968 | tf_op jit(solution)/shard_map/ppermute | solution.py:302
  64.2 1.6 %shard_map.71.refs_0_ = bf16[4,512,512]{2,1,0:T(8,128)(2,1)} custom-call(bf16[4,512,512]{2,1,0:T(8,128)(2,1)S(1)} %copy-done.1, bf16[4,512,512]{2,1,0:T(8,128)(2,1)S(1)} %add_convert_fusion.momentum_ref, f32[8,128]{1,0:T(8,128)S(1)} %get-tuple-element.21.peaks_ref, ...), custom_call_target="tpu_custom_call", output_to_operand_aliasing={{}: (5, {})} | custom-call | flops 268435456 | bytes 1572864 | tf_op jit(solution)/shard_map/pallas_call | solution.py:266
  66.3 2.6 %collective-permute-start.16 = (bf16[656,128]{1,0:T(8,128)(2,1)S(1)}, bf16[656,128]{1,0:T(8,128)(2,1)S(1)}, u32[]{:S(2)}, u32[]{:S(2)}) collective-permute-start(bf16[656,128]{1,0:T(8,128)(2,1)S(1)} %collective-permute-done.14.first_ref), channel_id=1, source_target_pairs={{0,16},{16,0},{32,48},{48,32},{64,80},{80,64},{96,112},{112,96},{1... | collective-permute-start | bytes 503816 | tf_op jit(solution)/shard_map/ppermute | solution.py:287
  69.0 1.6 %shard_map.72.refs_0_ = bf16[4,512,512]{2,1,0:T(8,128)(2,1)} custom-call(bf16[4,512,512]{2,1,0:T(8,128)(2,1)S(1)} %copy-done.1, bf16[4,512,512]{2,1,0:T(8,128)(2,1)S(1)} %add_convert_fusion.momentum_ref, f32[8,128]{1,0:T(8,128)S(1)} %get-tuple-element.21.peaks_ref, ...), custom_call_target="tpu_custom_call", output_to_operand_aliasing={{}: (5, {})} | custom-call | flops 268435456 | bytes 1572864 | tf_op jit(solution)/shard_map/pallas_call | solution.py:266
  70.6 1.6 %shard_map.73 = bf16[4,512,512]{2,1,0:T(8,128)(2,1)} custom-call(bf16[4,512,512]{2,1,0:T(8,128)(2,1)S(1)} %copy-done.1, bf16[4,512,512]{2,1,0:T(8,128)(2,1)S(1)} %add_convert_fusion.momentum_ref, f32[8,128]{1,0:T(8,128)S(1)} %get-tuple-element.21.peaks_ref, bf16[656,128]{1,0:T(8,128)(2,1)S(1)} %collective-permute-done.14.first_ref, ...), custom_call_target="tpu_custom_call", output_to_operand_aliasing={{}: (5, {})} | custom-call | flops 268435456 | bytes 1572864 | tf_op jit(solution)/shard_map/pallas_call | solution.py:266
  (40 shorter events, 5.2 us)
Async XLA Ops:
  0.6 5.6 %copy-start.3 = (s32[4]{0:T(128)S(1)}, s32[4]{0:T(128)}, u32[]{:S(2)}) copy-start(s32[4]{0:T(128)} %param.9) | copy-start | bytes 52
  0.6 11.6 %copy-start.2 = (f32[1,1,61,32]{2,3,1,0:T(8,128)S(1)}, f32[1,1,61,32]{2,3,1,0:T(8,128)}, u32[]{:S(2)}) copy-start(f32[1,1,61,32]{2,3,1,0:T(8,128)} %param.8) | copy-start | bytes 23428
  2.9 4.5 %collective-permute-start = (f32[160,128]{1,0:T(8,128)}, f32[160,128]{1,0:T(8,128)S(1)}, u32[]{:S(2)}, u32[]{:S(2)}) collective-permute-start(f32[160,128]{1,0:T(8,128)} %get-tuple-element.16), channel_id=1, source_target_pairs={{0,16},{16,0},{32,48},{48,32},{64,80},{80,64},{96,112},{112,96},{1... | collective-permute-start | bytes 245768 | tf_op jit(solution)/shard_map/ppermute | solution.py:287
  8.3 6.6 %collective-permute-start.1 = (f32[160,128]{1,0:T(8,128)S(1)}, f32[160,128]{1,0:T(8,128)S(1)}, u32[]{:S(2)}, u32[]{:S(2)}) collective-permute-start(f32[160,128]{1,0:T(8,128)S(1)} %add.15), channel_id=1, source_target_pairs={{0,32},{16,240},{32,0},{48,208},{64,96},{80,176},{96,64},{112,144}... | collective-permute-start | bytes 245768 | tf_op jit(solution)/shard_map/ppermute | solution.py:292
  12.4 3.5 %collective-permute-start.3 = (f32[8,128]{1,0:T(8,128)S(1)}, f32[8,128]{1,0:T(8,128)S(1)}, u32[]{:S(2)}, u32[]{:S(2)}) collective-permute-start(f32[8,128]{1,0:T(8,128)S(1)} %broadcast_in_dim.37), channel_id=1, source_target_pairs={{0,1},{1,0},{2,3},{3,2},{4,5},{5,4},{6,7},{7,6},{8,9},{9,8},{10,11... | collective-permute-start | bytes 12296 | tf_op jit(solution)/shard_map/ppermute | solution.py:287
  14.9 4.5 %collective-permute-start.2 = (f32[160,128]{1,0:T(8,128)S(1)}, f32[160,128]{1,0:T(8,128)S(1)}, u32[]{:S(2)}, u32[]{:S(2)}) collective-permute-start(f32[160,128]{1,0:T(8,128)S(1)} %add.16), channel_id=1, source_target_pairs={{0,96},{16,48},{32,64},{48,16},{64,32},{80,112},{96,0},{112,80},{1... | collective-permute-start | bytes 245768 | tf_op jit(solution)/shard_map/ppermute | solution.py:292
  19.4 5.9 %collective-permute-start.5 = (f32[8,128]{1,0:T(8,128)S(1)}, f32[8,128]{1,0:T(8,128)S(1)}, u32[]{:S(2)}, u32[]{:S(2)}) collective-permute-start(f32[8,128]{1,0:T(8,128)S(1)} %broadcast_maximum_fusion), channel_id=1, source_target_pairs={{0,3},{1,2},{2,1},{3,0},{4,7},{5,6},{6,5},{7,4},{8,11},{9,10},{10,... | collective-permute-start | bytes 12296 | tf_op jit(solution)/shard_map/ppermute | solution.py:287
  21.3 5.1 %collective-permute-start.4 = (f32[160,128]{1,0:T(8,128)S(1)}, f32[160,128]{1,0:T(8,128)S(1)}, u32[]{:S(2)}, u32[]{:S(2)}) collective-permute-start(f32[160,128]{1,0:T(8,128)S(1)} %add.17), channel_id=1, source_target_pairs={{0,224},{16,112},{32,192},{48,80},{64,160},{80,48},{96,128},{112,1... | collective-permute-start | bytes 245768 | tf_op jit(solution)/shard_map/ppermute | solution.py:292
  25.4 45.2 %copy-start = (bf16[4,512,512]{2,1,0:T(8,128)(2,1)}, bf16[4,512,512]{2,1,0:T(8,128)(2,1)S(1)}, u32[]{:S(2)}) copy-start(bf16[4,512,512]{2,1,0:T(8,128)(2,1)S(1)} %add_convert_fusion.momentum_ref) | copy-start | bytes 6291460
  26.5 32.9 %copy-start.1 = (bf16[4,512,512]{2,1,0:T(8,128)(2,1)S(1)}, bf16[4,512,512]{2,1,0:T(8,128)(2,1)}, u32[]{:S(2)}) copy-start(bf16[4,512,512]{2,1,0:T(8,128)(2,1)} %weights_ref.7) | copy-start | bytes 6291460
  26.5 4.7 %collective-permute-start.7 = (f32[168,128]{1,0:T(8,128)S(1)}, f32[168,128]{1,0:T(8,128)S(1)}, u32[]{:S(2)}, u32[]{:S(2)}) collective-permute-start(f32[168,128]{1,0:T(8,128)S(1)} %pad_maximum_fusion.refs_0_), channel_id=1, source_target_pairs={{0,4},{4,0},{8,12},{12,8},{16,28},{20,24},{24,20},{28,16},{32,36},... | collective-permute-start | bytes 258056 | tf_op jit(solution)/shard_map/ppermute | solution.py:302
  29.3 9.1 %collective-permute-start.8 = (f32[168,128]{1,0:T(8,128)S(1)}, f32[168,128]{1,0:T(8,128)S(1)}, u32[]{:S(2)}, u32[]{:S(2)}) collective-permute-start(f32[168,128]{1,0:T(8,128)S(1)} %pad_maximum_fusion.refs_0_), channel_id=1, source_target_pairs={{0,12},{4,8},{8,4},{12,0},{16,20},{20,16},{24,28},{28,24},{32,44},... | collective-permute-start | bytes 258056 | tf_op jit(solution)/shard_map/ppermute | solution.py:302
  31.2 7.7 %collective-permute-start.11 = (f32[168,128]{1,0:T(8,128)S(1)}, f32[168,128]{1,0:T(8,128)S(1)}, u32[]{:S(2)}, u32[]{:S(2)}) collective-permute-start(f32[168,128]{1,0:T(8,128)S(1)} %collective-permute-done.7.refs_2_), channel_id=1, source_target_pairs={{0,12},{4,8},{8,4},{12,0},{16,20},{20,16},{24,28},{28,24},{32,44},... | collective-permute-start | bytes 258056 | tf_op jit(solution)/shard_map/ppermute | solution.py:302
  31.2 9.8 %collective-permute-start.6 = (f32[168,128]{1,0:T(8,128)S(1)}, f32[168,128]{1,0:T(8,128)S(1)}, u32[]{:S(2)}, u32[]{:S(2)}) collective-permute-start(f32[168,128]{1,0:T(8,128)S(1)} %pad_maximum_fusion.refs_0_), channel_id=1, source_target_pairs={{0,16},{16,0},{32,48},{48,32},{64,80},{80,64},{96,112},{112,96},{1... | collective-permute-start | bytes 258056 | tf_op jit(solution)/shard_map/ppermute | solution.py:287
  38.4 2.6 %collective-permute-start.10 = (f32[168,128]{1,0:T(8,128)S(1)}, f32[168,128]{1,0:T(8,128)S(1)}, u32[]{:S(2)}, u32[]{:S(2)}) collective-permute-start(f32[168,128]{1,0:T(8,128)S(1)} %collective-permute-done.7.refs_2_), channel_id=1, source_target_pairs={{0,16},{16,0},{32,48},{48,32},{64,80},{80,64},{96,112},{112,96},{1... | collective-permute-start | bytes 258056 | tf_op jit(solution)/shard_map/ppermute | solution.py:287
  38.4 2.6 %collective-permute-start.9 = (f32[168,128]{1,0:T(8,128)S(1)}, f32[168,128]{1,0:T(8,128)S(1)}, u32[]{:S(2)}, u32[]{:S(2)}) collective-permute-start(f32[168,128]{1,0:T(8,128)S(1)} %collective-permute-done.8.refs_4_), channel_id=1, source_target_pairs={{0,16},{16,0},{32,48},{48,32},{64,80},{80,64},{96,112},{112,96},{1... | collective-permute-start | bytes 258056 | tf_op jit(solution)/shard_map/ppermute | solution.py:287
  38.9 3.0 %collective-permute-start.12 = (f32[168,128]{1,0:T(8,128)S(1)}, f32[168,128]{1,0:T(8,128)S(1)}, u32[]{:S(2)}, u32[]{:S(2)}) collective-permute-start(f32[168,128]{1,0:T(8,128)S(1)} %collective-permute-done.11.refs_6_), channel_id=1, source_target_pairs={{0,16},{16,0},{32,48},{48,32},{64,80},{80,64},{96,112},{112,96},{1... | collective-permute-start | bytes 258056 | tf_op jit(solution)/shard_map/ppermute | solution.py:287
  56.6 5.5 %collective-permute-start.13 = (bf16[656,128]{1,0:T(8,128)(2,1)S(1)}, bf16[656,128]{1,0:T(8,128)(2,1)S(1)}, u32[]{:S(2)}, u32[]{:S(2)}) collective-permute-start(bf16[656,128]{1,0:T(8,128)(2,1)S(1)} %get-tuple-element.22.first_ref), channel_id=1, source_target_pairs={{0,1},{1,0},{2,3},{3,2},{16,19},{17,18},{18,17},{19,16},{32,33},{3... | collective-permute-start | bytes 503816 | tf_op jit(solution)/shard_map/ppermute | solution.py:302
  56.8 7.2 %collective-permute-start.15 = (bf16[656,128]{1,0:T(8,128)(2,1)S(1)}, bf16[656,128]{1,0:T(8,128)(2,1)S(1)}, u32[]{:S(2)}, u32[]{:S(2)}) collective-permute-start(bf16[656,128]{1,0:T(8,128)(2,1)S(1)} %get-tuple-element.23.second_ref), channel_id=1, source_target_pairs={{0,1},{1,0},{2,3},{3,2},{16,19},{17,18},{18,17},{19,16},{32,33},{3... | collective-permute-start | bytes 503816 | tf_op jit(solution)/shard_map/ppermute | solution.py:302
  62.1 4.2 %collective-permute-start.14 = (bf16[656,128]{1,0:T(8,128)(2,1)S(1)}, bf16[656,128]{1,0:T(8,128)(2,1)S(1)}, u32[]{:S(2)}, u32[]{:S(2)}) collective-permute-start(bf16[656,128]{1,0:T(8,128)(2,1)S(1)} %collective-permute-done.13.first_ref), channel_id=1, source_target_pairs={{0,3},{1,2},{2,1},{3,0},{16,17},{17,16},{18,19},{19,18},{32,35},{3... | collective-permute-start | bytes 503816 | tf_op jit(solution)/shard_map/ppermute | solution.py:302
  62.1 6.9 %collective-permute-start.18 = (bf16[656,128]{1,0:T(8,128)(2,1)S(1)}, bf16[656,128]{1,0:T(8,128)(2,1)S(1)}, u32[]{:S(2)}, u32[]{:S(2)}) collective-permute-start(bf16[656,128]{1,0:T(8,128)(2,1)S(1)} %collective-permute-done.13.first_ref), channel_id=1, source_target_pairs={{0,16},{16,0},{32,48},{48,32},{64,80},{80,64},{96,112},{112,96},{1... | collective-permute-start | bytes 503816 | tf_op jit(solution)/shard_map/ppermute | solution.py:287
  63.9 5.1 %collective-permute-start.17 = (bf16[656,128]{1,0:T(8,128)(2,1)S(1)}, bf16[656,128]{1,0:T(8,128)(2,1)S(1)}, u32[]{:S(2)}, u32[]{:S(2)}) collective-permute-start(bf16[656,128]{1,0:T(8,128)(2,1)S(1)} %collective-permute-done.15.second_ref), channel_id=1, source_target_pairs={{0,16},{16,0},{32,48},{48,32},{64,80},{80,64},{96,112},{112,96},{1... | collective-permute-start | bytes 503816 | tf_op jit(solution)/shard_map/ppermute | solution.py:287
  66.3 4.2 %collective-permute-start.16 = (bf16[656,128]{1,0:T(8,128)(2,1)S(1)}, bf16[656,128]{1,0:T(8,128)(2,1)S(1)}, u32[]{:S(2)}, u32[]{:S(2)}) collective-permute-start(bf16[656,128]{1,0:T(8,128)(2,1)S(1)} %collective-permute-done.14.first_ref), channel_id=1, source_target_pairs={{0,16},{16,0},{32,48},{48,32},{64,80},{80,64},{96,112},{112,96},{1... | collective-permute-start | bytes 503816 | tf_op jit(solution)/shard_map/ppermute | solution.py:287

commit v2 on v1

--- a/solution.py
+++ b/solution.py
@@ -27,7 +27,8 @@
 TAIL = 8
 HALF = 640
 END = 16
-UPPER = [(row, column) for row in range(BLOCKS) for column in range(row, BLOCKS)]
+STRIP = 256
+KEPT = [[(0, 0), (0, 1), (1, 1), (2, 0), (3, 0)], [(1, 2), (1, 3), (2, 2), (2, 3), (3, 3)]]
 
 
 def decayed(momentum, gradient):
@@ -104,17 +105,16 @@
 
 
 def newton_kernel(*refs):
-    (own, near, cross, far), rest = [refs[2 * at : 2 * at + 2] for at in range(BLOCKS)], refs[2 * BLOCKS :]
-    first_ref, second_ref, peaks_ref, packed, stacks, a_now, pairs_q, pair_a, pair_b, pair_p = rest
-    rank = pair_a.shape[1]
+    parts, rest = [refs[2 * at : 2 * at + 2] for at in range(BLOCKS)], refs[2 * BLOCKS :]
+    first_ref, second_ref, peaks_ref, packed, stacks, a_now, left_a, left_q, right_a, right_b, right_p = rest
+    rank = a_now.shape[0]
     mid = rank // 2
     dp_at, core = lax.axis_index("dp"), lax.rem(lax.axis_index("fsdp"), 2)
-    for turn, pair in ((0, own), (1 + 2 * core, near), (3 - 2 * core, cross), (2, far)):
+    for turn, pair in enumerate(parts):
         for side, piece in enumerate(pair):
             half = core + side - 2 * core * side
             stacks[dp_at ^ turn, pl.ds(aligned(half, PART), PART), :] = piece[0:PART, :]
-    peaks = jnp.maximum(jnp.maximum(own[0][PART:, :], near[0][PART:, :]), jnp.maximum(cross[0][PART:, :], far[0][PART:, :]))
-    peaks_ref[...] = peaks
+    peaks_ref[...] = functools.reduce(jnp.maximum, [pair[0][PART:, :] for pair in parts])
 
     def own_block(block):
         return stacks[block, 0:BLOCK, :]
@@ -144,53 +144,57 @@
     rows_at = lax.broadcasted_iota(jnp.int32, (rank, mid), 0)
     columns_at = lax.broadcasted_iota(jnp.int32, (rank, mid), 1)
     shifts = [jnp.where(rows_at == columns_at + strip.start, quintic_a, 0.0) for strip in strips]
-    dot = functools.partial(jnp.dot, preferred_element_type=jnp.float32)
-
-    def keep(pair, strip, value):
-        pair[0, :, strip], pair[1, :, strip] = split_in_two(value)
-
-    def product(left, right, strip):
-        return dot(left[0], right[0, :, strip]) + (dot(left[0], right[1, :, strip]) + dot(left[1], right[0, :, strip]))
-
-    for strip in strips:
-        keep(pair_a, strip, a_now[:, strip])
+
+    def keep(value, at, left=None, right=None):
+        high, low = split_in_two(value)
+        for turn, term in enumerate((high, low, high)):
+            if left is not None:
+                left[:, (3 * at + turn) * mid : (3 * at + turn + 1) * mid] = term
+        for turn, term in enumerate((high, high, low)):
+            if right is not None:
+                for block, rows in enumerate(strips):
+                    right[(3 * block + turn) * mid : (3 * block + turn + 1) * mid, strips[at]] = term[rows, :]
+
+    def product(left, right, at):
+        return jnp.dot(left[...], right[:, strips[at]], preferred_element_type=jnp.float32)
+
+    for at, strip in enumerate(strips):
+        keep(a_now[:, strip], at, left_a, right_a)
     for iteration in range(ITERS):
-        pair_q = pairs_q.at[iteration % 2]
-        for strip, shift in zip(strips, shifts):
-            square = product(pair_a, pair_a, strip)
-            keep(pair_q, strip, shift + quintic_b * a_now[:, strip] + quintic_c * square)
+        for at, strip in enumerate(strips):
+            factor = shifts[at] + quintic_b * a_now[:, strip] + quintic_c * product(left_a, right_a, at)
+            keep(factor, at, left_q, right_p if iteration == 0 else None)
         if iteration == ITERS - 1:
             break
-        for strip in strips:
-            keep(pair_b, strip, product(pair_q, pair_a, strip))
-        if iteration == 0:
-            pair_p[...] = pair_q[...]
-        else:
-            keep(pair_p, strips[0], product(pair_q, pair_p, strips[0]))
-        for strip in strips:
-            a_now[:, strip] = product(pair_q, pair_b, strip)
-            keep(pair_a, strip, a_now[:, strip])
+        for at in range(2):
+            keep(product(left_q, right_a, at), at, None, right_b)
         if iteration > 0:
-            keep(pair_p, strips[1], product(pair_q, pair_p, strips[1]))
-    for strip in strips:
-        a_now[:, strip] = product(pair_q, pair_p, strip)
-    for at, (row, column) in enumerate(UPPER):
-        block = a_now[row * BLOCK : (row + 1) * BLOCK, column * BLOCK : (column + 1) * BLOCK]
-        at_row = at % (HALF // BLOCK) * BLOCK
-        packed[at // (HALF // BLOCK), at_row : at_row + BLOCK, :] = block.astype(jnp.bfloat16)
+            keep(product(left_q, right_p, 0), 0, None, right_p)
+        for at, strip in enumerate(strips):
+            value = product(left_q, right_b, at)
+            a_now[:, strip] = value
+            keep(value, at, left_a, right_a)
+        if iteration > 0:
+            keep(product(left_q, right_p, 1), 1, None, right_p)
+    for at, strip in enumerate(strips):
+        a_now[:, strip] = product(left_q, right_p, at)
+    for side, kept in enumerate(KEPT):
+        for at, (row, column) in enumerate(kept):
+            block = a_now[row * BLOCK : (row + 1) * BLOCK, column * BLOCK : (column + 1) * BLOCK]
+            packed[side, at * BLOCK : (at + 1) * BLOCK, :] = block.astype(jnp.bfloat16)
     line = lax.broadcasted_iota(jnp.int32, (END, BLOCK), 0)
     spread = jnp.zeros((END, BLOCK), jnp.float32)
     for at, term in enumerate(split_in_three(norm)):
         spread = jnp.where(line == at, term.astype(jnp.float32), spread)
-    for half in range(2):
-        packed[half, HALF:, :] = spread.astype(jnp.bfloat16)
+    for side in range(2):
+        packed[side, HALF:, :] = spread.astype(jnp.bfloat16)
     first_ref[...] = packed[core]
     second_ref[...] = packed[1 - core]
 
 
 def newton(parts, rank):
     whole = pl.BlockSpec(memory_space=pltpu.VMEM)
-    pair = pltpu.VMEM((2, rank, rank), jnp.bfloat16)
+    left, right = pltpu.VMEM((rank, 3 * rank), jnp.bfloat16), pltpu.VMEM((3 * rank, rank), jnp.bfloat16)
     piece = jax.ShapeDtypeStruct((HALF + END, BLOCK), jnp.bfloat16)
     return pl.pallas_call(
         newton_kernel,
@@ -201,10 +205,11 @@
             pltpu.VMEM((2, HALF + END, BLOCK), jnp.bfloat16),
             pltpu.VMEM((BLOCKS, 2 * PART, BLOCK), jnp.float32),
             pltpu.VMEM((rank, rank), jnp.float32),
-            pltpu.VMEM((2, 2, rank, rank), jnp.bfloat16),
-            pair,
-            pair,
-            pair,
+            left,
+            left,
+            right,
+            right,
+            right,
         ],
         compiler_params=pltpu.CompilerParams(vmem_limit_bytes=40 * 2**20),
         cost_estimate=pl.CostEstimate(flops=17 * 6 * rank**3, bytes_accessed=6 * rank * rank, transcendentals=0),
@@ -213,26 +218,31 @@
 
 def last_kernel(update_scale, masks, weights_ref, momentum_ref, peaks_ref, first_ref, second_ref, *refs):
     out_ref, packed, factors, weights, momentum, fresh, arrived, left = refs[-8:]
-    rank, cols = fresh.shape
+    rank, cols = factors.shape[0], out_ref.shape[2]
     shard = lax.axis_index("fsdp")
     core = lax.rem(shard, 2)
     matrix = lax.axis_index("ctx") ^ (masks[0] + (masks[1] - masks[0]) * core)
+    strips = [pl.ds(at * STRIP, STRIP) for at in range(cols // STRIP)]
     loads = [
-        pltpu.make_async_copy(source.at[matrix], target, arrived.at[at])
-        for at, (source, target) in enumerate(((momentum_ref, momentum), (weights_ref, weights)))
+        [
+            pltpu.make_async_copy(source.at[matrix, :, strip], target.at[at], arrived.at[side, at])
+            for side, (source, target) in enumerate(((momentum_ref, momentum), (weights_ref, weights)))
+        ]
+        for at, strip in enumerate(strips)
     ]
-    for load in loads:
-        load.start()
+    for pair in loads:
+        for load in pair:
+            load.start()
     packed[core] = first_ref[...]
     packed[1 - core] = second_ref[...]
-    for at, (row, column) in enumerate(UPPER):
-        at_row = at % (HALF // BLOCK) * BLOCK
-        block = packed[at // (HALF // BLOCK), at_row : at_row + BLOCK, :]
-        factors[row * BLOCK : (row + 1) * BLOCK, column * BLOCK : (column + 1) * BLOCK] = block
-        if row != column:
-            factors[column * BLOCK : (column + 1) * BLOCK, row * BLOCK : (row + 1) * BLOCK] = block.T
+    for side, kept in enumerate(KEPT):
+        for at, (row, column) in enumerate(kept):
+            block = packed[side, at * BLOCK : (at + 1) * BLOCK, :]
+            factors[row * BLOCK : (row + 1) * BLOCK, column * BLOCK : (column + 1) * BLOCK] = block
+            if row != column:
+                factors[column * BLOCK : (column + 1) * BLOCK, row * BLOCK : (row + 1) * BLOCK] = block.T
     end = first_ref[HALF:, :].astype(jnp.float32)
-    norm = (end[0:1, 0:1] + end[1:2, 0:1]) + end[2:3, 0:1]
+    inverse = 1.0 / ((end[0:1, 0:1] + end[1:2, 0:1]) + end[2:3, 0:1])
     heads = cols // (KNOPE + VDIM)
     column = lax.broadcasted_iota(jnp.int32, (1, cols), 1)
     lane = lax.broadcasted_iota(jnp.int32, (1, BLOCK), 1)
@@ -243,16 +253,15 @@
         first = head * (KNOPE + VDIM)
         column_peaks = jnp.where((column >= first) & (column < first + KNOPE), peak, column_peaks)
     scale = jnp.sqrt(jnp.minimum(1.0, clip_limit / column_peaks))
-    loads[0].wait()
-    momentum[...] = (momentum[...].astype(jnp.float32) / norm).astype(jnp.bfloat16)
-    loads[1].wait()
     stores = []
-    for at in range(BLOCKS):
-        rows = slice(at * BLOCK, (at + 1) * BLOCK)
-        orthogonal = jnp.dot(factors[rows, :], momentum[...], preferred_element_type=jnp.float32)
-        value = (weights[rows, :].astype(jnp.float32) - step_size * (update_scale * orthogonal)) * scale
-        fresh[rows, :] = value.astype(jnp.bfloat16)
-        stores.append(pltpu.make_async_copy(fresh.at[rows], out_ref.at[matrix, rows], left.at[at]))
+    for at, strip in enumerate(strips):
+        loads[at][0].wait()
+        start = (momentum[at].astype(jnp.float32) * inverse).astype(jnp.bfloat16)
+        orthogonal = jnp.dot(factors[...], start, preferred_element_type=jnp.float32)
+        loads[at][1].wait()
+        value = weights[at].astype(jnp.float32) - step_size * (update_scale * orthogonal)
+        fresh[at] = (value * scale[:, at * STRIP : (at + 1) * STRIP]).astype(jnp.bfloat16)
+        stores.append(pltpu.make_async_copy(fresh.at[at], out_ref.at[matrix, :, strip], left.at[at]))
         stores[-1].start()
     for store in stores:
         store.wait()
@@ -262,7 +271,8 @@
     rank, cols = weights.shape[1:]
     whole, outside = pl.BlockSpec(memory_space=pltpu.VMEM), pl.BlockSpec(memory_space=pl.ANY)
     earlier = [] if before is None else [before]
-    square, block = pltpu.VMEM((rank, rank), jnp.bfloat16), pltpu.VMEM((rank, cols), jnp.bfloat16)
+    count = cols // STRIP
+    square, block = pltpu.VMEM((rank, rank), jnp.bfloat16), pltpu.VMEM((count, rank, STRIP), jnp.bfloat16)
     return pl.pallas_call(
         functools.partial(last_kernel, update_scale, masks),
         out_shape=jax.ShapeDtypeStruct(weights.shape, jnp.bfloat16),
@@ -274,8 +284,8 @@
             block,
             block,
             block,
-            pltpu.SemaphoreType.DMA((2,)),
-            pltpu.SemaphoreType.DMA((BLOCKS,)),
+            pltpu.SemaphoreType.DMA((2, count)),
+            pltpu.SemaphoreType.DMA((count,)),
         ],
         input_output_aliases={5: 0} if earlier else {},
         compiler_params=pltpu.CompilerParams(vmem_limit_bytes=24 * 2**20),
@@ -287,8 +297,14 @@
     return lax.ppermute(value, axis, [(at, at ^ mask) for at in range(lax.axis_size(axis))])
 
 
-def along_z(value, masks):
-    pairs = [(at, (at // 2 ^ masks[at % 2]) * 2 + at % 2) for at in range(lax.axis_size("fsdp"))]
+def along_z(value, mask):
+    count = lax.axis_size("fsdp")
+    zs = count // 2
+    pairs = []
+    for at in range(count):
+        z_at, core = at // 2, at % 2
+        partner = (((z_at - 2 * core) % zs ^ mask) + 2 * core) % zs
+        pairs.append((at, 2 * partner + core))
     return lax.ppermute(value, "fsdp", pairs)
 
 
@@ -306,35 +322,29 @@
     return crossed(value, "fsdp", 1)
 
 
-def gather_halves(axis, half):
-    near, cross = by_core(half, axis, (1, 3)), by_core(half, axis, (3, 1))
-    far = by_core(near, axis, (3, 1))
-    return (half, swapped(half)), (near, swapped(cross)), (cross, swapped(near)), (far, swapped(far))
-
-
 def on_device(weights, momentum, gradient, logit_max, layer_of):
     rank, cols = weights.shape[1:]
     fsdp = lax.axis_size("fsdp")
     layers = logit_max.shape[2]
 
-    keep, send = partial_gram(momentum, gradient)
-    total = keep + swapped(send)
-
     layer_match = jnp.arange(layers, dtype=jnp.int32)[None, :] == layer_of[:, None]
     peaks = jnp.max(jnp.where(layer_match[:, :, None], logit_max[0, 0][None], 0.0), axis=1)
     peaks = jnp.broadcast_to(peaks.reshape(1, BLOCK), (TAIL, BLOCK))
-    total = total + along_z(total, (1, 7))
-    total = total + along_z(total, (3, 1))
+
+    keep, send = partial_gram(momentum, gradient)
+    total = keep + swapped(send)
+    total, peaks, late_momentum = lax.optimization_barrier((total, peaks, momentum))
+    third, second, first = along_z(total, 3), along_z(total, 2), along_z(total, 1)
+    total = (total + first) + (second + third)
     peaks = jnp.maximum(peaks, crossed(peaks, "ctx", 1))
-    total, peaks = lax.optimization_barrier((total, peaks))
-    total = total + along_z(total, (7, 3))
+    new_momentum = decayed(late_momentum, gradient)
+    total, peaks, new_momentum = lax.optimization_barrier((total, peaks, new_momentum))
+    total = total + along_z(total, 7)
     peaks = jnp.maximum(peaks, crossed(peaks, "ctx", 3))
-    new_momentum = decayed(momentum, gradient)
-    total, new_momentum = lax.optimization_barrier((total, new_momentum))
-
-    parts = gather_halves("dp", jnp.concatenate([total, peaks], axis=0))
-
-    first, second, peaks = newton([piece for pair in parts for piece in pair], rank)
+
+    mine = jnp.concatenate([total, peaks], axis=0)
+    halves = [mine] + [crossed(mine, "dp", mask) for mask in (1, 2, 3)]
+    first, second, peaks = newton([piece for one in halves for piece in (one, swapped(one))], rank)
     update_scale = rms_factor * math.sqrt(max(rank, cols * fsdp))
     last = functools.partial(last_product, update_scale)
     near = tuple(by_core(piece, "ctx", (1, 3)) for piece in (first, second))

time: 72.5 us -> 68.4 us (0.943)
  waiting for transfers between devices: 12.6 us -> 6.08 us
  Pallas kernels: 23.3 us -> 25.1 us
    ppermute x6 -> x3, waiting for transfers between devices: 4.75 us -> 0.57 us  [by_core(): return lax.ppermute(value, ('fsdp', axis), pairs)]
    ppermute x3 -> x4, waiting for transfers between devices: 5.84 us -> 1.98 us  [along_z(): return lax.ppermute(value, 'fsdp', pairs)]
    ppermute x6 -> x3, starting transfers between devices: 5.6 us -> 2.87 us  [by_core(): return lax.ppermute(value, ('fsdp', axis), pairs)]
    ppermute x10 -> x13, starting transfers between devices: 19.8 us -> 21.9 us  [crossed(): lax.ppermute(value, axis, [(at, at ^ mask) for at in range(lax.axis_size(...]
    pallas_call x4, Pallas kernels: 6.35 us -> 8.21 us  [last_product(): pl.pallas_call(functools.partial(last_kernel, update_scale, masks), out_s...]
    ppermute x10 -> x13, waiting for transfers between devices: 2 us -> 3.53 us  [crossed(): lax.ppermute(value, axis, [(at, at ^ mask) for at in range(lax.axis_size(...]
    ppermute x3 -> x4, starting transfers between devices: 6.04 us -> 7.27 us  [along_z(): return lax.ppermute(value, 'fsdp', pairs)]
  transfers between devices with their start and end apart: 19 -> 20, of which waited for: 9 -> 7; matrix products, arithmetic and copies ran while one was open for 4% -> 5% of each run, Pallas kernels for 7% -> 9%
where the time goes in v2:
time: 68.4 us; the launch traced here: 68.3 us
  starting transfers between devices  32.1 us (47%)
  Pallas kernels  25.1 us (37%)
  waiting for transfers between devices  6.08 us (9%)
  other arithmetic  3.96 us (6%)
  between operations  0.99 us (1%)
    ppermute x13, starting transfers between devices, crossed(): lax.ppermute(value, axis, [(at, at ^ mask) for at in range(lax.axis_size(...  21.9 us
    pallas_call x1, Pallas kernels, newton(): pl.pallas_call(newton_kernel, out_shape=(piece, piece, jax.ShapeDtypeStru...  14.6 us
    pallas_call x4, Pallas kernels, last_product(): pl.pallas_call(functools.partial(last_kernel, update_scale, masks), out_s...  8.21 us
    ppermute x4, starting transfers between devices, along_z(): return lax.ppermute(value, 'fsdp', pairs)  7.27 us
    ppermute x13, waiting for transfers between devices, crossed(): lax.ppermute(value, axis, [(at, at ^ mask) for at in range(lax.axis_size(...  3.53 us
    ppermute x3, starting transfers between devices, by_core(): return lax.ppermute(value, ('fsdp', axis), pairs)  2.87 us
    convert_element_type x1, other arithmetic, decayed(): (momentum_decay * momentum.astype(jnp.float32) + gradient.astype(jnp.floa...  2.85 us
    pallas_call x1, Pallas kernels, partial_gram(): pl.pallas_call(partial_gram_kernel, out_shape=(shape, shape), in_specs=[p...  2.25 us
  transfers between devices with their start and end apart: 20, of which 7 were waited for; matrix products, arithmetic and copies ran while one was open for 5% of the time, Pallas kernels for 9%

profile of v2, /device:TPU:1, one launch (start us, length us, event | category | flops | bytes accessed | tf_op | source)
XLA Modules:
  0.0 68.3 jit_solution(11469516105615186689)
XLA Ops:
  0.6 2.3 %shard_map.68 = (f32[160,128]{1,0:T(8,128)}, f32[160,128]{1,0:T(8,128)}) custom-call(bf16[4,512,512]{2,1,0:T(8,128)(2,1)} %momentum_ref.1, bf16[4,512,512]{2,1,0:T(8,128)(2,1)} %gradient_ref.1), custom_call_target="tpu_custom_call" | custom-call | flops 41943040 | bytes 786432 | tf_op jit(solution)/shard_map/pallas_call | solution.py:78
  2.9 3.3 %collective-permute-start = (f32[160,128]{1,0:T(8,128)}, f32[160,128]{1,0:T(8,128)S(1)}, u32[]{:S(2)}, u32[]{:S(2)}) collective-permute-start(f32[160,128]{1,0:T(8,128)} %get-tuple-element.18), channel_id=1, source_target_pairs={{0,16},{16,0},{32,48},{48,32},{64,80},{80,64},{96,112},{112,96},{1... | collective-permute-start | bytes 245768 | tf_op jit(solution)/shard_map/ppermute | solution.py:297
  7.4 0.9 %add.18 = f32[160,128]{1,0:T(8,128)S(1)} add(f32[160,128]{1,0:T(8,128)} %get-tuple-element.17, f32[160,128]{1,0:T(8,128)S(1)} %collective-permute-done) | non-fusion elementwise | flops 20480 | bytes 245760 | tf_op jit(solution)/shard_map/add | solution.py:335
  8.3 3.9 %collective-permute-start.3 = (f32[160,128]{1,0:T(8,128)S(1)}, f32[160,128]{1,0:T(8,128)S(1)}, u32[]{:S(2)}, u32[]{:S(2)}) collective-permute-start(f32[160,128]{1,0:T(8,128)S(1)} %add.18), channel_id=1, source_target_pairs={{0,96},{16,240},{32,64},{48,208},{64,32},{80,176},{96,0},{112,144}... | collective-permute-start | bytes 245768 | tf_op jit(solution)/shard_map/ppermute | solution.py:308
  12.8 1.1 %collective-permute-start.1 = (f32[160,128]{1,0:T(8,128)S(1)}, f32[160,128]{1,0:T(8,128)S(1)}, u32[]{:S(2)}, u32[]{:S(2)}) collective-permute-start(f32[160,128]{1,0:T(8,128)S(1)} %add.18), channel_id=1, source_target_pairs={{0,32},{16,48},{32,0},{48,16},{64,96},{80,112},{96,64},{112,80},{1... | collective-permute-start | bytes 245768 | tf_op jit(solution)/shard_map/ppermute | solution.py:308
  13.8 1.2 %collective-permute-start.4 = (f32[8,128]{1,0:T(8,128)S(1)}, f32[8,128]{1,0:T(8,128)S(1)}, u32[]{:S(2)}, u32[]{:S(2)}) collective-permute-start(f32[8,128]{1,0:T(8,128)S(1)} %broadcast_in_dim.37), channel_id=1, source_target_pairs={{0,1},{1,0},{2,3},{3,2},{4,5},{5,4},{6,7},{7,6},{8,9},{9,8},{10,11... | collective-permute-start | bytes 12296 | tf_op jit(solution)/shard_map/ppermute | solution.py:297
  15.0 2.8 %add_convert_fusion.momentum_ref = bf16[4,512,512]{2,1,0:T(8,128)(2,1)S(1)} fusion(bf16[4,512,512]{2,1,0:T(8,128)(2,1)} %gradient_ref.1, bf16[4,512,512]{2,1,0:T(8,128)(2,1)} %momentum_ref.1), kind=kLoop, calls=%fused_computation | loop fusion | flops 5242880 | bytes 6291456 | tf_op jit(solution)/shard_map/convert_element_type | solution.py:35
  17.9 2.0 %collective-permute-done.2 = f32[160,128]{1,0:T(8,128)S(1)} collective-permute-done((f32[160,128]{1,0:T(8,128)S(1)}, f32[160,128]{1,0:T(8,128)S(1)}, u32[]{:S(2)}, u32[]{:S(2)}) %collective-permute-start.2) | collective-permute-done | bytes 81952 | tf_op jit(solution)/shard_map/ppermute | solution.py:308
  19.9 1.7 %collective-permute-start.5 = (f32[160,128]{1,0:T(8,128)S(1)}, f32[160,128]{1,0:T(8,128)S(1)}, u32[]{:S(2)}, u32[]{:S(2)}) collective-permute-start(f32[160,128]{1,0:T(8,128)S(1)} %add_add_fusion), channel_id=1, source_target_pairs={{0,224},{16,112},{32,192},{48,80},{64,160},{80,48},{96,128},{112,1... | collective-permute-start | bytes 245768 | tf_op jit(solution)/shard_map/ppermute | solution.py:308
  21.7 2.5 %collective-permute-start.6 = (f32[8,128]{1,0:T(8,128)S(1)}, f32[8,128]{1,0:T(8,128)S(1)}, u32[]{:S(2)}, u32[]{:S(2)}) collective-permute-start(f32[8,128]{1,0:T(8,128)S(1)} %max.6), channel_id=1, source_target_pairs={{0,3},{1,2},{2,1},{3,0},{4,7},{5,6},{6,5},{7,4},{8,11},{9,10},{10,... | collective-permute-start | bytes 12296 | tf_op jit(solution)/shard_map/ppermute | solution.py:297
  24.1 1.2 %collective-permute-done.6 = f32[8,128]{1,0:T(8,128)S(1)} collective-permute-done((f32[8,128]{1,0:T(8,128)S(1)}, f32[8,128]{1,0:T(8,128)S(1)}, u32[]{:S(2)}, u32[]{:S(2)}) %collective-permute-start.6) | collective-permute-done | bytes 4128 | tf_op jit(solution)/shard_map/ppermute | solution.py:297
  25.4 2.8 %collective-permute-start.12 = (f32[168,128]{1,0:T(8,128)S(1)}, f32[168,128]{1,0:T(8,128)S(1)}, u32[]{:S(2)}, u32[]{:S(2)}) collective-permute-start(f32[168,128]{1,0:T(8,128)S(1)} %pad_maximum_fusion.refs_0_), channel_id=1, source_target_pairs={{0,12},{4,8},{8,4},{12,0},{1,13},{5,9},{9,5},{13,1},{2,14},{6,10},... | collective-permute-start | bytes 258056 | tf_op jit(solution)/shard_map/ppermute | solution.py:297
  28.9 2.1 %collective-permute-start.7 = (f32[168,128]{1,0:T(8,128)S(1)}, f32[168,128]{1,0:T(8,128)S(1)}, u32[]{:S(2)}, u32[]{:S(2)}) collective-permute-start(f32[168,128]{1,0:T(8,128)S(1)} %pad_maximum_fusion.refs_0_), channel_id=1, source_target_pairs={{0,16},{16,0},{32,48},{48,32},{64,80},{80,64},{96,112},{112,96},{1... | collective-permute-start | bytes 258056 | tf_op jit(solution)/shard_map/ppermute | solution.py:297
  31.0 1.9 %collective-permute-start.13 = (f32[168,128]{1,0:T(8,128)S(1)}, f32[168,128]{1,0:T(8,128)S(1)}, u32[]{:S(2)}, u32[]{:S(2)}) collective-permute-start(f32[168,128]{1,0:T(8,128)S(1)} %collective-permute-done.12.refs_6_), channel_id=1, source_target_pairs={{0,16},{16,0},{32,48},{48,32},{64,80},{80,64},{96,112},{112,96},{1... | collective-permute-start | bytes 258056 | tf_op jit(solution)/shard_map/ppermute | solution.py:297
  33.0 2.8 %collective-permute-start.11 = (f32[168,128]{1,0:T(8,128)S(1)}, f32[168,128]{1,0:T(8,128)S(1)}, u32[]{:S(2)}, u32[]{:S(2)}) collective-permute-start(f32[168,128]{1,0:T(8,128)S(1)} %collective-permute-done.10.refs_4_), channel_id=1, source_target_pairs={{0,16},{16,0},{32,48},{48,32},{64,80},{80,64},{96,112},{112,96},{1... | collective-permute-start | bytes 258056 | tf_op jit(solution)/shard_map/ppermute | solution.py:297
  35.9 0.9 %collective-permute-done.11.refs_5_ = f32[168,128]{1,0:T(8,128)S(1)} collective-permute-done((f32[168,128]{1,0:T(8,128)S(1)}, f32[168,128]{1,0:T(8,128)S(1)}, u32[]{:S(2)}, u32[]{:S(2)}) %collective-permute-start.11) | collective-permute-done | bytes 86048 | tf_op jit(solution)/shard_map/ppermute | solution.py:297
  37.2 14.6 %shard_map.69 = (bf16[656,128]{1,0:T(8,128)(2,1)S(1)}, bf16[656,128]{1,0:T(8,128)(2,1)S(1)}, f32[8,128]{1,0:T(8,128)S(1)}) custom-call(f32[168,128]{1,0:T(8,128)S(1)} %pad_maximum_fusion.refs_0_, f32[168,128]{1,0:T(8,128)S(1)} %collective-permute-done.7.refs_1_, f32[168,128]{1,0:T(8,128)S(1)} %collective-permute-done.8.refs_2_, ...), custom_call_target="tpu_custom_call" | custom-call | flops 13690208256 | bytes 1572864 | tf_op jit(solution)/shard_map/pallas_call | solution.py:199
  51.8 2.6 %collective-permute-start.14 = (bf16[656,128]{1,0:T(8,128)(2,1)S(1)}, bf16[656,128]{1,0:T(8,128)(2,1)S(1)}, u32[]{:S(2)}, u32[]{:S(2)}) collective-permute-start(bf16[656,128]{1,0:T(8,128)(2,1)S(1)} %get-tuple-element.26.first_ref), channel_id=1, source_target_pairs={{0,1},{1,0},{2,3},{3,2},{16,19},{17,18},{18,17},{19,16},{32,33},{3... | collective-permute-start | bytes 503816 | tf_op jit(solution)/shard_map/ppermute | solution.py:318
  54.7 2.0 %shard_map.70.refs_0_ = bf16[4,512,512]{2,1,0:T(8,128)(2,1)} custom-call(bf16[4,512,512]{2,1,0:T(8,128)(2,1)S(1)} %copy-done.1, bf16[4,512,512]{2,1,0:T(8,128)(2,1)S(1)} %add_convert_fusion.momentum_ref, f32[8,128]{1,0:T(8,128)S(1)} %get-tuple-element.25.peaks_ref, bf16[656,128]{1,0:T(8,128)(2,1)S(1)} %get-tuple-element.26.first_ref, ...), custom_call_target="tpu_custom_call" | custom-call | flops 268435456 | bytes 1572864 | tf_op jit(solution)/shard_map/pallas_call | solution.py:276
  57.3 2.8 %collective-permute-start.19 = (bf16[656,128]{1,0:T(8,128)(2,1)S(1)}, bf16[656,128]{1,0:T(8,128)(2,1)S(1)}, u32[]{:S(2)}, u32[]{:S(2)}) collective-permute-start(bf16[656,128]{1,0:T(8,128)(2,1)S(1)} %collective-permute-done.14.first_ref), channel_id=1, source_target_pairs={{0,16},{16,0},{32,48},{48,32},{64,80},{80,64},{96,112},{112,96},{1... | collective-permute-start | bytes 503816 | tf_op jit(solution)/shard_map/ppermute | solution.py:297
  60.1 2.0 %shard_map.71.refs_0_ = bf16[4,512,512]{2,1,0:T(8,128)(2,1)} custom-call(bf16[4,512,512]{2,1,0:T(8,128)(2,1)S(1)} %copy-done.1, bf16[4,512,512]{2,1,0:T(8,128)(2,1)S(1)} %add_convert_fusion.momentum_ref, f32[8,128]{1,0:T(8,128)S(1)} %get-tuple-element.25.peaks_ref, ...), custom_call_target="tpu_custom_call", output_to_operand_aliasing={{}: (5, {})} | custom-call | flops 268435456 | bytes 1572864 | tf_op jit(solution)/shard_map/pallas_call | solution.py:276
  62.2 1.7 %collective-permute-start.17 = (bf16[656,128]{1,0:T(8,128)(2,1)S(1)}, bf16[656,128]{1,0:T(8,128)(2,1)S(1)}, u32[]{:S(2)}, u32[]{:S(2)}) collective-permute-start(bf16[656,128]{1,0:T(8,128)(2,1)S(1)} %collective-permute-done.15.first_ref), channel_id=1, source_target_pairs={{0,16},{16,0},{32,48},{48,32},{64,80},{80,64},{96,112},{112,96},{1... | collective-permute-start | bytes 503816 | tf_op jit(solution)/shard_map/ppermute | solution.py:297
  63.9 2.0 %shard_map.72.refs_0_ = bf16[4,512,512]{2,1,0:T(8,128)(2,1)} custom-call(bf16[4,512,512]{2,1,0:T(8,128)(2,1)S(1)} %copy-done.1, bf16[4,512,512]{2,1,0:T(8,128)(2,1)S(1)} %add_convert_fusion.momentum_ref, f32[8,128]{1,0:T(8,128)S(1)} %get-tuple-element.25.peaks_ref, ...), custom_call_target="tpu_custom_call", output_to_operand_aliasing={{}: (5, {})} | custom-call | flops 268435456 | bytes 1572864 | tf_op jit(solution)/shard_map/pallas_call | solution.py:276
  66.0 2.1 %shard_map.73 = bf16[4,512,512]{2,1,0:T(8,128)(2,1)} custom-call(bf16[4,512,512]{2,1,0:T(8,128)(2,1)S(1)} %copy-done.1, bf16[4,512,512]{2,1,0:T(8,128)(2,1)S(1)} %add_convert_fusion.momentum_ref, f32[8,128]{1,0:T(8,128)S(1)} %get-tuple-element.25.peaks_ref, bf16[656,128]{1,0:T(8,128)(2,1)S(1)} %collective-permute-done.15.first_ref, ...), custom_call_target="tpu_custom_call", output_to_operand_aliasing={{}: (5, {})} | custom-call | flops 268435456 | bytes 1572864 | tf_op jit(solution)/shard_map/pallas_call | solution.py:276
  (41 shorter events, 3.9 us)
Async XLA Ops:
  0.6 5.6 %copy-start.3 = (s32[4]{0:T(128)S(1)}, s32[4]{0:T(128)}, u32[]{:S(2)}) copy-start(s32[4]{0:T(128)} %param.9) | copy-start | bytes 52
  0.6 5.7 %copy-start.2 = (f32[1,1,61,32]{2,3,1,0:T(8,128)S(1)}, f32[1,1,61,32]{2,3,1,0:T(8,128)}, u32[]{:S(2)}) copy-start(f32[1,1,61,32]{2,3,1,0:T(8,128)} %param.8) | copy-start | bytes 23428
  2.9 4.5 %collective-permute-start = (f32[160,128]{1,0:T(8,128)}, f32[160,128]{1,0:T(8,128)S(1)}, u32[]{:S(2)}, u32[]{:S(2)}) collective-permute-start(f32[160,128]{1,0:T(8,128)} %get-tuple-element.18), channel_id=1, source_target_pairs={{0,16},{16,0},{32,48},{48,32},{64,80},{80,64},{96,112},{112,96},{1... | collective-permute-start | bytes 245768 | tf_op jit(solution)/shard_map/ppermute | solution.py:297
  8.3 9.7 %collective-permute-start.3 = (f32[160,128]{1,0:T(8,128)S(1)}, f32[160,128]{1,0:T(8,128)S(1)}, u32[]{:S(2)}, u32[]{:S(2)}) collective-permute-start(f32[160,128]{1,0:T(8,128)S(1)} %add.18), channel_id=1, source_target_pairs={{0,96},{16,240},{32,64},{48,208},{64,32},{80,176},{96,0},{112,144}... | collective-permute-start | bytes 245768 | tf_op jit(solution)/shard_map/ppermute | solution.py:308
  12.2 7.7 %collective-permute-start.2 = (f32[160,128]{1,0:T(8,128)S(1)}, f32[160,128]{1,0:T(8,128)S(1)}, u32[]{:S(2)}, u32[]{:S(2)}) collective-permute-start(f32[160,128]{1,0:T(8,128)S(1)} %add.18), channel_id=1, source_target_pairs={{0,64},{16,208},{32,96},{48,240},{64,0},{80,144},{96,32},{112,176}... | collective-permute-start | bytes 245768 | tf_op jit(solution)/shard_map/ppermute | solution.py:308
  12.8 7.2 %collective-permute-start.1 = (f32[160,128]{1,0:T(8,128)S(1)}, f32[160,128]{1,0:T(8,128)S(1)}, u32[]{:S(2)}, u32[]{:S(2)}) collective-permute-start(f32[160,128]{1,0:T(8,128)S(1)} %add.18), channel_id=1, source_target_pairs={{0,32},{16,48},{32,0},{48,16},{64,96},{80,112},{96,64},{112,80},{1... | collective-permute-start | bytes 245768 | tf_op jit(solution)/shard_map/ppermute | solution.py:308
  13.8 4.1 %collective-permute-start.4 = (f32[8,128]{1,0:T(8,128)S(1)}, f32[8,128]{1,0:T(8,128)S(1)}, u32[]{:S(2)}, u32[]{:S(2)}) collective-permute-start(f32[8,128]{1,0:T(8,128)S(1)} %broadcast_in_dim.37), channel_id=1, source_target_pairs={{0,1},{1,0},{2,3},{3,2},{4,5},{5,4},{6,7},{7,6},{8,9},{9,8},{10,11... | collective-permute-start | bytes 12296 | tf_op jit(solution)/shard_map/ppermute | solution.py:297
  17.9 48.1 %copy-start = (bf16[4,512,512]{2,1,0:T(8,128)(2,1)}, bf16[4,512,512]{2,1,0:T(8,128)(2,1)S(1)}, u32[]{:S(2)}) copy-start(bf16[4,512,512]{2,1,0:T(8,128)(2,1)S(1)} %add_convert_fusion.momentum_ref) | copy-start | bytes 6291460
  19.9 5.4 %collective-permute-start.5 = (f32[160,128]{1,0:T(8,128)S(1)}, f32[160,128]{1,0:T(8,128)S(1)}, u32[]{:S(2)}, u32[]{:S(2)}) collective-permute-start(f32[160,128]{1,0:T(8,128)S(1)} %add_add_fusion), channel_id=1, source_target_pairs={{0,224},{16,112},{32,192},{48,80},{64,160},{80,48},{96,128},{112,1... | collective-permute-start | bytes 245768 | tf_op jit(solution)/shard_map/ppermute | solution.py:308
  21.7 3.7 %collective-permute-start.6 = (f32[8,128]{1,0:T(8,128)S(1)}, f32[8,128]{1,0:T(8,128)S(1)}, u32[]{:S(2)}, u32[]{:S(2)}) collective-permute-start(f32[8,128]{1,0:T(8,128)S(1)} %max.6), channel_id=1, source_target_pairs={{0,3},{1,2},{2,1},{3,0},{4,7},{5,6},{6,5},{7,4},{8,11},{9,10},{10,... | collective-permute-start | bytes 12296 | tf_op jit(solution)/shard_map/ppermute | solution.py:297
  25.4 29.3 %copy-start.1 = (bf16[4,512,512]{2,1,0:T(8,128)(2,1)S(1)}, bf16[4,512,512]{2,1,0:T(8,128)(2,1)}, u32[]{:S(2)}) copy-start(bf16[4,512,512]{2,1,0:T(8,128)(2,1)} %weights_ref.7) | copy-start | bytes 6291460
  25.4 5.6 %collective-permute-start.12 = (f32[168,128]{1,0:T(8,128)S(1)}, f32[168,128]{1,0:T(8,128)S(1)}, u32[]{:S(2)}, u32[]{:S(2)}) collective-permute-start(f32[168,128]{1,0:T(8,128)S(1)} %pad_maximum_fusion.refs_0_), channel_id=1, source_target_pairs={{0,12},{4,8},{8,4},{12,0},{1,13},{5,9},{9,5},{13,1},{2,14},{6,10},... | collective-permute-start | bytes 258056 | tf_op jit(solution)/shard_map/ppermute | solution.py:297
  28.2 4.8 %collective-permute-start.10 = (f32[168,128]{1,0:T(8,128)S(1)}, f32[168,128]{1,0:T(8,128)S(1)}, u32[]{:S(2)}, u32[]{:S(2)}) collective-permute-start(f32[168,128]{1,0:T(8,128)S(1)} %pad_maximum_fusion.refs_0_), channel_id=1, source_target_pairs={{0,8},{4,12},{8,0},{12,4},{1,9},{5,13},{9,1},{13,5},{2,10},{6,14},... | collective-permute-start | bytes 258056 | tf_op jit(solution)/shard_map/ppermute | solution.py:297
  28.5 7.3 %collective-permute-start.8 = (f32[168,128]{1,0:T(8,128)S(1)}, f32[168,128]{1,0:T(8,128)S(1)}, u32[]{:S(2)}, u32[]{:S(2)}) collective-permute-start(f32[168,128]{1,0:T(8,128)S(1)} %pad_maximum_fusion.refs_0_), channel_id=1, source_target_pairs={{0,4},{4,0},{8,12},{12,8},{1,5},{5,1},{9,13},{13,9},{2,6},{6,2},{1... | collective-permute-start | bytes 258056 | tf_op jit(solution)/shard_map/ppermute | solution.py:297
  28.9 7.0 %collective-permute-start.7 = (f32[168,128]{1,0:T(8,128)S(1)}, f32[168,128]{1,0:T(8,128)S(1)}, u32[]{:S(2)}, u32[]{:S(2)}) collective-permute-start(f32[168,128]{1,0:T(8,128)S(1)} %pad_maximum_fusion.refs_0_), channel_id=1, source_target_pairs={{0,16},{16,0},{32,48},{48,32},{64,80},{80,64},{96,112},{112,96},{1... | collective-permute-start | bytes 258056 | tf_op jit(solution)/shard_map/ppermute | solution.py:297
  31.0 4.9 %collective-permute-start.13 = (f32[168,128]{1,0:T(8,128)S(1)}, f32[168,128]{1,0:T(8,128)S(1)}, u32[]{:S(2)}, u32[]{:S(2)}) collective-permute-start(f32[168,128]{1,0:T(8,128)S(1)} %collective-permute-done.12.refs_6_), channel_id=1, source_target_pairs={{0,16},{16,0},{32,48},{48,32},{64,80},{80,64},{96,112},{112,96},{1... | collective-permute-start | bytes 258056 | tf_op jit(solution)/shard_map/ppermute | solution.py:297
  33.0 3.8 %collective-permute-start.11 = (f32[168,128]{1,0:T(8,128)S(1)}, f32[168,128]{1,0:T(8,128)S(1)}, u32[]{:S(2)}, u32[]{:S(2)}) collective-permute-start(f32[168,128]{1,0:T(8,128)S(1)} %collective-permute-done.10.refs_4_), channel_id=1, source_target_pairs={{0,16},{16,0},{32,48},{48,32},{64,80},{80,64},{96,112},{112,96},{1... | collective-permute-start | bytes 258056 | tf_op jit(solution)/shard_map/ppermute | solution.py:297
  35.9 1.3 %collective-permute-start.9 = (f32[168,128]{1,0:T(8,128)S(1)}, f32[168,128]{1,0:T(8,128)S(1)}, u32[]{:S(2)}, u32[]{:S(2)}) collective-permute-start(f32[168,128]{1,0:T(8,128)S(1)} %collective-permute-done.8.refs_2_), channel_id=1, source_target_pairs={{0,16},{16,0},{32,48},{48,32},{64,80},{80,64},{96,112},{112,96},{1... | collective-permute-start | bytes 258056 | tf_op jit(solution)/shard_map/ppermute | solution.py:297
  51.8 5.5 %collective-permute-start.14 = (bf16[656,128]{1,0:T(8,128)(2,1)S(1)}, bf16[656,128]{1,0:T(8,128)(2,1)S(1)}, u32[]{:S(2)}, u32[]{:S(2)}) collective-permute-start(bf16[656,128]{1,0:T(8,128)(2,1)S(1)} %get-tuple-element.26.first_ref), channel_id=1, source_target_pairs={{0,1},{1,0},{2,3},{3,2},{16,19},{17,18},{18,17},{19,16},{32,33},{3... | collective-permute-start | bytes 503816 | tf_op jit(solution)/shard_map/ppermute | solution.py:318
  54.3 5.8 %collective-permute-start.16 = (bf16[656,128]{1,0:T(8,128)(2,1)S(1)}, bf16[656,128]{1,0:T(8,128)(2,1)S(1)}, u32[]{:S(2)}, u32[]{:S(2)}) collective-permute-start(bf16[656,128]{1,0:T(8,128)(2,1)S(1)} %get-tuple-element.27.second_ref), channel_id=1, source_target_pairs={{0,1},{1,0},{2,3},{3,2},{16,19},{17,18},{18,17},{19,16},{32,33},{3... | collective-permute-start | bytes 503816 | tf_op jit(solution)/shard_map/ppermute | solution.py:318
  57.3 4.9 %collective-permute-start.15 = (bf16[656,128]{1,0:T(8,128)(2,1)S(1)}, bf16[656,128]{1,0:T(8,128)(2,1)S(1)}, u32[]{:S(2)}, u32[]{:S(2)}) collective-permute-start(bf16[656,128]{1,0:T(8,128)(2,1)S(1)} %collective-permute-done.14.first_ref), channel_id=1, source_target_pairs={{0,3},{1,2},{2,1},{3,0},{16,17},{17,16},{18,19},{19,18},{32,35},{3... | collective-permute-start | bytes 503816 | tf_op jit(solution)/shard_map/ppermute | solution.py:318
  57.3 6.7 %collective-permute-start.19 = (bf16[656,128]{1,0:T(8,128)(2,1)S(1)}, bf16[656,128]{1,0:T(8,128)(2,1)S(1)}, u32[]{:S(2)}, u32[]{:S(2)}) collective-permute-start(bf16[656,128]{1,0:T(8,128)(2,1)S(1)} %collective-permute-done.14.first_ref), channel_id=1, source_target_pairs={{0,16},{16,0},{32,48},{48,32},{64,80},{80,64},{96,112},{112,96},{1... | collective-permute-start | bytes 503816 | tf_op jit(solution)/shard_map/ppermute | solution.py:297
  60.1 3.8 %collective-permute-start.18 = (bf16[656,128]{1,0:T(8,128)(2,1)S(1)}, bf16[656,128]{1,0:T(8,128)(2,1)S(1)}, u32[]{:S(2)}, u32[]{:S(2)}) collective-permute-start(bf16[656,128]{1,0:T(8,128)(2,1)S(1)} %collective-permute-done.16.second_ref), channel_id=1, source_target_pairs={{0,16},{16,0},{32,48},{48,32},{64,80},{80,64},{96,112},{112,96},{1... | collective-permute-start | bytes 503816 | tf_op jit(solution)/shard_map/ppermute | solution.py:297
  62.2 3.8 %collective-permute-start.17 = (bf16[656,128]{1,0:T(8,128)(2,1)S(1)}, bf16[656,128]{1,0:T(8,128)(2,1)S(1)}, u32[]{:S(2)}, u32[]{:S(2)}) collective-permute-start(bf16[656,128]{1,0:T(8,128)(2,1)S(1)} %collective-permute-done.15.first_ref), channel_id=1, source_target_pairs={{0,16},{16,0},{32,48},{48,32},{64,80},{80,64},{96,112},{112,96},{1... | collective-permute-start | bytes 503816 | tf_op jit(solution)/shard_map/ppermute | solution.py:297

commit v3 on v2

--- a/solution.py
+++ b/solution.py
@@ -28,7 +28,7 @@
 HALF = 640
 END = 16
 STRIP = 256
-KEPT = [[(0, 0), (0, 1), (1, 1), (2, 0), (3, 0)], [(1, 2), (1, 3), (2, 2), (2, 3), (3, 3)]]
+KEPT = [[(0, 0), (0, 1), (0, 2), (0, 3), (1, 1)], [(1, 2), (1, 3), (2, 2), (2, 3), (3, 3)]]
 
 
 def decayed(momentum, gradient):
@@ -106,7 +106,7 @@
 
 def newton_kernel(*refs):
     parts, rest = [refs[2 * at : 2 * at + 2] for at in range(BLOCKS)], refs[2 * BLOCKS :]
-    first_ref, second_ref, peaks_ref, packed, stacks, a_now, left_a, left_q, right_a, right_b, right_p = rest
+    first_ref, second_ref, peaks_ref, packed, stacks, a_now, pair_a, pair_q, pair_b, pair_p, next_p = rest
     rank = a_now.shape[0]
     mid = rank // 2
     dp_at, core = lax.axis_index("dp"), lax.rem(lax.axis_index("fsdp"), 2)
@@ -140,44 +140,49 @@
         place(block, block + 2, far_block)
         place(block + 2, block, far_block.T)
 
-    strips = [slice(0, mid), slice(mid, rank)]
-    rows_at = lax.broadcasted_iota(jnp.int32, (rank, mid), 0)
-    columns_at = lax.broadcasted_iota(jnp.int32, (rank, mid), 1)
-    shifts = [jnp.where(rows_at == columns_at + strip.start, quintic_a, 0.0) for strip in strips]
-
-    def keep(value, at, left=None, right=None):
-        high, low = split_in_two(value)
-        for turn, term in enumerate((high, low, high)):
-            if left is not None:
-                left[:, (3 * at + turn) * mid : (3 * at + turn + 1) * mid] = term
-        for turn, term in enumerate((high, high, low)):
-            if right is not None:
-                for block, rows in enumerate(strips):
-                    right[(3 * block + turn) * mid : (3 * block + turn + 1) * mid, strips[at]] = term[rows, :]
-
-    def product(left, right, at):
-        return jnp.dot(left[...], right[:, strips[at]], preferred_element_type=jnp.float32)
-
-    for at, strip in enumerate(strips):
-        keep(a_now[:, strip], at, left_a, right_a)
-    for iteration in range(ITERS):
-        for at, strip in enumerate(strips):
-            factor = shifts[at] + quintic_b * a_now[:, strip] + quintic_c * product(left_a, right_a, at)
-            keep(factor, at, left_q, right_p if iteration == 0 else None)
-        if iteration == ITERS - 1:
-            break
-        for at in range(2):
-            keep(product(left_q, right_a, at), at, None, right_b)
-        if iteration > 0:
-            keep(product(left_q, right_p, 0), 0, None, right_p)
-        for at, strip in enumerate(strips):
-            value = product(left_q, right_b, at)
-            a_now[:, strip] = value
-            keep(value, at, left_a, right_a)
-        if iteration > 0:
-            keep(product(left_q, right_p, 1), 1, None, right_p)
-    for at, strip in enumerate(strips):
-        a_now[:, strip] = product(left_q, right_p, at)
+    first, last = slice(0, mid), slice(mid, rank)
+    rows_at = lax.broadcasted_iota(jnp.int32, (mid, rank), 0)
+    columns_at = lax.broadcasted_iota(jnp.int32, (mid, rank), 1)
+    shift = jnp.where(rows_at == columns_at, quintic_a, 0.0)
+    dot = functools.partial(jnp.dot, preferred_element_type=jnp.float32)
+
+    def keep(pair, rows, columns, value):
+        pair[0, rows, columns], pair[1, rows, columns] = split_in_two(value)
+
+    def product(left, right, rows, columns):
+        high, low = left[0, rows, :], left[1, rows, :]
+        return dot(high, right[0, :, columns]) + (dot(high, right[1, :, columns]) + dot(low, right[0, :, columns]))
+
+    def whole_product(left, right, target, finish=None):
+        for rows, columns in ((first, slice(0, rank)), (last, last)):
+            value = product(left, right, rows, columns)
+            if finish is not None:
+                value = finish(value, rows, columns)
+            keep(target, rows, columns, value)
+            if rows == first:
+                keep(target, last, first, value[:, mid:].T)
+
+    def to_factor(square, rows, columns):
+        return shift[:, 0 : square.shape[1]] + quintic_b * a_now[rows, columns] + quintic_c * square
+
+    def store(value, rows, columns):
+        a_now[rows, columns] = value
+        return value
+
+    for rows in (first, last):
+        keep(pair_a, rows, slice(0, rank), a_now[rows, :])
+    for iteration in range(ITERS - 1):
+        whole_product(pair_a, pair_a, pair_q, to_factor)
+        whole_product(pair_q, pair_a, pair_b)
+        whole_product(pair_b, pair_q, pair_a, store)
+        if iteration == 0:
+            pair_p[...] = pair_q[...]
+        else:
+            whole_product(pair_p, pair_q, next_p)
+            pair_p, next_p = next_p, pair_p
+    whole_product(pair_a, pair_a, pair_q, to_factor)
+    for rows, columns in ((first, slice(0, rank)), (last, last)):
+        a_now[rows, columns] = product(pair_p, pair_q, rows, columns)
     for side, kept in enumerate(KEPT):
         for at, (row, column) in enumerate(kept):
             block = a_now[row * BLOCK : (row + 1) * BLOCK, column * BLOCK : (column + 1) * BLOCK]
@@ -194,7 +199,7 @@
 
 def newton(parts, rank):
     whole = pl.BlockSpec(memory_space=pltpu.VMEM)
-    left, right = pltpu.VMEM((rank, 3 * rank), jnp.bfloat16), pltpu.VMEM((3 * rank, rank), jnp.bfloat16)
+    pair = pltpu.VMEM((2, rank, rank), jnp.bfloat16)
     piece = jax.ShapeDtypeStruct((HALF + END, BLOCK), jnp.bfloat16)
     return pl.pallas_call(
         newton_kernel,
@@ -205,11 +210,11 @@
             pltpu.VMEM((2, HALF + END, BLOCK), jnp.bfloat16),
             pltpu.VMEM((BLOCKS, 2 * PART, BLOCK), jnp.float32),
             pltpu.VMEM((rank, rank), jnp.float32),
-            left,
-            left,
-            right,
-            right,
-            right,
+            pair,
+            pair,
+            pair,
+            pair,
+            pair,
         ],
         compiler_params=pltpu.CompilerParams(vmem_limit_bytes=40 * 2**20),
         cost_estimate=pl.CostEstimate(flops=17 * 6 * rank**3, bytes_accessed=6 * rank * rank, transcendentals=0),
@@ -217,22 +222,11 @@
 
 
 def last_kernel(update_scale, masks, weights_ref, momentum_ref, peaks_ref, first_ref, second_ref, *refs):
-    out_ref, packed, factors, weights, momentum, fresh, arrived, left = refs[-8:]
-    rank, cols = factors.shape[0], out_ref.shape[2]
+    out_ref, packed, factors, fresh, left = refs[-5:]
+    rank, cols = fresh.shape
     shard = lax.axis_index("fsdp")
     core = lax.rem(shard, 2)
     matrix = lax.axis_index("ctx") ^ (masks[0] + (masks[1] - masks[0]) * core)
-    strips = [pl.ds(at * STRIP, STRIP) for at in range(cols // STRIP)]
-    loads = [
-        [
-            pltpu.make_async_copy(source.at[matrix, :, strip], target.at[at], arrived.at[side, at])
-            for side, (source, target) in enumerate(((momentum_ref, momentum), (weights_ref, weights)))
-        ]
-        for at, strip in enumerate(strips)
-    ]
-    for pair in loads:
-        for load in pair:
-            load.start()
     packed[core] = first_ref[...]
     packed[1 - core] = second_ref[...]
     for side, kept in enumerate(KEPT):
@@ -253,15 +247,14 @@
         first = head * (KNOPE + VDIM)
         column_peaks = jnp.where((column >= first) & (column < first + KNOPE), peak, column_peaks)
     scale = jnp.sqrt(jnp.minimum(1.0, clip_limit / column_peaks))
+    start = (momentum_ref[matrix].astype(jnp.float32) * inverse).astype(jnp.bfloat16)
     stores = []
-    for at, strip in enumerate(strips):
-        loads[at][0].wait()
-        start = (momentum[at].astype(jnp.float32) * inverse).astype(jnp.bfloat16)
-        orthogonal = jnp.dot(factors[...], start, preferred_element_type=jnp.float32)
-        loads[at][1].wait()
-        value = weights[at].astype(jnp.float32) - step_size * (update_scale * orthogonal)
-        fresh[at] = (value * scale[:, at * STRIP : (at + 1) * STRIP]).astype(jnp.bfloat16)
-        stores.append(pltpu.make_async_copy(fresh.at[at], out_ref.at[matrix, :, strip], left.at[at]))
+    for at in range(rank // STRIP):
+        rows = slice(at * STRIP, (at + 1) * STRIP)
+        orthogonal = jnp.dot(factors[rows, :], start, preferred_element_type=jnp.float32)
+        value = weights_ref[matrix, rows, :].astype(jnp.float32) - step_size * (update_scale * orthogonal)
+        fresh[rows, :] = (value * scale).astype(jnp.bfloat16)
+        stores.append(pltpu.make_async_copy(fresh.at[rows], out_ref.at[matrix, rows], left.at[at]))
         stores[-1].start()
     for store in stores:
         store.wait()
@@ -271,26 +264,54 @@
     rank, cols = weights.shape[1:]
     whole, outside = pl.BlockSpec(memory_space=pltpu.VMEM), pl.BlockSpec(memory_space=pl.ANY)
     earlier = [] if before is None else [before]
-    count = cols // STRIP
-    square, block = pltpu.VMEM((rank, rank), jnp.bfloat16), pltpu.VMEM((count, rank, STRIP), jnp.bfloat16)
     return pl.pallas_call(
         functools.partial(last_kernel, update_scale, masks),
         out_shape=jax.ShapeDtypeStruct(weights.shape, jnp.bfloat16),
-        in_specs=[outside] * 2 + [whole] * 3 + [outside] * len(earlier),
+        in_specs=[whole] * 5 + [outside] * len(earlier),
         out_specs=outside,
         scratch_shapes=[
             pltpu.VMEM((2, HALF + END, BLOCK), jnp.bfloat16),
-            square,
-            block,
-            block,
-            block,
-            pltpu.SemaphoreType.DMA((2, count)),
-            pltpu.SemaphoreType.DMA((count,)),
+            pltpu.VMEM((rank, rank), jnp.bfloat16),
+            pltpu.VMEM((rank, cols), jnp.bfloat16),
+            pltpu.SemaphoreType.DMA((rank // STRIP,)),
         ],
         input_output_aliases={5: 0} if earlier else {},
         compiler_params=pltpu.CompilerParams(vmem_limit_bytes=24 * 2**20),
         cost_estimate=pl.CostEstimate(flops=2 * rank * rank * cols, bytes_accessed=6 * rank * cols, transcendentals=0),
     )(weights, momentum, peaks, *pair, *earlier)
+
+
+def fetch_kernel(source_ref, out_ref):
+    out_ref[...] = source_ref[...]
+
+
+def fetch(value):
+    whole = pl.BlockSpec(memory_space=pltpu.VMEM)
+    return pl.pallas_call(
+        fetch_kernel,
+        out_shape=jax.ShapeDtypeStruct(value.shape, value.dtype),
+        in_specs=[whole],
+        out_specs=whole,
+        compiler_params=pltpu.CompilerParams(vmem_limit_bytes=8 * 2**20),
+        cost_estimate=pl.CostEstimate(flops=0, bytes_accessed=8 * value.size, transcendentals=0),
+    )(value)
+
+
+def join_kernel(total_ref, arrived_ref, peaks_ref, peaks_arrived_ref, out_ref):
+    out_ref[0:PART, :] = total_ref[...] + arrived_ref[...]
+    out_ref[PART:, :] = jnp.maximum(peaks_ref[...], peaks_arrived_ref[...])
+
+
+def join(*arrays):
+    whole = pl.BlockSpec(memory_space=pltpu.VMEM)
+    return pl.pallas_call(
+        join_kernel,
+        out_shape=jax.ShapeDtypeStruct((PART + TAIL, BLOCK), jnp.float32),
+        in_specs=[whole] * 4,
+        out_specs=whole,
+        compiler_params=pltpu.CompilerParams(vmem_limit_bytes=8 * 2**20),
+        cost_estimate=pl.CostEstimate(flops=PART * BLOCK, bytes_accessed=12 * PART * BLOCK, transcendentals=0),
+    )(*arrays)
 
 
 def crossed(value, axis, mask):
@@ -332,17 +353,14 @@
     peaks = jnp.broadcast_to(peaks.reshape(1, BLOCK), (TAIL, BLOCK))
 
     keep, send = partial_gram(momentum, gradient)
-    total = keep + swapped(send)
+    total = fetch(keep) + swapped(send)
     total, peaks, late_momentum = lax.optimization_barrier((total, peaks, momentum))
     third, second, first = along_z(total, 3), along_z(total, 2), along_z(total, 1)
     total = (total + first) + (second + third)
     peaks = jnp.maximum(peaks, crossed(peaks, "ctx", 1))
     new_momentum = decayed(late_momentum, gradient)
     total, peaks, new_momentum = lax.optimization_barrier((total, peaks, new_momentum))
-    total = total + along_z(total, 7)
-    peaks = jnp.maximum(peaks, crossed(peaks, "ctx", 3))
-
-    mine = jnp.concatenate([total, peaks], axis=0)
+    mine = join(total, along_z(total, 7), peaks, crossed(peaks, "ctx", 3))
     halves = [mine] + [crossed(mine, "dp", mask) for mask in (1, 2, 3)]
     first, second, peaks = newton([piece for one in halves for piece in (one, swapped(one))], rank)
     update_scale = rms_factor * math.sqrt(max(rank, cols * fsdp))

time: 68.4 us -> 63.5 us (0.928)
  Pallas kernels: 25.1 us -> 19.6 us
  other arithmetic: 3.96 us -> 3.06 us
  local copies, waits for them, and re-layouts: 0.11 us -> 1 us
    pallas_call x4, Pallas kernels: 8.21 us -> 5.37 us  [last_product(): pl.pallas_call(functools.partial(last_kernel, update_scale, masks), out_s...]
    pallas_call x1, Pallas kernels: 14.6 us -> 12 us  [newton(): pl.pallas_call(newton_kernel, out_shape=(piece, piece, jax.ShapeDtypeStru...]
    ppermute x3, waiting for transfers between devices: 0.57 us -> 1.7 us  [by_core(): return lax.ppermute(value, ('fsdp', axis), pairs)]
    add x2 -> x1, other arithmetic: 0.91 us -> 0.01 us  [on_device(): total = fetch(keep) + swapped(send)]
    unnamed x8 -> x10, local copies, waits for them, and re-layouts: 0.02 us -> 0.91 us
    ppermute x13, waiting for transfers between devices: 3.53 us -> 2.69 us  [crossed(): lax.ppermute(value, axis, [(at, at ^ mask) for at in range(lax.axis_size(...]
  transfers between devices with their start and end apart: 20 -> 20, of which waited for: 7 -> 7; matrix products, arithmetic and copies ran while one was open for 5% -> 5% of each run, Pallas kernels for 9% -> 6%
where the time goes in v3:
time: 63.5 us; the launch traced here: 63.3 us
  starting transfers between devices  32.3 us (51%)
  Pallas kernels  19.6 us (31%)
  waiting for transfers between devices  6.42 us (10%)
  other arithmetic  3.06 us (5%)
  local copies, waits for them, and re-layouts  1 us (2%)
  between operations  0.98 us (2%)
    ppermute x13, starting transfers between devices, crossed(): lax.ppermute(value, axis, [(at, at ^ mask) for at in range(lax.axis_size(...  22.2 us
    pallas_call x1, Pallas kernels, newton(): pl.pallas_call(newton_kernel, out_shape=(piece, piece, jax.ShapeDtypeStru...  12 us
    ppermute x4, starting transfers between devices, along_z(): return lax.ppermute(value, 'fsdp', pairs)  7.27 us
    pallas_call x4, Pallas kernels, last_product(): pl.pallas_call(functools.partial(last_kernel, update_scale, masks), out_s...  5.37 us
    convert_element_type x1, other arithmetic, decayed(): (momentum_decay * momentum.astype(jnp.float32) + gradient.astype(jnp.floa...  2.85 us
    ppermute x3, starting transfers between devices, by_core(): return lax.ppermute(value, ('fsdp', axis), pairs)  2.75 us
    ppermute x13, waiting for transfers between devices, crossed(): lax.ppermute(value, axis, [(at, at ^ mask) for at in range(lax.axis_size(...  2.69 us
    pallas_call x1, Pallas kernels, partial_gram(): pl.pallas_call(partial_gram_kernel, out_shape=(shape, shape), in_specs=[p...  2.25 us
  transfers between devices with their start and end apart: 20, of which 7 were waited for; matrix products, arithmetic and copies ran while one was open for 5% of the time, Pallas kernels for 6%

profile of v3, /device:TPU:1, one launch (start us, length us, event | category | flops | bytes accessed | tf_op | source)
XLA Modules:
  0.0 63.3 jit_solution(8371710960372319732)
XLA Ops:
  0.6 2.3 %shard_map.68 = (f32[160,128]{1,0:T(8,128)}, f32[160,128]{1,0:T(8,128)}) custom-call(bf16[4,512,512]{2,1,0:T(8,128)(2,1)} %momentum_ref.1, bf16[4,512,512]{2,1,0:T(8,128)(2,1)} %gradient_ref.1), custom_call_target="tpu_custom_call" | custom-call | flops 41943040 | bytes 786432 | tf_op jit(solution)/shard_map/pallas_call | solution.py:78
  2.9 3.3 %collective-permute-start = (f32[160,128]{1,0:T(8,128)}, f32[160,128]{1,0:T(8,128)S(1)}, u32[]{:S(2)}, u32[]{:S(2)}) collective-permute-start(f32[160,128]{1,0:T(8,128)} %get-tuple-element.18), channel_id=1, source_target_pairs={{0,16},{16,0},{32,48},{48,32},{64,80},{80,64},{96,112},{112,96},{1... | collective-permute-start | bytes 245768 | tf_op jit(solution)/shard_map/ppermute | solution.py:318
  7.4 3.9 %collective-permute-start.3 = (f32[160,128]{1,0:T(8,128)S(1)}, f32[160,128]{1,0:T(8,128)S(1)}, u32[]{:S(2)}, u32[]{:S(2)}) collective-permute-start(f32[160,128]{1,0:T(8,128)S(1)} %add.15), channel_id=1, source_target_pairs={{0,96},{16,240},{32,64},{48,208},{64,32},{80,176},{96,0},{112,144}... | collective-permute-start | bytes 245768 | tf_op jit(solution)/shard_map/ppermute | solution.py:329
  11.9 1.1 %collective-permute-start.1 = (f32[160,128]{1,0:T(8,128)S(1)}, f32[160,128]{1,0:T(8,128)S(1)}, u32[]{:S(2)}, u32[]{:S(2)}) collective-permute-start(f32[160,128]{1,0:T(8,128)S(1)} %add.15), channel_id=1, source_target_pairs={{0,32},{16,48},{32,0},{48,16},{64,96},{80,112},{96,64},{112,80},{1... | collective-permute-start | bytes 245768 | tf_op jit(solution)/shard_map/ppermute | solution.py:329
  13.0 1.2 %collective-permute-start.4 = (f32[8,128]{1,0:T(8,128)S(1)}, f32[8,128]{1,0:T(8,128)S(1)}, u32[]{:S(2)}, u32[]{:S(2)}) collective-permute-start(f32[8,128]{1,0:T(8,128)S(1)} %broadcast_in_dim.37), channel_id=1, source_target_pairs={{0,1},{1,0},{2,3},{3,2},{4,5},{5,4},{6,7},{7,6},{8,9},{9,8},{10,11... | collective-permute-start | bytes 12296 | tf_op jit(solution)/shard_map/ppermute | solution.py:318
  14.2 2.8 %add_convert_fusion.momentum_ref = bf16[4,512,512]{2,1,0:T(8,128)(2,1)S(1)} fusion(bf16[4,512,512]{2,1,0:T(8,128)(2,1)} %gradient_ref.1, bf16[4,512,512]{2,1,0:T(8,128)(2,1)} %momentum_ref.1), kind=kLoop, calls=%fused_computation | loop fusion | flops 5242880 | bytes 6291456 | tf_op jit(solution)/shard_map/convert_element_type | solution.py:35
  17.1 2.0 %collective-permute-done.2 = f32[160,128]{1,0:T(8,128)S(1)} collective-permute-done((f32[160,128]{1,0:T(8,128)S(1)}, f32[160,128]{1,0:T(8,128)S(1)}, u32[]{:S(2)}, u32[]{:S(2)}) %collective-permute-start.2) | collective-permute-done | bytes 81952 | tf_op jit(solution)/shard_map/ppermute | solution.py:329
  19.1 1.7 %collective-permute-start.5 = (f32[160,128]{1,0:T(8,128)S(1)}, f32[160,128]{1,0:T(8,128)S(1)}, u32[]{:S(2)}, u32[]{:S(2)}) collective-permute-start(f32[160,128]{1,0:T(8,128)S(1)} %add_add_fusion.total_ref), channel_id=1, source_target_pairs={{0,224},{16,112},{32,192},{48,80},{64,160},{80,48},{96,128},{112,1... | collective-permute-start | bytes 245768 | tf_op jit(solution)/shard_map/ppermute | solution.py:329
  20.9 2.5 %collective-permute-start.6 = (f32[8,128]{1,0:T(8,128)S(1)}, f32[8,128]{1,0:T(8,128)S(1)}, u32[]{:S(2)}, u32[]{:S(2)}) collective-permute-start(f32[8,128]{1,0:T(8,128)S(1)} %max.3.peaks_ref), channel_id=1, source_target_pairs={{0,3},{1,2},{2,1},{3,0},{4,7},{5,6},{6,5},{7,4},{8,11},{9,10},{10,... | collective-permute-start | bytes 12296 | tf_op jit(solution)/shard_map/ppermute | solution.py:318
  23.3 1.2 %collective-permute-done.6.peaks_arrived_ref = f32[8,128]{1,0:T(8,128)S(1)} collective-permute-done((f32[8,128]{1,0:T(8,128)S(1)}, f32[8,128]{1,0:T(8,128)S(1)}, u32[]{:S(2)}, u32[]{:S(2)}) %collective-permute-start.6) | collective-permute-done | bytes 4128 | tf_op jit(solution)/shard_map/ppermute | solution.py:318
  24.6 2.8 %collective-permute-start.12 = (f32[168,128]{1,0:T(8,128)S(1)}, f32[168,128]{1,0:T(8,128)S(1)}, u32[]{:S(2)}, u32[]{:S(2)}) collective-permute-start(f32[168,128]{1,0:T(8,128)S(1)} %shard_map.70.refs_0_), channel_id=1, source_target_pairs={{0,12},{4,8},{8,4},{12,0},{1,13},{5,9},{9,5},{13,1},{2,14},{6,10},... | collective-permute-start | bytes 258056 | tf_op jit(solution)/shard_map/ppermute | solution.py:318
  28.0 2.0 %collective-permute-start.7 = (f32[168,128]{1,0:T(8,128)S(1)}, f32[168,128]{1,0:T(8,128)S(1)}, u32[]{:S(2)}, u32[]{:S(2)}) collective-permute-start(f32[168,128]{1,0:T(8,128)S(1)} %shard_map.70.refs_0_), channel_id=1, source_target_pairs={{0,16},{16,0},{32,48},{48,32},{64,80},{80,64},{96,112},{112,96},{1... | collective-permute-start | bytes 258056 | tf_op jit(solution)/shard_map/ppermute | solution.py:318
  30.1 1.9 %collective-permute-start.13 = (f32[168,128]{1,0:T(8,128)S(1)}, f32[168,128]{1,0:T(8,128)S(1)}, u32[]{:S(2)}, u32[]{:S(2)}) collective-permute-start(f32[168,128]{1,0:T(8,128)S(1)} %collective-permute-done.12.refs_6_), channel_id=1, source_target_pairs={{0,16},{16,0},{32,48},{48,32},{64,80},{80,64},{96,112},{112,96},{1... | collective-permute-start | bytes 258056 | tf_op jit(solution)/shard_map/ppermute | solution.py:318
  32.2 2.8 %collective-permute-start.11 = (f32[168,128]{1,0:T(8,128)S(1)}, f32[168,128]{1,0:T(8,128)S(1)}, u32[]{:S(2)}, u32[]{:S(2)}) collective-permute-start(f32[168,128]{1,0:T(8,128)S(1)} %collective-permute-done.10.refs_4_), channel_id=1, source_target_pairs={{0,16},{16,0},{32,48},{48,32},{64,80},{80,64},{96,112},{112,96},{1... | collective-permute-start | bytes 258056 | tf_op jit(solution)/shard_map/ppermute | solution.py:318
  35.0 0.9 %collective-permute-done.11.refs_5_ = f32[168,128]{1,0:T(8,128)S(1)} collective-permute-done((f32[168,128]{1,0:T(8,128)S(1)}, f32[168,128]{1,0:T(8,128)S(1)}, u32[]{:S(2)}, u32[]{:S(2)}) %collective-permute-start.11) | collective-permute-done | bytes 86048 | tf_op jit(solution)/shard_map/ppermute | solution.py:318
  36.3 12.0 %shard_map.71 = (bf16[656,128]{1,0:T(8,128)(2,1)S(1)}, bf16[656,128]{1,0:T(8,128)(2,1)S(1)}, f32[8,128]{1,0:T(8,128)S(1)}) custom-call(f32[168,128]{1,0:T(8,128)S(1)} %shard_map.70.refs_0_, f32[168,128]{1,0:T(8,128)S(1)} %collective-permute-done.7.refs_1_, f32[168,128]{1,0:T(8,128)S(1)} %collective-permute-done.8.refs_2_, ...), custom_call_target="tpu_custom_call" | custom-call | flops 13690208256 | bytes 1572864 | tf_op jit(solution)/shard_map/pallas_call | solution.py:204
  48.2 2.6 %collective-permute-start.14 = (bf16[656,128]{1,0:T(8,128)(2,1)S(1)}, bf16[656,128]{1,0:T(8,128)(2,1)S(1)}, u32[]{:S(2)}, u32[]{:S(2)}) collective-permute-start(bf16[656,128]{1,0:T(8,128)(2,1)S(1)} %get-tuple-element.26.first_ref), channel_id=1, source_target_pairs={{0,1},{1,0},{2,3},{3,2},{16,19},{17,18},{18,17},{19,16},{32,33},{3... | collective-permute-start | bytes 503816 | tf_op jit(solution)/shard_map/ppermute | solution.py:339
  51.0 1.3 %shard_map.72.refs_0_ = bf16[4,512,512]{2,1,0:T(8,128)(2,1)} custom-call(bf16[4,512,512]{2,1,0:T(8,128)(2,1)S(1)} %copy-done.1, bf16[4,512,512]{2,1,0:T(8,128)(2,1)S(1)} %add_convert_fusion.momentum_ref, f32[8,128]{1,0:T(8,128)S(1)} %get-tuple-element.25.peaks_ref, bf16[656,128]{1,0:T(8,128)(2,1)S(1)} %get-tuple-element.26.first_ref, ...), custom_call_target="tpu_custom_call" | custom-call | flops 268435456 | bytes 1572864 | tf_op jit(solution)/shard_map/pallas_call | solution.py:267
  52.3 1.4 %collective-permute-done.14.first_ref = bf16[656,128]{1,0:T(8,128)(2,1)S(1)} collective-permute-done((bf16[656,128]{1,0:T(8,128)(2,1)S(1)}, bf16[656,128]{1,0:T(8,128)(2,1)S(1)}, u32[]{:S(2)}, u32[]{:S(2)}) %collective-permute-start.14) | collective-permute-done | bytes 167968 | tf_op jit(solution)/shard_map/ppermute | solution.py:339
  53.7 2.8 %collective-permute-start.19 = (bf16[656,128]{1,0:T(8,128)(2,1)S(1)}, bf16[656,128]{1,0:T(8,128)(2,1)S(1)}, u32[]{:S(2)}, u32[]{:S(2)}) collective-permute-start(bf16[656,128]{1,0:T(8,128)(2,1)S(1)} %collective-permute-done.14.first_ref), channel_id=1, source_target_pairs={{0,16},{16,0},{32,48},{48,32},{64,80},{80,64},{96,112},{112,96},{1... | collective-permute-start | bytes 503816 | tf_op jit(solution)/shard_map/ppermute | solution.py:318
  56.6 1.3 %shard_map.73.refs_0_ = bf16[4,512,512]{2,1,0:T(8,128)(2,1)} custom-call(bf16[4,512,512]{2,1,0:T(8,128)(2,1)S(1)} %copy-done.1, bf16[4,512,512]{2,1,0:T(8,128)(2,1)S(1)} %add_convert_fusion.momentum_ref, f32[8,128]{1,0:T(8,128)S(1)} %get-tuple-element.25.peaks_ref, ...), custom_call_target="tpu_custom_call", output_to_operand_aliasing={{}: (5, {})} | custom-call | flops 268435456 | bytes 1572864 | tf_op jit(solution)/shard_map/pallas_call | solution.py:267
  58.2 2.2 %collective-permute-start.17 = (bf16[656,128]{1,0:T(8,128)(2,1)S(1)}, bf16[656,128]{1,0:T(8,128)(2,1)S(1)}, u32[]{:S(2)}, u32[]{:S(2)}) collective-permute-start(bf16[656,128]{1,0:T(8,128)(2,1)S(1)} %collective-permute-done.15.first_ref), channel_id=1, source_target_pairs={{0,16},{16,0},{32,48},{48,32},{64,80},{80,64},{96,112},{112,96},{1... | collective-permute-start | bytes 503816 | tf_op jit(solution)/shard_map/ppermute | solution.py:318
  60.4 1.4 %shard_map.74.refs_0_ = bf16[4,512,512]{2,1,0:T(8,128)(2,1)} custom-call(bf16[4,512,512]{2,1,0:T(8,128)(2,1)S(1)} %copy-done.1, bf16[4,512,512]{2,1,0:T(8,128)(2,1)S(1)} %add_convert_fusion.momentum_ref, f32[8,128]{1,0:T(8,128)S(1)} %get-tuple-element.25.peaks_ref, ...), custom_call_target="tpu_custom_call", output_to_operand_aliasing={{}: (5, {})} | custom-call | flops 268435456 | bytes 1572864 | tf_op jit(solution)/shard_map/pallas_call | solution.py:267
  61.8 1.3 %shard_map.75 = bf16[4,512,512]{2,1,0:T(8,128)(2,1)} custom-call(bf16[4,512,512]{2,1,0:T(8,128)(2,1)S(1)} %copy-done.1, bf16[4,512,512]{2,1,0:T(8,128)(2,1)S(1)} %add_convert_fusion.momentum_ref, f32[8,128]{1,0:T(8,128)S(1)} %get-tuple-element.25.peaks_ref, bf16[656,128]{1,0:T(8,128)(2,1)S(1)} %collective-permute-done.15.first_ref, ...), custom_call_target="tpu_custom_call", output_to_operand_aliasing={{}: (5, {})} | custom-call | flops 268435456 | bytes 1572864 | tf_op jit(solution)/shard_map/pallas_call | solution.py:267
  (42 shorter events, 3.6 us)
Async XLA Ops:
  0.6 5.6 %copy-start.4 = (s32[4]{0:T(128)S(1)}, s32[4]{0:T(128)}, u32[]{:S(2)}) copy-start(s32[4]{0:T(128)} %param.9) | copy-start | bytes 52
  0.6 5.7 %copy-start.3 = (f32[1,1,61,32]{2,3,1,0:T(8,128)S(1)}, f32[1,1,61,32]{2,3,1,0:T(8,128)}, u32[]{:S(2)}) copy-start(f32[1,1,61,32]{2,3,1,0:T(8,128)} %param.8) | copy-start | bytes 23428
  2.9 4.5 %collective-permute-start = (f32[160,128]{1,0:T(8,128)}, f32[160,128]{1,0:T(8,128)S(1)}, u32[]{:S(2)}, u32[]{:S(2)}) collective-permute-start(f32[160,128]{1,0:T(8,128)} %get-tuple-element.18), channel_id=1, source_target_pairs={{0,16},{16,0},{32,48},{48,32},{64,80},{80,64},{96,112},{112,96},{1... | collective-permute-start | bytes 245768 | tf_op jit(solution)/shard_map/ppermute | solution.py:318
  7.4 9.7 %collective-permute-start.3 = (f32[160,128]{1,0:T(8,128)S(1)}, f32[160,128]{1,0:T(8,128)S(1)}, u32[]{:S(2)}, u32[]{:S(2)}) collective-permute-start(f32[160,128]{1,0:T(8,128)S(1)} %add.15), channel_id=1, source_target_pairs={{0,96},{16,240},{32,64},{48,208},{64,32},{80,176},{96,0},{112,144}... | collective-permute-start | bytes 245768 | tf_op jit(solution)/shard_map/ppermute | solution.py:329
  11.4 7.8 %collective-permute-start.2 = (f32[160,128]{1,0:T(8,128)S(1)}, f32[160,128]{1,0:T(8,128)S(1)}, u32[]{:S(2)}, u32[]{:S(2)}) collective-permute-start(f32[160,128]{1,0:T(8,128)S(1)} %add.15), channel_id=1, source_target_pairs={{0,64},{16,208},{32,96},{48,240},{64,0},{80,144},{96,32},{112,176}... | collective-permute-start | bytes 245768 | tf_op jit(solution)/shard_map/ppermute | solution.py:329
  11.9 7.2 %collective-permute-start.1 = (f32[160,128]{1,0:T(8,128)S(1)}, f32[160,128]{1,0:T(8,128)S(1)}, u32[]{:S(2)}, u32[]{:S(2)}) collective-permute-start(f32[160,128]{1,0:T(8,128)S(1)} %add.15), channel_id=1, source_target_pairs={{0,32},{16,48},{32,0},{48,16},{64,96},{80,112},{96,64},{112,80},{1... | collective-permute-start | bytes 245768 | tf_op jit(solution)/shard_map/ppermute | solution.py:329
  13.0 4.1 %collective-permute-start.4 = (f32[8,128]{1,0:T(8,128)S(1)}, f32[8,128]{1,0:T(8,128)S(1)}, u32[]{:S(2)}, u32[]{:S(2)}) collective-permute-start(f32[8,128]{1,0:T(8,128)S(1)} %broadcast_in_dim.37), channel_id=1, source_target_pairs={{0,1},{1,0},{2,3},{3,2},{4,5},{5,4},{6,7},{7,6},{8,9},{9,8},{10,11... | collective-permute-start | bytes 12296 | tf_op jit(solution)/shard_map/ppermute | solution.py:318
  17.1 44.7 %copy-start = (bf16[4,512,512]{2,1,0:T(8,128)(2,1)}, bf16[4,512,512]{2,1,0:T(8,128)(2,1)S(1)}, u32[]{:S(2)}) copy-start(bf16[4,512,512]{2,1,0:T(8,128)(2,1)S(1)} %add_convert_fusion.momentum_ref) | copy-start | bytes 6291460
  19.1 5.4 %collective-permute-start.5 = (f32[160,128]{1,0:T(8,128)S(1)}, f32[160,128]{1,0:T(8,128)S(1)}, u32[]{:S(2)}, u32[]{:S(2)}) collective-permute-start(f32[160,128]{1,0:T(8,128)S(1)} %add_add_fusion.total_ref), channel_id=1, source_target_pairs={{0,224},{16,112},{32,192},{48,80},{64,160},{80,48},{96,128},{112,1... | collective-permute-start | bytes 245768 | tf_op jit(solution)/shard_map/ppermute | solution.py:329
  20.9 3.7 %collective-permute-start.6 = (f32[8,128]{1,0:T(8,128)S(1)}, f32[8,128]{1,0:T(8,128)S(1)}, u32[]{:S(2)}, u32[]{:S(2)}) collective-permute-start(f32[8,128]{1,0:T(8,128)S(1)} %max.3.peaks_ref), channel_id=1, source_target_pairs={{0,3},{1,2},{2,1},{3,0},{4,7},{5,6},{6,5},{7,4},{8,11},{9,10},{10,... | collective-permute-start | bytes 12296 | tf_op jit(solution)/shard_map/ppermute | solution.py:318
  24.5 26.5 %copy-start.1 = (bf16[4,512,512]{2,1,0:T(8,128)(2,1)S(1)}, bf16[4,512,512]{2,1,0:T(8,128)(2,1)}, u32[]{:S(2)}) copy-start(bf16[4,512,512]{2,1,0:T(8,128)(2,1)} %weights_ref.7) | copy-start | bytes 6291460
  24.6 5.5 %collective-permute-start.12 = (f32[168,128]{1,0:T(8,128)S(1)}, f32[168,128]{1,0:T(8,128)S(1)}, u32[]{:S(2)}, u32[]{:S(2)}) collective-permute-start(f32[168,128]{1,0:T(8,128)S(1)} %shard_map.70.refs_0_), channel_id=1, source_target_pairs={{0,12},{4,8},{8,4},{12,0},{1,13},{5,9},{9,5},{13,1},{2,14},{6,10},... | collective-permute-start | bytes 258056 | tf_op jit(solution)/shard_map/ppermute | solution.py:318
  27.4 4.8 %collective-permute-start.10 = (f32[168,128]{1,0:T(8,128)S(1)}, f32[168,128]{1,0:T(8,128)S(1)}, u32[]{:S(2)}, u32[]{:S(2)}) collective-permute-start(f32[168,128]{1,0:T(8,128)S(1)} %shard_map.70.refs_0_), channel_id=1, source_target_pairs={{0,8},{4,12},{8,0},{12,4},{1,9},{5,13},{9,1},{13,5},{2,10},{6,14},... | collective-permute-start | bytes 258056 | tf_op jit(solution)/shard_map/ppermute | solution.py:318
  27.7 7.3 %collective-permute-start.8 = (f32[168,128]{1,0:T(8,128)S(1)}, f32[168,128]{1,0:T(8,128)S(1)}, u32[]{:S(2)}, u32[]{:S(2)}) collective-permute-start(f32[168,128]{1,0:T(8,128)S(1)} %shard_map.70.refs_0_), channel_id=1, source_target_pairs={{0,4},{4,0},{8,12},{12,8},{1,5},{5,1},{9,13},{13,9},{2,6},{6,2},{1... | collective-permute-start | bytes 258056 | tf_op jit(solution)/shard_map/ppermute | solution.py:318
  28.0 6.9 %collective-permute-start.7 = (f32[168,128]{1,0:T(8,128)S(1)}, f32[168,128]{1,0:T(8,128)S(1)}, u32[]{:S(2)}, u32[]{:S(2)}) collective-permute-start(f32[168,128]{1,0:T(8,128)S(1)} %shard_map.70.refs_0_), channel_id=1, source_target_pairs={{0,16},{16,0},{32,48},{48,32},{64,80},{80,64},{96,112},{112,96},{1... | collective-permute-start | bytes 258056 | tf_op jit(solution)/shard_map/ppermute | solution.py:318
  30.1 4.9 %collective-permute-start.13 = (f32[168,128]{1,0:T(8,128)S(1)}, f32[168,128]{1,0:T(8,128)S(1)}, u32[]{:S(2)}, u32[]{:S(2)}) collective-permute-start(f32[168,128]{1,0:T(8,128)S(1)} %collective-permute-done.12.refs_6_), channel_id=1, source_target_pairs={{0,16},{16,0},{32,48},{48,32},{64,80},{80,64},{96,112},{112,96},{1... | collective-permute-start | bytes 258056 | tf_op jit(solution)/shard_map/ppermute | solution.py:318
  32.2 3.7 %collective-permute-start.11 = (f32[168,128]{1,0:T(8,128)S(1)}, f32[168,128]{1,0:T(8,128)S(1)}, u32[]{:S(2)}, u32[]{:S(2)}) collective-permute-start(f32[168,128]{1,0:T(8,128)S(1)} %collective-permute-done.10.refs_4_), channel_id=1, source_target_pairs={{0,16},{16,0},{32,48},{48,32},{64,80},{80,64},{96,112},{112,96},{1... | collective-permute-start | bytes 258056 | tf_op jit(solution)/shard_map/ppermute | solution.py:318
  35.0 1.3 %collective-permute-start.9 = (f32[168,128]{1,0:T(8,128)S(1)}, f32[168,128]{1,0:T(8,128)S(1)}, u32[]{:S(2)}, u32[]{:S(2)}) collective-permute-start(f32[168,128]{1,0:T(8,128)S(1)} %collective-permute-done.8.refs_2_), channel_id=1, source_target_pairs={{0,16},{16,0},{32,48},{48,32},{64,80},{80,64},{96,112},{112,96},{1... | collective-permute-start | bytes 258056 | tf_op jit(solution)/shard_map/ppermute | solution.py:318
  48.2 5.5 %collective-permute-start.14 = (bf16[656,128]{1,0:T(8,128)(2,1)S(1)}, bf16[656,128]{1,0:T(8,128)(2,1)S(1)}, u32[]{:S(2)}, u32[]{:S(2)}) collective-permute-start(bf16[656,128]{1,0:T(8,128)(2,1)S(1)} %get-tuple-element.26.first_ref), channel_id=1, source_target_pairs={{0,1},{1,0},{2,3},{3,2},{16,19},{17,18},{18,17},{19,16},{32,33},{3... | collective-permute-start | bytes 503816 | tf_op jit(solution)/shard_map/ppermute | solution.py:339
  50.8 5.8 %collective-permute-start.16 = (bf16[656,128]{1,0:T(8,128)(2,1)S(1)}, bf16[656,128]{1,0:T(8,128)(2,1)S(1)}, u32[]{:S(2)}, u32[]{:S(2)}) collective-permute-start(bf16[656,128]{1,0:T(8,128)(2,1)S(1)} %get-tuple-element.27.second_ref), channel_id=1, source_target_pairs={{0,1},{1,0},{2,3},{3,2},{16,19},{17,18},{18,17},{19,16},{32,33},{3... | collective-permute-start | bytes 503816 | tf_op jit(solution)/shard_map/ppermute | solution.py:339
  53.7 4.5 %collective-permute-start.15 = (bf16[656,128]{1,0:T(8,128)(2,1)S(1)}, bf16[656,128]{1,0:T(8,128)(2,1)S(1)}, u32[]{:S(2)}, u32[]{:S(2)}) collective-permute-start(bf16[656,128]{1,0:T(8,128)(2,1)S(1)} %collective-permute-done.14.first_ref), channel_id=1, source_target_pairs={{0,3},{1,2},{2,1},{3,0},{16,17},{17,16},{18,19},{19,18},{32,35},{3... | collective-permute-start | bytes 503816 | tf_op jit(solution)/shard_map/ppermute | solution.py:339
  53.7 6.7 %collective-permute-start.19 = (bf16[656,128]{1,0:T(8,128)(2,1)S(1)}, bf16[656,128]{1,0:T(8,128)(2,1)S(1)}, u32[]{:S(2)}, u32[]{:S(2)}) collective-permute-start(bf16[656,128]{1,0:T(8,128)(2,1)S(1)} %collective-permute-done.14.first_ref), channel_id=1, source_target_pairs={{0,16},{16,0},{32,48},{48,32},{64,80},{80,64},{96,112},{112,96},{1... | collective-permute-start | bytes 503816 | tf_op jit(solution)/shard_map/ppermute | solution.py:318
  56.6 3.8 %collective-permute-start.18 = (bf16[656,128]{1,0:T(8,128)(2,1)S(1)}, bf16[656,128]{1,0:T(8,128)(2,1)S(1)}, u32[]{:S(2)}, u32[]{:S(2)}) collective-permute-start(bf16[656,128]{1,0:T(8,128)(2,1)S(1)} %collective-permute-done.16.second_ref), channel_id=1, source_target_pairs={{0,16},{16,0},{32,48},{48,32},{64,80},{80,64},{96,112},{112,96},{1... | collective-permute-start | bytes 503816 | tf_op jit(solution)/shard_map/ppermute | solution.py:318
  58.2 3.5 %collective-permute-start.17 = (bf16[656,128]{1,0:T(8,128)(2,1)S(1)}, bf16[656,128]{1,0:T(8,128)(2,1)S(1)}, u32[]{:S(2)}, u32[]{:S(2)}) collective-permute-start(bf16[656,128]{1,0:T(8,128)(2,1)S(1)} %collective-permute-done.15.first_ref), channel_id=1, source_target_pairs={{0,16},{16,0},{32,48},{48,32},{64,80},{80,64},{96,112},{112,96},{1... | collective-permute-start | bytes 503816 | tf_op jit(solution)/shard_map/ppermute | solution.py:318
  (1 other events, 0.9 us)

commit v4 on v3

--- a/solution.py
+++ b/solution.py
@@ -23,7 +23,8 @@
 
 BLOCK = 128
 BLOCKS = 4
-PART = 160
+HALF_BLOCK = 64
+PART = 144
 TAIL = 8
 HALF = 640
 END = 16
@@ -62,11 +63,16 @@
     early = dp_at < BLOCKS // 2
     far_rows = jnp.where(early, 0, 5)
     far_columns = jnp.where(early, 2, 0)
-    packed[2 * BLOCK :, :] = gram(
+    packed[7 * HALF_BLOCK // 2 :, :] = gram(
         fresh[pl.ds(aligned(far_rows, BLOCK // 2), BLOCK // 2), :], fresh[pl.ds(aligned(far_columns, BLOCK), BLOCK), :]
     )
-    packed[0:BLOCK, :] = gram(fresh[0:BLOCK, :], fresh[0:BLOCK, :])
-    packed[BLOCK : 2 * BLOCK, :] = gram(fresh[0:BLOCK, :], fresh[BLOCK : 2 * BLOCK, :])
+    own = gram(fresh[0:BLOCK, :], fresh[0:BLOCK, :])
+    packed[0:HALF_BLOCK, :] = own[0:HALF_BLOCK, :]
+    quarter = HALF_BLOCK // 2
+    left_half = lax.broadcasted_iota(jnp.int32, (quarter, BLOCK), 1) < HALF_BLOCK
+    third, fourth = own[2 * quarter : 3 * quarter, :], own[3 * quarter :, :]
+    packed[HALF_BLOCK : 3 * quarter, :] = jnp.where(left_half, pltpu.roll(third, HALF_BLOCK, 1), fourth)
+    packed[3 * quarter : 3 * quarter + BLOCK, :] = gram(fresh[0:BLOCK, :], fresh[BLOCK : 2 * BLOCK, :])
     keep_ref[...] = packed[pl.ds(aligned(core, PART), PART), :]
     send_ref[...] = packed[pl.ds(aligned(1 - core, PART), PART), :]
 
@@ -116,27 +122,37 @@
             stacks[dp_at ^ turn, pl.ds(aligned(half, PART), PART), :] = piece[0:PART, :]
     peaks_ref[...] = functools.reduce(jnp.maximum, [pair[0][PART:, :] for pair in parts])
 
+    quarter = HALF_BLOCK // 2
+    rows_in = lax.broadcasted_iota(jnp.int32, (BLOCK, BLOCK), 0)
+    columns_in = lax.broadcasted_iota(jnp.int32, (BLOCK, BLOCK), 1)
+    missing = (rows_in >= HALF_BLOCK) & (columns_in < HALF_BLOCK)
+
     def own_block(block):
-        return stacks[block, 0:BLOCK, :]
+        low = stacks[block, HALF_BLOCK : 3 * quarter, :]
+        return jnp.concatenate([stacks[block, 0:HALF_BLOCK, :], pltpu.roll(low, HALF_BLOCK, 1), low], axis=0)
 
     def beside(block):
-        return stacks[block, BLOCK : 2 * BLOCK, :]
-
-    eye = lax.broadcasted_iota(jnp.int32, (BLOCK, BLOCK), 0) == lax.broadcasted_iota(jnp.int32, (BLOCK, BLOCK), 1)
-    diagonal = (own_block(0) + own_block(1)) + (own_block(2) + own_block(3))
-    norm = jnp.sqrt(jnp.full((1, 1), jnp.sum(jnp.where(eye, diagonal, 0.0)), jnp.float32)) + norm_eps
+        return stacks[block, 3 * quarter : 3 * quarter + BLOCK, :]
+
+    def far(block):
+        return stacks[block, 3 * quarter + BLOCK :, :]
+
+    owns = [own_block(block) for block in range(BLOCKS)]
+    diagonal = (owns[0] + owns[1]) + (owns[2] + owns[3])
+    trace = jnp.sum(jnp.where(rows_in == columns_in, diagonal, 0.0))
+    norm = jnp.sqrt(jnp.full((1, 1), trace, jnp.float32)) + norm_eps
     inverse = 1.0 / (norm * norm)
 
     def place(row, column, value):
         a_now[row * BLOCK : (row + 1) * BLOCK, column * BLOCK : (column + 1) * BLOCK] = value
 
     for block in range(BLOCKS):
-        place(block, block, own_block(block) * inverse)
+        place(block, block, jnp.where(missing, owns[block].T, owns[block]))
         after = (block + 1) % BLOCKS
-        place(block, after, beside(block) * inverse)
-        place(after, block, beside(block).T * inverse)
+        place(block, after, beside(block))
+        place(after, block, beside(block).T)
     for block in range(2):
-        far_block = jnp.concatenate([stacks[block, 2 * BLOCK :, :], stacks[block + 2, 2 * BLOCK :, :]], axis=0) * inverse
+        far_block = jnp.concatenate([far(block), far(block + 2)], axis=0)
         place(block, block + 2, far_block)
         place(block + 2, block, far_block.T)
 
@@ -147,11 +163,14 @@
     dot = functools.partial(jnp.dot, preferred_element_type=jnp.float32)
 
     def keep(pair, rows, columns, value):
-        pair[0, rows, columns], pair[1, rows, columns] = split_in_two(value)
+        strip = rows.start // mid
+        pair[strip, 0, :, columns], pair[strip, 1, :, columns] = split_in_two(value)
 
     def product(left, right, rows, columns):
-        high, low = left[0, rows, :], left[1, rows, :]
-        return dot(high, right[0, :, columns]) + (dot(high, right[1, :, columns]) + dot(low, right[0, :, columns]))
+        strip = rows.start // mid
+        high, low = [right[:, term, :, columns].reshape(rank, -1) for term in range(2)]
+        both = dot(left[strip].reshape(rank, rank), high)
+        return both[0:mid] + (both[mid:] + dot(left[strip, 0], low))
 
     def whole_product(left, right, target, finish=None):
         for rows, columns in ((first, slice(0, rank)), (last, last)):
@@ -165,6 +184,12 @@
     def to_factor(square, rows, columns):
         return shift[:, 0 : square.shape[1]] + quintic_b * a_now[rows, columns] + quintic_c * square
 
+    def to_first_factor(square, rows, columns):
+        return shift[:, 0 : square.shape[1]] + (quintic_b * inverse) * a_now[rows, columns] + (quintic_c * inverse) * (square * inverse)
+
+    def scaled(value, rows, columns):
+        return value * inverse
+
     def store(value, rows, columns):
         a_now[rows, columns] = value
         return value
@@ -172,8 +197,8 @@
     for rows in (first, last):
         keep(pair_a, rows, slice(0, rank), a_now[rows, :])
     for iteration in range(ITERS - 1):
-        whole_product(pair_a, pair_a, pair_q, to_factor)
-        whole_product(pair_q, pair_a, pair_b)
+        whole_product(pair_a, pair_a, pair_q, to_factor if iteration else to_first_factor)
+        whole_product(pair_q, pair_a, pair_b, None if iteration else scaled)
         whole_product(pair_b, pair_q, pair_a, store)
         if iteration == 0:
             pair_p[...] = pair_q[...]
@@ -199,7 +224,7 @@
 
 def newton(parts, rank):
     whole = pl.BlockSpec(memory_space=pltpu.VMEM)
-    pair = pltpu.VMEM((2, rank, rank), jnp.bfloat16)
+    pair = pltpu.VMEM((2, 2, rank // 2, rank), jnp.bfloat16)
     piece = jax.ShapeDtypeStruct((HALF + END, BLOCK), jnp.bfloat16)
     return pl.pallas_call(
         newton_kernel,
@@ -354,17 +379,18 @@
 
     keep, send = partial_gram(momentum, gradient)
     total = fetch(keep) + swapped(send)
-    total, peaks, late_momentum = lax.optimization_barrier((total, peaks, momentum))
+    total, peaks = lax.optimization_barrier((total, peaks))
     third, second, first = along_z(total, 3), along_z(total, 2), along_z(total, 1)
     total = (total + first) + (second + third)
     peaks = jnp.maximum(peaks, crossed(peaks, "ctx", 1))
-    new_momentum = decayed(late_momentum, gradient)
-    total, peaks, new_momentum = lax.optimization_barrier((total, peaks, new_momentum))
+    total, peaks = lax.optimization_barrier((total, peaks))
     mine = join(total, along_z(total, 7), peaks, crossed(peaks, "ctx", 3))
     halves = [mine] + [crossed(mine, "dp", mask) for mask in (1, 2, 3)]
     first, second, peaks = newton([piece for one in halves for piece in (one, swapped(one))], rank)
     update_scale = rms_factor * math.sqrt(max(rank, cols * fsdp))
     last = functools.partial(last_product, update_scale)
+    peaks, late_momentum = lax.optimization_barrier((peaks, momentum))
+    new_momentum = decayed(late_momentum, gradient)
     near = tuple(by_core(piece, "ctx", (1, 3)) for piece in (first, second))
     new_weights = last((0, 0), weights, new_momentum, peaks, (first, second), None)
     near_first, new_weights = lax.optimization_barrier((near[0], new_weights))

time: 63.5 us -> 62.6 us (0.986)
  other arithmetic: 3.06 us -> 0.87 us
  waiting for transfers between devices: 6.42 us -> 8.2 us
  starting transfers between devices: 32.3 us -> 31.3 us
  local copies, waits for them, and re-layouts: 1 us -> 1.72 us
    convert_element_type x1, other arithmetic: 2.85 us -> 0.66 us  [decayed(): (momentum_decay * momentum.astype(jnp.float32) + gradient.astype(jnp.floa...]
    ppermute x13, waiting for transfers between devices: 2.69 us -> 4.38 us  [crossed(): lax.ppermute(value, axis, [(at, at ^ mask) for at in range(lax.axis_size(...]
    ppermute x13, starting transfers between devices: 22.2 us -> 21 us  [crossed(): lax.ppermute(value, axis, [(at, at ^ mask) for at in range(lax.axis_size(...]
    ppermute x4, waiting for transfers between devices: 2.02 us -> 3.03 us  [along_z(): return lax.ppermute(value, 'fsdp', pairs)]
    ppermute x3, waiting for transfers between devices: 1.7 us -> 0.78 us  [by_core(): return lax.ppermute(value, ('fsdp', axis), pairs)]
    unnamed x10 -> x14, local copies, waits for them, and re-layouts: 0.91 us -> 1.63 us
  transfers between devices with their start and end apart: 20 -> 20, of which waited for: 7 -> 7; matrix products, arithmetic and copies ran while one was open for 5% -> 1% of each run, Pallas kernels for 6% -> 7%
where the time goes in v4:
time: 62.6 us; the launch traced here: 62.4 us
  starting transfers between devices  31.3 us (50%)
  Pallas kernels  19.3 us (31%)
  waiting for transfers between devices  8.2 us (13%)
  local copies, waits for them, and re-layouts  1.72 us (3%)
  between operations  0.98 us (2%)
  other arithmetic  0.87 us (1%)
    ppermute x13, starting transfers between devices, crossed(): lax.ppermute(value, axis, [(at, at ^ mask) for at in range(lax.axis_size(...  21 us
    pallas_call x1, Pallas kernels, newton(): pl.pallas_call(newton_kernel, out_shape=(piece, piece, jax.ShapeDtypeStru...  11.5 us
    ppermute x4, starting transfers between devices, along_z(): return lax.ppermute(value, 'fsdp', pairs)  7.27 us
    pallas_call x4, Pallas kernels, last_product(): pl.pallas_call(functools.partial(last_kernel, update_scale, masks), out_s...  5.53 us
    ppermute x13, waiting for transfers between devices, crossed(): lax.ppermute(value, axis, [(at, at ^ mask) for at in range(lax.axis_size(...  4.38 us
    ppermute x3, starting transfers between devices, by_core(): return lax.ppermute(value, ('fsdp', axis), pairs)  3.06 us
    ppermute x4, waiting for transfers between devices, along_z(): return lax.ppermute(value, 'fsdp', pairs)  3.03 us
    pallas_call x1, Pallas kernels, partial_gram(): pl.pallas_call(partial_gram_kernel, out_shape=(shape, shape), in_specs=[p...  2.28 us
  transfers between devices with their start and end apart: 20, of which 7 were waited for; matrix products, arithmetic and copies ran while one was open for 1% of the time, Pallas kernels for 7%

profile of v4, /device:TPU:1, one launch (start us, length us, event | category | flops | bytes accessed | tf_op | source)
XLA Modules:
  0.0 62.4 jit_solution(7724246542140636193)
XLA Ops:
  0.6 2.3 %shard_map.68 = (f32[144,128]{1,0:T(8,128)}, f32[144,128]{1,0:T(8,128)}) custom-call(bf16[4,512,512]{2,1,0:T(8,128)(2,1)} %momentum_ref.1, bf16[4,512,512]{2,1,0:T(8,128)(2,1)} %gradient_ref.1), custom_call_target="tpu_custom_call" | custom-call | flops 37748736 | bytes 786432 | tf_op jit(solution)/shard_map/pallas_call | solution.py:84
  2.9 3.3 %collective-permute-start = (f32[144,128]{1,0:T(8,128)}, f32[144,128]{1,0:T(8,128)S(1)}, u32[]{:S(2)}, u32[]{:S(2)}) collective-permute-start(f32[144,128]{1,0:T(8,128)} %get-tuple-element.18), channel_id=1, source_target_pairs={{0,16},{16,0},{32,48},{48,32},{64,80},{80,64},{96,112},{112,96},{1... | collective-permute-start | bytes 221192 | tf_op jit(solution)/shard_map/ppermute | solution.py:343
  6.5 0.9 %copy-done.2 = f32[144,128]{1,0:T(8,128)S(1)} copy-done((f32[144,128]{1,0:T(8,128)S(1)}, f32[144,128]{1,0:T(8,128)}, u32[]{:S(2)}) %copy-start.2) | copy-done | bytes 73752
  7.5 3.9 %collective-permute-start.3 = (f32[144,128]{1,0:T(8,128)S(1)}, f32[144,128]{1,0:T(8,128)S(1)}, u32[]{:S(2)}, u32[]{:S(2)}) collective-permute-start(f32[144,128]{1,0:T(8,128)S(1)} %add.15), channel_id=1, source_target_pairs={{0,96},{16,240},{32,64},{48,208},{64,32},{80,176},{96,0},{112,144}... | collective-permute-start | bytes 221192 | tf_op jit(solution)/shard_map/ppermute | solution.py:354
  11.9 1.1 %collective-permute-start.1 = (f32[144,128]{1,0:T(8,128)S(1)}, f32[144,128]{1,0:T(8,128)S(1)}, u32[]{:S(2)}, u32[]{:S(2)}) collective-permute-start(f32[144,128]{1,0:T(8,128)S(1)} %add.15), channel_id=1, source_target_pairs={{0,32},{16,48},{32,0},{48,16},{64,96},{80,112},{96,64},{112,80},{1... | collective-permute-start | bytes 221192 | tf_op jit(solution)/shard_map/ppermute | solution.py:354
  13.0 1.2 %collective-permute-start.4 = (f32[8,128]{1,0:T(8,128)S(1)}, f32[8,128]{1,0:T(8,128)S(1)}, u32[]{:S(2)}, u32[]{:S(2)}) collective-permute-start(f32[8,128]{1,0:T(8,128)S(1)} %broadcast_in_dim.37), channel_id=1, source_target_pairs={{0,1},{1,0},{2,3},{3,2},{4,5},{5,4},{6,7},{7,6},{8,9},{9,8},{10,11... | collective-permute-start | bytes 12296 | tf_op jit(solution)/shard_map/ppermute | solution.py:343
  14.2 1.5 %collective-permute-done.4 = f32[8,128]{1,0:T(8,128)S(1)} collective-permute-done((f32[8,128]{1,0:T(8,128)S(1)}, f32[8,128]{1,0:T(8,128)S(1)}, u32[]{:S(2)}, u32[]{:S(2)}) %collective-permute-start.4) | collective-permute-done | bytes 4128 | tf_op jit(solution)/shard_map/ppermute | solution.py:343
  15.8 3.0 %collective-permute-done.2 = f32[144,128]{1,0:T(8,128)S(1)} collective-permute-done((f32[144,128]{1,0:T(8,128)S(1)}, f32[144,128]{1,0:T(8,128)S(1)}, u32[]{:S(2)}, u32[]{:S(2)}) %collective-permute-start.2) | collective-permute-done | bytes 73760 | tf_op jit(solution)/shard_map/ppermute | solution.py:354
  18.8 1.7 %collective-permute-start.5 = (f32[144,128]{1,0:T(8,128)S(1)}, f32[144,128]{1,0:T(8,128)S(1)}, u32[]{:S(2)}, u32[]{:S(2)}) collective-permute-start(f32[144,128]{1,0:T(8,128)S(1)} %add_add_fusion.total_ref), channel_id=1, source_target_pairs={{0,224},{16,112},{32,192},{48,80},{64,160},{80,48},{96,128},{112,1... | collective-permute-start | bytes 221192 | tf_op jit(solution)/shard_map/ppermute | solution.py:354
  20.5 2.5 %collective-permute-start.6 = (f32[8,128]{1,0:T(8,128)S(1)}, f32[8,128]{1,0:T(8,128)S(1)}, u32[]{:S(2)}, u32[]{:S(2)}) collective-permute-start(f32[8,128]{1,0:T(8,128)S(1)} %max.3.peaks_ref), channel_id=1, source_target_pairs={{0,3},{1,2},{2,1},{3,0},{4,7},{5,6},{6,5},{7,4},{8,11},{9,10},{10,... | collective-permute-start | bytes 12296 | tf_op jit(solution)/shard_map/ppermute | solution.py:343
  23.0 1.2 %collective-permute-done.6.peaks_arrived_ref = f32[8,128]{1,0:T(8,128)S(1)} collective-permute-done((f32[8,128]{1,0:T(8,128)S(1)}, f32[8,128]{1,0:T(8,128)S(1)}, u32[]{:S(2)}, u32[]{:S(2)}) %collective-permute-start.6) | collective-permute-done | bytes 4128 | tf_op jit(solution)/shard_map/ppermute | solution.py:343
  24.2 2.8 %collective-permute-start.12 = (f32[152,128]{1,0:T(8,128)S(1)}, f32[152,128]{1,0:T(8,128)S(1)}, u32[]{:S(2)}, u32[]{:S(2)}) collective-permute-start(f32[152,128]{1,0:T(8,128)S(1)} %shard_map.70.refs_0_), channel_id=1, source_target_pairs={{0,12},{4,8},{8,4},{12,0},{1,13},{5,9},{9,5},{13,1},{2,14},{6,10},... | collective-permute-start | bytes 233480 | tf_op jit(solution)/shard_map/ppermute | solution.py:343
  27.7 2.0 %collective-permute-start.7 = (f32[152,128]{1,0:T(8,128)S(1)}, f32[152,128]{1,0:T(8,128)S(1)}, u32[]{:S(2)}, u32[]{:S(2)}) collective-permute-start(f32[152,128]{1,0:T(8,128)S(1)} %shard_map.70.refs_0_), channel_id=1, source_target_pairs={{0,16},{16,0},{32,48},{48,32},{64,80},{80,64},{96,112},{112,96},{1... | collective-permute-start | bytes 233480 | tf_op jit(solution)/shard_map/ppermute | solution.py:343
  29.7 1.7 %collective-permute-start.13 = (f32[152,128]{1,0:T(8,128)S(1)}, f32[152,128]{1,0:T(8,128)S(1)}, u32[]{:S(2)}, u32[]{:S(2)}) collective-permute-start(f32[152,128]{1,0:T(8,128)S(1)} %collective-permute-done.12.refs_6_), channel_id=1, source_target_pairs={{0,16},{16,0},{32,48},{48,32},{64,80},{80,64},{96,112},{112,96},{1... | collective-permute-start | bytes 233480 | tf_op jit(solution)/shard_map/ppermute | solution.py:343
  31.8 2.7 %collective-permute-start.11 = (f32[152,128]{1,0:T(8,128)S(1)}, f32[152,128]{1,0:T(8,128)S(1)}, u32[]{:S(2)}, u32[]{:S(2)}) collective-permute-start(f32[152,128]{1,0:T(8,128)S(1)} %collective-permute-done.10.refs_4_), channel_id=1, source_target_pairs={{0,16},{16,0},{32,48},{48,32},{64,80},{80,64},{96,112},{112,96},{1... | collective-permute-start | bytes 233480 | tf_op jit(solution)/shard_map/ppermute | solution.py:343
  34.6 0.9 %collective-permute-done.11.refs_5_ = f32[152,128]{1,0:T(8,128)S(1)} collective-permute-done((f32[152,128]{1,0:T(8,128)S(1)}, f32[152,128]{1,0:T(8,128)S(1)}, u32[]{:S(2)}, u32[]{:S(2)}) %collective-permute-start.11) | collective-permute-done | bytes 77856 | tf_op jit(solution)/shard_map/ppermute | solution.py:343
  35.8 11.5 %shard_map.71 = (bf16[656,128]{1,0:T(8,128)(2,1)S(1)}, bf16[656,128]{1,0:T(8,128)(2,1)S(1)}, f32[8,128]{1,0:T(8,128)S(1)}) custom-call(f32[152,128]{1,0:T(8,128)S(1)} %shard_map.70.refs_0_, f32[152,128]{1,0:T(8,128)S(1)} %collective-permute-done.7.refs_1_, f32[152,128]{1,0:T(8,128)S(1)} %collective-permute-done.8.refs_2_, ...), custom_call_target="tpu_custom_call" | custom-call | flops 13690208256 | bytes 1572864 | tf_op jit(solution)/shard_map/pallas_call | solution.py:229
  47.3 2.6 %collective-permute-start.14 = (bf16[656,128]{1,0:T(8,128)(2,1)S(1)}, bf16[656,128]{1,0:T(8,128)(2,1)S(1)}, u32[]{:S(2)}, u32[]{:S(2)}) collective-permute-start(bf16[656,128]{1,0:T(8,128)(2,1)S(1)} %get-tuple-element.26.first_ref), channel_id=1, source_target_pairs={{0,1},{1,0},{2,3},{3,2},{16,19},{17,18},{18,17},{19,16},{32,33},{3... | collective-permute-start | bytes 503816 | tf_op jit(solution)/shard_map/ppermute | solution.py:364
  51.5 1.5 %shard_map.72.refs_0_ = bf16[4,512,512]{2,1,0:T(8,128)(2,1)} custom-call(bf16[4,512,512]{2,1,0:T(8,128)(2,1)S(1)} %copy-done.1, bf16[4,512,512]{2,1,0:T(8,128)(2,1)S(1)} %add_convert_fusion.momentum_ref, f32[8,128]{1,0:T(8,128)S(1)} %get-tuple-element.25.peaks_ref, bf16[656,128]{1,0:T(8,128)(2,1)S(1)} %get-tuple-element.26.first_ref, ...), custom_call_target="tpu_custom_call" | custom-call | flops 268435456 | bytes 1572864 | tf_op jit(solution)/shard_map/pallas_call | solution.py:292
  53.3 2.4 %collective-permute-start.19 = (bf16[656,128]{1,0:T(8,128)(2,1)S(1)}, bf16[656,128]{1,0:T(8,128)(2,1)S(1)}, u32[]{:S(2)}, u32[]{:S(2)}) collective-permute-start(bf16[656,128]{1,0:T(8,128)(2,1)S(1)} %collective-permute-done.14.first_ref), channel_id=1, source_target_pairs={{0,16},{16,0},{32,48},{48,32},{64,80},{80,64},{96,112},{112,96},{1... | collective-permute-start | bytes 503816 | tf_op jit(solution)/shard_map/ppermute | solution.py:343
  55.7 1.3 %shard_map.73.refs_0_ = bf16[4,512,512]{2,1,0:T(8,128)(2,1)} custom-call(bf16[4,512,512]{2,1,0:T(8,128)(2,1)S(1)} %copy-done.1, bf16[4,512,512]{2,1,0:T(8,128)(2,1)S(1)} %add_convert_fusion.momentum_ref, f32[8,128]{1,0:T(8,128)S(1)} %get-tuple-element.25.peaks_ref, ...), custom_call_target="tpu_custom_call", output_to_operand_aliasing={{}: (5, {})} | custom-call | flops 268435456 | bytes 1572864 | tf_op jit(solution)/shard_map/pallas_call | solution.py:292
  57.8 1.7 %collective-permute-start.17 = (bf16[656,128]{1,0:T(8,128)(2,1)S(1)}, bf16[656,128]{1,0:T(8,128)(2,1)S(1)}, u32[]{:S(2)}, u32[]{:S(2)}) collective-permute-start(bf16[656,128]{1,0:T(8,128)(2,1)S(1)} %collective-permute-done.15.first_ref), channel_id=1, source_target_pairs={{0,16},{16,0},{32,48},{48,32},{64,80},{80,64},{96,112},{112,96},{1... | collective-permute-start | bytes 503816 | tf_op jit(solution)/shard_map/ppermute | solution.py:343
  59.5 1.3 %shard_map.74.refs_0_ = bf16[4,512,512]{2,1,0:T(8,128)(2,1)} custom-call(bf16[4,512,512]{2,1,0:T(8,128)(2,1)S(1)} %copy-done.1, bf16[4,512,512]{2,1,0:T(8,128)(2,1)S(1)} %add_convert_fusion.momentum_ref, f32[8,128]{1,0:T(8,128)S(1)} %get-tuple-element.25.peaks_ref, ...), custom_call_target="tpu_custom_call", output_to_operand_aliasing={{}: (5, {})} | custom-call | flops 268435456 | bytes 1572864 | tf_op jit(solution)/shard_map/pallas_call | solution.py:292
  60.8 1.4 %shard_map.75 = bf16[4,512,512]{2,1,0:T(8,128)(2,1)} custom-call(bf16[4,512,512]{2,1,0:T(8,128)(2,1)S(1)} %copy-done.1, bf16[4,512,512]{2,1,0:T(8,128)(2,1)S(1)} %add_convert_fusion.momentum_ref, f32[8,128]{1,0:T(8,128)S(1)} %get-tuple-element.25.peaks_ref, bf16[656,128]{1,0:T(8,128)(2,1)S(1)} %collective-permute-done.15.first_ref, ...), custom_call_target="tpu_custom_call", output_to_operand_aliasing={{}: (5, {})} | custom-call | flops 268435456 | bytes 1572864 | tf_op jit(solution)/shard_map/pallas_call | solution.py:292
  (46 shorter events, 5.0 us)
Async XLA Ops:
  0.6 5.7 %copy-start.5 = (f32[1,1,61,32]{2,3,1,0:T(8,128)S(1)}, f32[1,1,61,32]{2,3,1,0:T(8,128)}, u32[]{:S(2)}) copy-start(f32[1,1,61,32]{2,3,1,0:T(8,128)} %param.8) | copy-start | bytes 23428
  2.9 4.5 %collective-permute-start = (f32[144,128]{1,0:T(8,128)}, f32[144,128]{1,0:T(8,128)S(1)}, u32[]{:S(2)}, u32[]{:S(2)}) collective-permute-start(f32[144,128]{1,0:T(8,128)} %get-tuple-element.18), channel_id=1, source_target_pairs={{0,16},{16,0},{32,48},{48,32},{64,80},{80,64},{96,112},{112,96},{1... | collective-permute-start | bytes 221192 | tf_op jit(solution)/shard_map/ppermute | solution.py:343
  7.5 8.3 %collective-permute-start.3 = (f32[144,128]{1,0:T(8,128)S(1)}, f32[144,128]{1,0:T(8,128)S(1)}, u32[]{:S(2)}, u32[]{:S(2)}) collective-permute-start(f32[144,128]{1,0:T(8,128)S(1)} %add.15), channel_id=1, source_target_pairs={{0,96},{16,240},{32,64},{48,208},{64,32},{80,176},{96,0},{112,144}... | collective-permute-start | bytes 221192 | tf_op jit(solution)/shard_map/ppermute | solution.py:354
  11.4 7.4 %collective-permute-start.2 = (f32[144,128]{1,0:T(8,128)S(1)}, f32[144,128]{1,0:T(8,128)S(1)}, u32[]{:S(2)}, u32[]{:S(2)}) collective-permute-start(f32[144,128]{1,0:T(8,128)S(1)} %add.15), channel_id=1, source_target_pairs={{0,64},{16,208},{32,96},{48,240},{64,0},{80,144},{96,32},{112,176}... | collective-permute-start | bytes 221192 | tf_op jit(solution)/shard_map/ppermute | solution.py:354
  11.9 6.9 %collective-permute-start.1 = (f32[144,128]{1,0:T(8,128)S(1)}, f32[144,128]{1,0:T(8,128)S(1)}, u32[]{:S(2)}, u32[]{:S(2)}) collective-permute-start(f32[144,128]{1,0:T(8,128)S(1)} %add.15), channel_id=1, source_target_pairs={{0,32},{16,48},{32,0},{48,16},{64,96},{80,112},{96,64},{112,80},{1... | collective-permute-start | bytes 221192 | tf_op jit(solution)/shard_map/ppermute | solution.py:354
  13.0 2.8 %collective-permute-start.4 = (f32[8,128]{1,0:T(8,128)S(1)}, f32[8,128]{1,0:T(8,128)S(1)}, u32[]{:S(2)}, u32[]{:S(2)}) collective-permute-start(f32[8,128]{1,0:T(8,128)S(1)} %broadcast_in_dim.37), channel_id=1, source_target_pairs={{0,1},{1,0},{2,3},{3,2},{4,5},{5,4},{6,7},{7,6},{8,9},{9,8},{10,11... | collective-permute-start | bytes 12296 | tf_op jit(solution)/shard_map/ppermute | solution.py:343
  18.8 5.4 %collective-permute-start.5 = (f32[144,128]{1,0:T(8,128)S(1)}, f32[144,128]{1,0:T(8,128)S(1)}, u32[]{:S(2)}, u32[]{:S(2)}) collective-permute-start(f32[144,128]{1,0:T(8,128)S(1)} %add_add_fusion.total_ref), channel_id=1, source_target_pairs={{0,224},{16,112},{32,192},{48,80},{64,160},{80,48},{96,128},{112,1... | collective-permute-start | bytes 221192 | tf_op jit(solution)/shard_map/ppermute | solution.py:354
  20.5 3.7 %collective-permute-start.6 = (f32[8,128]{1,0:T(8,128)S(1)}, f32[8,128]{1,0:T(8,128)S(1)}, u32[]{:S(2)}, u32[]{:S(2)}) collective-permute-start(f32[8,128]{1,0:T(8,128)S(1)} %max.3.peaks_ref), channel_id=1, source_target_pairs={{0,3},{1,2},{2,1},{3,0},{4,7},{5,6},{6,5},{7,4},{8,11},{9,10},{10,... | collective-permute-start | bytes 12296 | tf_op jit(solution)/shard_map/ppermute | solution.py:343
  24.2 25.8 %copy-start.3 = (bf16[4,512,512]{2,1,0:T(8,128)(2,1)S(1)}, bf16[4,512,512]{2,1,0:T(8,128)(2,1)}, u32[]{:S(2)}) copy-start(bf16[4,512,512]{2,1,0:T(8,128)(2,1)} %gradient_ref.1) | copy-start | bytes 6291460
  24.2 25.8 %copy-start.4 = (bf16[4,512,512]{2,1,0:T(8,128)(2,1)S(1)}, bf16[4,512,512]{2,1,0:T(8,128)(2,1)}, u32[]{:S(2)}) copy-start(bf16[4,512,512]{2,1,0:T(8,128)(2,1)} %momentum_ref.1) | copy-start | bytes 6291460
  24.2 5.5 %collective-permute-start.12 = (f32[152,128]{1,0:T(8,128)S(1)}, f32[152,128]{1,0:T(8,128)S(1)}, u32[]{:S(2)}, u32[]{:S(2)}) collective-permute-start(f32[152,128]{1,0:T(8,128)S(1)} %shard_map.70.refs_0_), channel_id=1, source_target_pairs={{0,12},{4,8},{8,4},{12,0},{1,13},{5,9},{9,5},{13,1},{2,14},{6,10},... | collective-permute-start | bytes 233480 | tf_op jit(solution)/shard_map/ppermute | solution.py:343
  27.1 4.8 %collective-permute-start.10 = (f32[152,128]{1,0:T(8,128)S(1)}, f32[152,128]{1,0:T(8,128)S(1)}, u32[]{:S(2)}, u32[]{:S(2)}) collective-permute-start(f32[152,128]{1,0:T(8,128)S(1)} %shard_map.70.refs_0_), channel_id=1, source_target_pairs={{0,8},{4,12},{8,0},{12,4},{1,9},{5,13},{9,1},{13,5},{2,10},{6,14},... | collective-permute-start | bytes 233480 | tf_op jit(solution)/shard_map/ppermute | solution.py:343
  27.4 7.1 %collective-permute-start.8 = (f32[152,128]{1,0:T(8,128)S(1)}, f32[152,128]{1,0:T(8,128)S(1)}, u32[]{:S(2)}, u32[]{:S(2)}) collective-permute-start(f32[152,128]{1,0:T(8,128)S(1)} %shard_map.70.refs_0_), channel_id=1, source_target_pairs={{0,4},{4,0},{8,12},{12,8},{1,5},{5,1},{9,13},{13,9},{2,6},{6,2},{1... | collective-permute-start | bytes 233480 | tf_op jit(solution)/shard_map/ppermute | solution.py:343
  27.7 6.8 %collective-permute-start.7 = (f32[152,128]{1,0:T(8,128)S(1)}, f32[152,128]{1,0:T(8,128)S(1)}, u32[]{:S(2)}, u32[]{:S(2)}) collective-permute-start(f32[152,128]{1,0:T(8,128)S(1)} %shard_map.70.refs_0_), channel_id=1, source_target_pairs={{0,16},{16,0},{32,48},{48,32},{64,80},{80,64},{96,112},{112,96},{1... | collective-permute-start | bytes 233480 | tf_op jit(solution)/shard_map/ppermute | solution.py:343
  29.7 4.8 %collective-permute-start.13 = (f32[152,128]{1,0:T(8,128)S(1)}, f32[152,128]{1,0:T(8,128)S(1)}, u32[]{:S(2)}, u32[]{:S(2)}) collective-permute-start(f32[152,128]{1,0:T(8,128)S(1)} %collective-permute-done.12.refs_6_), channel_id=1, source_target_pairs={{0,16},{16,0},{32,48},{48,32},{64,80},{80,64},{96,112},{112,96},{1... | collective-permute-start | bytes 233480 | tf_op jit(solution)/shard_map/ppermute | solution.py:343
  31.8 3.7 %collective-permute-start.11 = (f32[152,128]{1,0:T(8,128)S(1)}, f32[152,128]{1,0:T(8,128)S(1)}, u32[]{:S(2)}, u32[]{:S(2)}) collective-permute-start(f32[152,128]{1,0:T(8,128)S(1)} %collective-permute-done.10.refs_4_), channel_id=1, source_target_pairs={{0,16},{16,0},{32,48},{48,32},{64,80},{80,64},{96,112},{112,96},{1... | collective-permute-start | bytes 233480 | tf_op jit(solution)/shard_map/ppermute | solution.py:343
  34.6 1.3 %collective-permute-start.9 = (f32[152,128]{1,0:T(8,128)S(1)}, f32[152,128]{1,0:T(8,128)S(1)}, u32[]{:S(2)}, u32[]{:S(2)}) collective-permute-start(f32[152,128]{1,0:T(8,128)S(1)} %collective-permute-done.8.refs_2_), channel_id=1, source_target_pairs={{0,16},{16,0},{32,48},{48,32},{64,80},{80,64},{96,112},{112,96},{1... | collective-permute-start | bytes 233480 | tf_op jit(solution)/shard_map/ppermute | solution.py:343
  47.3 5.7 %collective-permute-start.14 = (bf16[656,128]{1,0:T(8,128)(2,1)S(1)}, bf16[656,128]{1,0:T(8,128)(2,1)S(1)}, u32[]{:S(2)}, u32[]{:S(2)}) collective-permute-start(bf16[656,128]{1,0:T(8,128)(2,1)S(1)} %get-tuple-element.26.first_ref), channel_id=1, source_target_pairs={{0,1},{1,0},{2,3},{3,2},{16,19},{17,18},{18,17},{19,16},{32,33},{3... | collective-permute-start | bytes 503816 | tf_op jit(solution)/shard_map/ppermute | solution.py:364
  49.9 5.8 %collective-permute-start.16 = (bf16[656,128]{1,0:T(8,128)(2,1)S(1)}, bf16[656,128]{1,0:T(8,128)(2,1)S(1)}, u32[]{:S(2)}, u32[]{:S(2)}) collective-permute-start(bf16[656,128]{1,0:T(8,128)(2,1)S(1)} %get-tuple-element.27.second_ref), channel_id=1, source_target_pairs={{0,1},{1,0},{2,3},{3,2},{16,19},{17,18},{18,17},{19,16},{32,33},{3... | collective-permute-start | bytes 503816 | tf_op jit(solution)/shard_map/ppermute | solution.py:364
  51.5 9.4 %copy-start = (bf16[4,512,512]{2,1,0:T(8,128)(2,1)}, bf16[4,512,512]{2,1,0:T(8,128)(2,1)S(1)}, u32[]{:S(2)}) copy-start(bf16[4,512,512]{2,1,0:T(8,128)(2,1)S(1)} %add_convert_fusion.momentum_ref) | copy-start | bytes 6291460
  53.0 4.8 %collective-permute-start.15 = (bf16[656,128]{1,0:T(8,128)(2,1)S(1)}, bf16[656,128]{1,0:T(8,128)(2,1)S(1)}, u32[]{:S(2)}, u32[]{:S(2)}) collective-permute-start(bf16[656,128]{1,0:T(8,128)(2,1)S(1)} %collective-permute-done.14.first_ref), channel_id=1, source_target_pairs={{0,3},{1,2},{2,1},{3,0},{16,17},{17,16},{18,19},{19,18},{32,35},{3... | collective-permute-start | bytes 503816 | tf_op jit(solution)/shard_map/ppermute | solution.py:364
  53.3 6.2 %collective-permute-start.19 = (bf16[656,128]{1,0:T(8,128)(2,1)S(1)}, bf16[656,128]{1,0:T(8,128)(2,1)S(1)}, u32[]{:S(2)}, u32[]{:S(2)}) collective-permute-start(bf16[656,128]{1,0:T(8,128)(2,1)S(1)} %collective-permute-done.14.first_ref), channel_id=1, source_target_pairs={{0,16},{16,0},{32,48},{48,32},{64,80},{80,64},{96,112},{112,96},{1... | collective-permute-start | bytes 503816 | tf_op jit(solution)/shard_map/ppermute | solution.py:343
  55.7 3.8 %collective-permute-start.18 = (bf16[656,128]{1,0:T(8,128)(2,1)S(1)}, bf16[656,128]{1,0:T(8,128)(2,1)S(1)}, u32[]{:S(2)}, u32[]{:S(2)}) collective-permute-start(bf16[656,128]{1,0:T(8,128)(2,1)S(1)} %collective-permute-done.16.second_ref), channel_id=1, source_target_pairs={{0,16},{16,0},{32,48},{48,32},{64,80},{80,64},{96,112},{112,96},{1... | collective-permute-start | bytes 503816 | tf_op jit(solution)/shard_map/ppermute | solution.py:343
  57.8 3.0 %collective-permute-start.17 = (bf16[656,128]{1,0:T(8,128)(2,1)S(1)}, bf16[656,128]{1,0:T(8,128)(2,1)S(1)}, u32[]{:S(2)}, u32[]{:S(2)}) collective-permute-start(bf16[656,128]{1,0:T(8,128)(2,1)S(1)} %collective-permute-done.15.first_ref), channel_id=1, source_target_pairs={{0,16},{16,0},{32,48},{48,32},{64,80},{80,64},{96,112},{112,96},{1... | collective-permute-start | bytes 503816 | tf_op jit(solution)/shard_map/ppermute | solution.py:343
  (3 other events, 8.1 us)

commit v5 on v4

--- a/solution.py
+++ b/solution.py
@@ -93,7 +93,7 @@
             pltpu.VMEM((2 * PART, BLOCK), jnp.float32),
             pltpu.SemaphoreType.DMA((2, 3)),
         ],
-        compiler_params=pltpu.CompilerParams(vmem_limit_bytes=62 * 2**20),
+        compiler_params=pltpu.CompilerParams(vmem_limit_bytes=53 * 2**20),
         cost_estimate=pl.CostEstimate(flops=4 * PART * BLOCK * cols, bytes_accessed=3 * rank * cols, transcendentals=0),
     )(momentum, gradient)
 
@@ -246,17 +246,28 @@
     )(*parts)
 
 
-def last_kernel(update_scale, masks, weights_ref, momentum_ref, peaks_ref, first_ref, second_ref, *refs):
-    out_ref, packed, factors, fresh, left = refs[-5:]
+def matrix_at(masks):
+    core = lax.rem(lax.axis_index("fsdp"), 2)
+    return lax.axis_index("ctx") ^ (masks[0] + (masks[1] - masks[0]) * core)
+
+
+def last_kernel(update_scale, masks, waiting_masks, keeps, weights_ref, momentum_ref, peaks_ref, first_ref, second_ref, *refs):
+    stores = []
+    if keeps:
+        fresh, factors = refs[-2:]
+    else:
+        out_ref, factors, fresh, left = refs[-4:]
+    if waiting_masks is not None:
+        stores.append(pltpu.make_async_copy(refs[0], out_ref.at[matrix_at(waiting_masks)], left.at[2]))
+        stores[0].start()
     rank, cols = fresh.shape
     shard = lax.axis_index("fsdp")
     core = lax.rem(shard, 2)
-    matrix = lax.axis_index("ctx") ^ (masks[0] + (masks[1] - masks[0]) * core)
-    packed[core] = first_ref[...]
-    packed[1 - core] = second_ref[...]
+    matrix = matrix_at(masks)
     for side, kept in enumerate(KEPT):
         for at, (row, column) in enumerate(kept):
-            block = packed[side, at * BLOCK : (at + 1) * BLOCK, :]
+            rows = slice(at * BLOCK, (at + 1) * BLOCK)
+            block = jnp.where(core == side, first_ref[rows, :], second_ref[rows, :])
             factors[row * BLOCK : (row + 1) * BLOCK, column * BLOCK : (column + 1) * BLOCK] = block
             if row != column:
                 factors[column * BLOCK : (column + 1) * BLOCK, row * BLOCK : (row + 1) * BLOCK] = block.T
@@ -273,53 +284,36 @@
         column_peaks = jnp.where((column >= first) & (column < first + KNOPE), peak, column_peaks)
     scale = jnp.sqrt(jnp.minimum(1.0, clip_limit / column_peaks))
     start = (momentum_ref[matrix].astype(jnp.float32) * inverse).astype(jnp.bfloat16)
-    stores = []
     for at in range(rank // STRIP):
         rows = slice(at * STRIP, (at + 1) * STRIP)
         orthogonal = jnp.dot(factors[rows, :], start, preferred_element_type=jnp.float32)
         value = weights_ref[matrix, rows, :].astype(jnp.float32) - step_size * (update_scale * orthogonal)
         fresh[rows, :] = (value * scale).astype(jnp.bfloat16)
-        stores.append(pltpu.make_async_copy(fresh.at[rows], out_ref.at[matrix, rows], left.at[at]))
-        stores[-1].start()
+        if not keeps:
+            stores.append(pltpu.make_async_copy(fresh.at[rows], out_ref.at[matrix, rows], left.at[at]))
+            stores[-1].start()
     for store in stores:
         store.wait()
 
 
-def last_product(update_scale, masks, weights, momentum, peaks, pair, before):
+def last_product(update_scale, masks, weights, momentum, peaks, pair, before=None, waiting=None, keeps=False):
     rank, cols = weights.shape[1:]
     whole, outside = pl.BlockSpec(memory_space=pltpu.VMEM), pl.BlockSpec(memory_space=pl.ANY)
+    waiting_masks, waiting_block = waiting or (None, None)
+    extra = [] if waiting is None else [waiting_block]
     earlier = [] if before is None else [before]
+    block = jax.ShapeDtypeStruct((rank, cols), weights.dtype)
+    staging = [pltpu.VMEM((rank, cols), jnp.bfloat16), pltpu.SemaphoreType.DMA((3,))]
     return pl.pallas_call(
-        functools.partial(last_kernel, update_scale, masks),
-        out_shape=jax.ShapeDtypeStruct(weights.shape, jnp.bfloat16),
-        in_specs=[whole] * 5 + [outside] * len(earlier),
-        out_specs=outside,
-        scratch_shapes=[
-            pltpu.VMEM((2, HALF + END, BLOCK), jnp.bfloat16),
-            pltpu.VMEM((rank, rank), jnp.bfloat16),
-            pltpu.VMEM((rank, cols), jnp.bfloat16),
-            pltpu.SemaphoreType.DMA((rank // STRIP,)),
-        ],
-        input_output_aliases={5: 0} if earlier else {},
+        functools.partial(last_kernel, update_scale, masks, waiting_masks, keeps),
+        out_shape=block if keeps else jax.ShapeDtypeStruct(weights.shape, weights.dtype),
+        in_specs=[whole] * (5 + len(extra)) + [outside] * len(earlier),
+        out_specs=whole if keeps else outside,
+        scratch_shapes=[pltpu.VMEM((rank, rank), jnp.bfloat16)] + ([] if keeps else staging),
+        input_output_aliases={5 + len(extra): 0} if earlier else {},
         compiler_params=pltpu.CompilerParams(vmem_limit_bytes=24 * 2**20),
         cost_estimate=pl.CostEstimate(flops=2 * rank * rank * cols, bytes_accessed=6 * rank * cols, transcendentals=0),
-    )(weights, momentum, peaks, *pair, *earlier)
-
-
-def fetch_kernel(source_ref, out_ref):
-    out_ref[...] = source_ref[...]
-
-
-def fetch(value):
-    whole = pl.BlockSpec(memory_space=pltpu.VMEM)
-    return pl.pallas_call(
-        fetch_kernel,
-        out_shape=jax.ShapeDtypeStruct(value.shape, value.dtype),
-        in_specs=[whole],
-        out_specs=whole,
-        compiler_params=pltpu.CompilerParams(vmem_limit_bytes=8 * 2**20),
-        cost_estimate=pl.CostEstimate(flops=0, bytes_accessed=8 * value.size, transcendentals=0),
-    )(value)
+    )(weights, momentum, peaks, *pair, *extra, *earlier)
 
 
 def join_kernel(total_ref, arrived_ref, peaks_ref, peaks_arrived_ref, out_ref):
@@ -378,7 +372,7 @@
     peaks = jnp.broadcast_to(peaks.reshape(1, BLOCK), (TAIL, BLOCK))
 
     keep, send = partial_gram(momentum, gradient)
-    total = fetch(keep) + swapped(send)
+    total = keep + swapped(send)
     total, peaks = lax.optimization_barrier((total, peaks))
     third, second, first = along_z(total, 3), along_z(total, 2), along_z(total, 1)
     total = (total + first) + (second + third)
@@ -392,15 +386,16 @@
     peaks, late_momentum = lax.optimization_barrier((peaks, momentum))
     new_momentum = decayed(late_momentum, gradient)
     near = tuple(by_core(piece, "ctx", (1, 3)) for piece in (first, second))
-    new_weights = last((0, 0), weights, new_momentum, peaks, (first, second), None)
+    new_weights = last((0, 0), weights, new_momentum, peaks, (first, second))
     near_first, new_weights = lax.optimization_barrier((near[0], new_weights))
     far = by_core(near_first, "ctx", (3, 1))
     cross = swapped(near[1]), swapped(near_first)
     new_weights = last((1, 3), weights, new_momentum, peaks, (near_first, near[1]), new_weights)
     far, new_weights = lax.optimization_barrier((far, new_weights))
     far = far, swapped(far)
-    new_weights = last((3, 1), weights, new_momentum, peaks, cross, new_weights)
-    new_weights = last((2, 2), weights, new_momentum, peaks, far, new_weights)
+    waiting = last((3, 1), weights, new_momentum, peaks, cross, keeps=True)
+    far, waiting = lax.optimization_barrier((far, waiting))
+    new_weights = last((2, 2), weights, new_momentum, peaks, far, new_weights, ((3, 1), waiting))
     return (new_weights, new_momentum)
 
 

time: 62.6 us -> 61.4 us (0.981)
  Pallas kernels: 19.3 us -> 18 us
  waiting for transfers between devices: 8.2 us -> 9.1 us
  local copies, waits for them, and re-layouts: 1.72 us -> 0.83 us
    ppermute x13, waiting for transfers between devices: 4.38 us -> 5.34 us  [crossed(): lax.ppermute(value, axis, [(at, at ^ mask) for at in range(lax.axis_size(...]
    unnamed x14 -> x12, local copies, waits for them, and re-layouts: 1.63 us -> 0.74 us
    pallas_call x1, Pallas kernels: 2.28 us -> 1.62 us  [partial_gram(): pl.pallas_call(partial_gram_kernel, out_shape=(shape, shape), in_specs=[p...]
    pallas_call x5 -> x4, Pallas kernels: 5.53 us -> 4.89 us  [last_product(): pl.pallas_call(functools.partial(last_kernel, update_scale, masks, waitin...]
  transfers between devices with their start and end apart: 20 -> 20, of which waited for: 7 -> 9; matrix products, arithmetic and copies ran while one was open for 1% -> 2% of each run, Pallas kernels for 7% -> 6%
where the time goes in v5:
time: 61.4 us; the launch traced here: 61.2 us
  starting transfers between devices  31.5 us (51%)
  Pallas kernels  18 us (29%)
  waiting for transfers between devices  9.1 us (15%)
  between operations  0.95 us (2%)
  other arithmetic  0.87 us (1%)
  local copies, waits for them, and re-layouts  0.83 us (1%)
    ppermute x13, starting transfers between devices, crossed(): lax.ppermute(value, axis, [(at, at ^ mask) for at in range(lax.axis_size(...  21.2 us
    pallas_call x1, Pallas kernels, newton(): pl.pallas_call(newton_kernel, out_shape=(piece, piece, jax.ShapeDtypeStru...  11.5 us
    ppermute x4, starting transfers between devices, along_z(): return lax.ppermute(value, 'fsdp', pairs)  7.27 us
    ppermute x13, waiting for transfers between devices, crossed(): lax.ppermute(value, axis, [(at, at ^ mask) for at in range(lax.axis_size(...  5.34 us
    pallas_call x4, Pallas kernels, last_product(): pl.pallas_call(functools.partial(last_kernel, update_scale, masks, waitin...  4.89 us
    ppermute x3, starting transfers between devices, by_core(): return lax.ppermute(value, ('fsdp', axis), pairs)  3.06 us
    ppermute x4, waiting for transfers between devices, along_z(): return lax.ppermute(value, 'fsdp', pairs)  2.98 us
    pallas_call x1, Pallas kernels, partial_gram(): pl.pallas_call(partial_gram_kernel, out_shape=(shape, shape), in_specs=[p...  1.62 us
  transfers between devices with their start and end apart: 20, of which 9 were waited for; matrix products, arithmetic and copies ran while one was open for 2% of the time, Pallas kernels for 6%

profile of v5, /device:TPU:1, one launch (start us, length us, event | category | flops | bytes accessed | tf_op | source)
XLA Modules:
  0.0 61.2 jit_solution(2320393783951916935)
XLA Ops:
  0.6 1.6 %shard_map.68 = (f32[144,128]{1,0:T(8,128)S(1)}, f32[144,128]{1,0:T(8,128)S(1)}) custom-call(bf16[4,512,512]{2,1,0:T(8,128)(2,1)} %momentum_ref.1, bf16[4,512,512]{2,1,0:T(8,128)(2,1)} %gradient_ref.1), custom_call_target="tpu_custom_call" | custom-call | flops 37748736 | bytes 786432 | tf_op jit(solution)/shard_map/pallas_call | solution.py:84
  2.3 3.3 %collective-permute-start = (f32[144,128]{1,0:T(8,128)S(1)}, f32[144,128]{1,0:T(8,128)S(1)}, u32[]{:S(2)}, u32[]{:S(2)}) collective-permute-start(f32[144,128]{1,0:T(8,128)S(1)} %get-tuple-element.21), channel_id=1, source_target_pairs={{0,16},{16,0},{32,48},{48,32},{64,80},{80,64},{96,112},{112,96},{1... | collective-permute-start | bytes 221192 | tf_op jit(solution)/shard_map/ppermute | solution.py:337
  6.5 3.9 %collective-permute-start.3 = (f32[144,128]{1,0:T(8,128)S(1)}, f32[144,128]{1,0:T(8,128)S(1)}, u32[]{:S(2)}, u32[]{:S(2)}) collective-permute-start(f32[144,128]{1,0:T(8,128)S(1)} %add.15), channel_id=1, source_target_pairs={{0,96},{16,240},{32,64},{48,208},{64,32},{80,176},{96,0},{112,144}... | collective-permute-start | bytes 221192 | tf_op jit(solution)/shard_map/ppermute | solution.py:348
  11.0 1.1 %collective-permute-start.1 = (f32[144,128]{1,0:T(8,128)S(1)}, f32[144,128]{1,0:T(8,128)S(1)}, u32[]{:S(2)}, u32[]{:S(2)}) collective-permute-start(f32[144,128]{1,0:T(8,128)S(1)} %add.15), channel_id=1, source_target_pairs={{0,32},{16,48},{32,0},{48,16},{64,96},{80,112},{96,64},{112,80},{1... | collective-permute-start | bytes 221192 | tf_op jit(solution)/shard_map/ppermute | solution.py:348
  12.1 1.2 %collective-permute-start.4 = (f32[8,128]{1,0:T(8,128)S(1)}, f32[8,128]{1,0:T(8,128)S(1)}, u32[]{:S(2)}, u32[]{:S(2)}) collective-permute-start(f32[8,128]{1,0:T(8,128)S(1)} %broadcast_in_dim.37), channel_id=1, source_target_pairs={{0,1},{1,0},{2,3},{3,2},{4,5},{5,4},{6,7},{7,6},{8,9},{9,8},{10,11... | collective-permute-start | bytes 12296 | tf_op jit(solution)/shard_map/ppermute | solution.py:337
  13.3 1.5 %collective-permute-done.4 = f32[8,128]{1,0:T(8,128)S(1)} collective-permute-done((f32[8,128]{1,0:T(8,128)S(1)}, f32[8,128]{1,0:T(8,128)S(1)}, u32[]{:S(2)}, u32[]{:S(2)}) %collective-permute-start.4) | collective-permute-done | bytes 4128 | tf_op jit(solution)/shard_map/ppermute | solution.py:337
  14.9 3.0 %collective-permute-done.2 = f32[144,128]{1,0:T(8,128)S(1)} collective-permute-done((f32[144,128]{1,0:T(8,128)S(1)}, f32[144,128]{1,0:T(8,128)S(1)}, u32[]{:S(2)}, u32[]{:S(2)}) %collective-permute-start.2) | collective-permute-done | bytes 73760 | tf_op jit(solution)/shard_map/ppermute | solution.py:348
  17.9 1.7 %collective-permute-start.5 = (f32[144,128]{1,0:T(8,128)S(1)}, f32[144,128]{1,0:T(8,128)S(1)}, u32[]{:S(2)}, u32[]{:S(2)}) collective-permute-start(f32[144,128]{1,0:T(8,128)S(1)} %add_add_fusion.total_ref), channel_id=1, source_target_pairs={{0,224},{16,112},{32,192},{48,80},{64,160},{80,48},{96,128},{112,1... | collective-permute-start | bytes 221192 | tf_op jit(solution)/shard_map/ppermute | solution.py:348
  19.6 2.5 %collective-permute-start.6 = (f32[8,128]{1,0:T(8,128)S(1)}, f32[8,128]{1,0:T(8,128)S(1)}, u32[]{:S(2)}, u32[]{:S(2)}) collective-permute-start(f32[8,128]{1,0:T(8,128)S(1)} %max.3.peaks_ref), channel_id=1, source_target_pairs={{0,3},{1,2},{2,1},{3,0},{4,7},{5,6},{6,5},{7,4},{8,11},{9,10},{10,... | collective-permute-start | bytes 12296 | tf_op jit(solution)/shard_map/ppermute | solution.py:337
  22.0 1.2 %collective-permute-done.6.peaks_arrived_ref = f32[8,128]{1,0:T(8,128)S(1)} collective-permute-done((f32[8,128]{1,0:T(8,128)S(1)}, f32[8,128]{1,0:T(8,128)S(1)}, u32[]{:S(2)}, u32[]{:S(2)}) %collective-permute-start.6) | collective-permute-done | bytes 4128 | tf_op jit(solution)/shard_map/ppermute | solution.py:337
  23.3 2.8 %collective-permute-start.12 = (f32[152,128]{1,0:T(8,128)S(1)}, f32[152,128]{1,0:T(8,128)S(1)}, u32[]{:S(2)}, u32[]{:S(2)}) collective-permute-start(f32[152,128]{1,0:T(8,128)S(1)} %shard_map.69.refs_0_), channel_id=1, source_target_pairs={{0,12},{4,8},{8,4},{12,0},{1,13},{5,9},{9,5},{13,1},{2,14},{6,10},... | collective-permute-start | bytes 233480 | tf_op jit(solution)/shard_map/ppermute | solution.py:337
  26.8 2.1 %collective-permute-start.7 = (f32[152,128]{1,0:T(8,128)S(1)}, f32[152,128]{1,0:T(8,128)S(1)}, u32[]{:S(2)}, u32[]{:S(2)}) collective-permute-start(f32[152,128]{1,0:T(8,128)S(1)} %shard_map.69.refs_0_), channel_id=1, source_target_pairs={{0,16},{16,0},{32,48},{48,32},{64,80},{80,64},{96,112},{112,96},{1... | collective-permute-start | bytes 233480 | tf_op jit(solution)/shard_map/ppermute | solution.py:337
  28.9 1.7 %collective-permute-start.13 = (f32[152,128]{1,0:T(8,128)S(1)}, f32[152,128]{1,0:T(8,128)S(1)}, u32[]{:S(2)}, u32[]{:S(2)}) collective-permute-start(f32[152,128]{1,0:T(8,128)S(1)} %collective-permute-done.12.refs_6_), channel_id=1, source_target_pairs={{0,16},{16,0},{32,48},{48,32},{64,80},{80,64},{96,112},{112,96},{1... | collective-permute-start | bytes 233480 | tf_op jit(solution)/shard_map/ppermute | solution.py:337
  30.9 2.8 %collective-permute-start.11 = (f32[152,128]{1,0:T(8,128)S(1)}, f32[152,128]{1,0:T(8,128)S(1)}, u32[]{:S(2)}, u32[]{:S(2)}) collective-permute-start(f32[152,128]{1,0:T(8,128)S(1)} %collective-permute-done.10.refs_4_), channel_id=1, source_target_pairs={{0,16},{16,0},{32,48},{48,32},{64,80},{80,64},{96,112},{112,96},{1... | collective-permute-start | bytes 233480 | tf_op jit(solution)/shard_map/ppermute | solution.py:337
  33.7 0.9 %collective-permute-done.11.refs_5_ = f32[152,128]{1,0:T(8,128)S(1)} collective-permute-done((f32[152,128]{1,0:T(8,128)S(1)}, f32[152,128]{1,0:T(8,128)S(1)}, u32[]{:S(2)}, u32[]{:S(2)}) %collective-permute-start.11) | collective-permute-done | bytes 77856 | tf_op jit(solution)/shard_map/ppermute | solution.py:337
  35.0 11.5 %shard_map.70 = (bf16[656,128]{1,0:T(8,128)(2,1)S(1)}, bf16[656,128]{1,0:T(8,128)(2,1)S(1)}, f32[8,128]{1,0:T(8,128)S(1)}) custom-call(f32[152,128]{1,0:T(8,128)S(1)} %shard_map.69.refs_0_, f32[152,128]{1,0:T(8,128)S(1)} %collective-permute-done.7.refs_1_, f32[152,128]{1,0:T(8,128)S(1)} %collective-permute-done.8.refs_2_, ...), custom_call_target="tpu_custom_call" | custom-call | flops 13690208256 | bytes 1572864 | tf_op jit(solution)/shard_map/pallas_call | solution.py:229
  46.4 2.6 %collective-permute-start.14 = (bf16[656,128]{1,0:T(8,128)(2,1)S(1)}, bf16[656,128]{1,0:T(8,128)(2,1)S(1)}, u32[]{:S(2)}, u32[]{:S(2)}) collective-permute-start(bf16[656,128]{1,0:T(8,128)(2,1)S(1)} %get-tuple-element.29.first_ref), channel_id=1, source_target_pairs={{0,1},{1,0},{2,3},{3,2},{16,19},{17,18},{18,17},{19,16},{32,33},{3... | collective-permute-start | bytes 503816 | tf_op jit(solution)/shard_map/ppermute | solution.py:358
  49.9 0.7 %copy-done.1 = bf16[4,512,512]{2,1,0:T(8,128)(2,1)S(1)} copy-done((bf16[4,512,512]{2,1,0:T(8,128)(2,1)S(1)}, bf16[4,512,512]{2,1,0:T(8,128)(2,1)}, u32[]{:S(2)}) %copy-start.1) | copy-done | bytes 2097176
  50.6 1.5 %shard_map.71.refs_0_ = bf16[4,512,512]{2,1,0:T(8,128)(2,1)} custom-call(bf16[4,512,512]{2,1,0:T(8,128)(2,1)S(1)} %copy-done.1, bf16[4,512,512]{2,1,0:T(8,128)(2,1)S(1)} %add_convert_fusion.momentum_ref, f32[8,128]{1,0:T(8,128)S(1)} %get-tuple-element.28.peaks_ref, bf16[656,128]{1,0:T(8,128)(2,1)S(1)} %get-tuple-element.29.first_ref, ...), custom_call_target="tpu_custom_call" | custom-call | flops 268435456 | bytes 1572864 | tf_op jit(solution)/shard_map/pallas_call | solution.py:307
  52.4 2.4 %collective-permute-start.19 = (bf16[656,128]{1,0:T(8,128)(2,1)S(1)}, bf16[656,128]{1,0:T(8,128)(2,1)S(1)}, u32[]{:S(2)}, u32[]{:S(2)}) collective-permute-start(bf16[656,128]{1,0:T(8,128)(2,1)S(1)} %collective-permute-done.14.first_ref), channel_id=1, source_target_pairs={{0,16},{16,0},{32,48},{48,32},{64,80},{80,64},{96,112},{112,96},{1... | collective-permute-start | bytes 503816 | tf_op jit(solution)/shard_map/ppermute | solution.py:337
  54.8 1.3 %shard_map.72.refs_1_ = bf16[4,512,512]{2,1,0:T(8,128)(2,1)} custom-call(bf16[4,512,512]{2,1,0:T(8,128)(2,1)S(1)} %copy-done.1, bf16[4,512,512]{2,1,0:T(8,128)(2,1)S(1)} %add_convert_fusion.momentum_ref, f32[8,128]{1,0:T(8,128)S(1)} %get-tuple-element.28.peaks_ref, ...), custom_call_target="tpu_custom_call", output_to_operand_aliasing={{}: (5, {})} | custom-call | flops 268435456 | bytes 1572864 | tf_op jit(solution)/shard_map/pallas_call | solution.py:307
  56.1 0.8 %collective-permute-done.15.first_ref = bf16[656,128]{1,0:T(8,128)(2,1)S(1)} collective-permute-done((bf16[656,128]{1,0:T(8,128)(2,1)S(1)}, bf16[656,128]{1,0:T(8,128)(2,1)S(1)}, u32[]{:S(2)}, u32[]{:S(2)}) %collective-permute-start.15) | collective-permute-done | bytes 167968 | tf_op jit(solution)/shard_map/ppermute | solution.py:358
  56.9 1.7 %collective-permute-start.17 = (bf16[656,128]{1,0:T(8,128)(2,1)S(1)}, bf16[656,128]{1,0:T(8,128)(2,1)S(1)}, u32[]{:S(2)}, u32[]{:S(2)}) collective-permute-start(bf16[656,128]{1,0:T(8,128)(2,1)S(1)} %collective-permute-done.15.first_ref), channel_id=1, source_target_pairs={{0,16},{16,0},{32,48},{48,32},{64,80},{80,64},{96,112},{112,96},{1... | collective-permute-start | bytes 503816 | tf_op jit(solution)/shard_map/ppermute | solution.py:337
  59.6 1.4 %shard_map.74 = bf16[4,512,512]{2,1,0:T(8,128)(2,1)} custom-call(bf16[4,512,512]{2,1,0:T(8,128)(2,1)S(1)} %copy-done.1, bf16[4,512,512]{2,1,0:T(8,128)(2,1)S(1)} %add_convert_fusion.momentum_ref, f32[8,128]{1,0:T(8,128)S(1)} %get-tuple-element.28.peaks_ref, bf16[656,128]{1,0:T(8,128)(2,1)S(1)} %collective-permute-done.15.first_ref, ...), custom_call_target="tpu_custom_call", output_to_operand_aliasing={{}: (6, {})} | custom-call | flops 268435456 | bytes 1572864 | tf_op jit(solution)/shard_map/pallas_call | solution.py:307
  (43 shorter events, 5.1 us)
Async XLA Ops:
  0.6 5.0 %copy-start.4 = (f32[1,1,61,32]{2,3,1,0:T(8,128)S(1)}, f32[1,1,61,32]{2,3,1,0:T(8,128)}, u32[]{:S(2)}) copy-start(f32[1,1,61,32]{2,3,1,0:T(8,128)} %param.8) | copy-start | bytes 23428
  2.3 4.2 %collective-permute-start = (f32[144,128]{1,0:T(8,128)S(1)}, f32[144,128]{1,0:T(8,128)S(1)}, u32[]{:S(2)}, u32[]{:S(2)}) collective-permute-start(f32[144,128]{1,0:T(8,128)S(1)} %get-tuple-element.21), channel_id=1, source_target_pairs={{0,16},{16,0},{32,48},{48,32},{64,80},{80,64},{96,112},{112,96},{1... | collective-permute-start | bytes 221192 | tf_op jit(solution)/shard_map/ppermute | solution.py:337
  6.5 8.3 %collective-permute-start.3 = (f32[144,128]{1,0:T(8,128)S(1)}, f32[144,128]{1,0:T(8,128)S(1)}, u32[]{:S(2)}, u32[]{:S(2)}) collective-permute-start(f32[144,128]{1,0:T(8,128)S(1)} %add.15), channel_id=1, source_target_pairs={{0,96},{16,240},{32,64},{48,208},{64,32},{80,176},{96,0},{112,144}... | collective-permute-start | bytes 221192 | tf_op jit(solution)/shard_map/ppermute | solution.py:348
  10.5 7.4 %collective-permute-start.2 = (f32[144,128]{1,0:T(8,128)S(1)}, f32[144,128]{1,0:T(8,128)S(1)}, u32[]{:S(2)}, u32[]{:S(2)}) collective-permute-start(f32[144,128]{1,0:T(8,128)S(1)} %add.15), channel_id=1, source_target_pairs={{0,64},{16,208},{32,96},{48,240},{64,0},{80,144},{96,32},{112,176}... | collective-permute-start | bytes 221192 | tf_op jit(solution)/shard_map/ppermute | solution.py:348
  11.0 6.8 %collective-permute-start.1 = (f32[144,128]{1,0:T(8,128)S(1)}, f32[144,128]{1,0:T(8,128)S(1)}, u32[]{:S(2)}, u32[]{:S(2)}) collective-permute-start(f32[144,128]{1,0:T(8,128)S(1)} %add.15), channel_id=1, source_target_pairs={{0,32},{16,48},{32,0},{48,16},{64,96},{80,112},{96,64},{112,80},{1... | collective-permute-start | bytes 221192 | tf_op jit(solution)/shard_map/ppermute | solution.py:348
  12.1 2.8 %collective-permute-start.4 = (f32[8,128]{1,0:T(8,128)S(1)}, f32[8,128]{1,0:T(8,128)S(1)}, u32[]{:S(2)}, u32[]{:S(2)}) collective-permute-start(f32[8,128]{1,0:T(8,128)S(1)} %broadcast_in_dim.37), channel_id=1, source_target_pairs={{0,1},{1,0},{2,3},{3,2},{4,5},{5,4},{6,7},{7,6},{8,9},{9,8},{10,11... | collective-permute-start | bytes 12296 | tf_op jit(solution)/shard_map/ppermute | solution.py:337
  17.9 5.4 %collective-permute-start.5 = (f32[144,128]{1,0:T(8,128)S(1)}, f32[144,128]{1,0:T(8,128)S(1)}, u32[]{:S(2)}, u32[]{:S(2)}) collective-permute-start(f32[144,128]{1,0:T(8,128)S(1)} %add_add_fusion.total_ref), channel_id=1, source_target_pairs={{0,224},{16,112},{32,192},{48,80},{64,160},{80,48},{96,128},{112,1... | collective-permute-start | bytes 221192 | tf_op jit(solution)/shard_map/ppermute | solution.py:348
  19.6 3.7 %collective-permute-start.6 = (f32[8,128]{1,0:T(8,128)S(1)}, f32[8,128]{1,0:T(8,128)S(1)}, u32[]{:S(2)}, u32[]{:S(2)}) collective-permute-start(f32[8,128]{1,0:T(8,128)S(1)} %max.3.peaks_ref), channel_id=1, source_target_pairs={{0,3},{1,2},{2,1},{3,0},{4,7},{5,6},{6,5},{7,4},{8,11},{9,10},{10,... | collective-permute-start | bytes 12296 | tf_op jit(solution)/shard_map/ppermute | solution.py:337
  23.3 25.9 %copy-start.2 = (bf16[4,512,512]{2,1,0:T(8,128)(2,1)S(1)}, bf16[4,512,512]{2,1,0:T(8,128)(2,1)}, u32[]{:S(2)}) copy-start(bf16[4,512,512]{2,1,0:T(8,128)(2,1)} %gradient_ref.1) | copy-start | bytes 6291460
  23.3 25.9 %copy-start.3 = (bf16[4,512,512]{2,1,0:T(8,128)(2,1)S(1)}, bf16[4,512,512]{2,1,0:T(8,128)(2,1)}, u32[]{:S(2)}) copy-start(bf16[4,512,512]{2,1,0:T(8,128)(2,1)} %momentum_ref.1) | copy-start | bytes 6291460
  23.3 5.6 %collective-permute-start.12 = (f32[152,128]{1,0:T(8,128)S(1)}, f32[152,128]{1,0:T(8,128)S(1)}, u32[]{:S(2)}, u32[]{:S(2)}) collective-permute-start(f32[152,128]{1,0:T(8,128)S(1)} %shard_map.69.refs_0_), channel_id=1, source_target_pairs={{0,12},{4,8},{8,4},{12,0},{1,13},{5,9},{9,5},{13,1},{2,14},{6,10},... | collective-permute-start | bytes 233480 | tf_op jit(solution)/shard_map/ppermute | solution.py:337
  26.1 4.8 %collective-permute-start.10 = (f32[152,128]{1,0:T(8,128)S(1)}, f32[152,128]{1,0:T(8,128)S(1)}, u32[]{:S(2)}, u32[]{:S(2)}) collective-permute-start(f32[152,128]{1,0:T(8,128)S(1)} %shard_map.69.refs_0_), channel_id=1, source_target_pairs={{0,8},{4,12},{8,0},{12,4},{1,9},{5,13},{9,1},{13,5},{2,10},{6,14},... | collective-permute-start | bytes 233480 | tf_op jit(solution)/shard_map/ppermute | solution.py:337
  26.4 7.2 %collective-permute-start.8 = (f32[152,128]{1,0:T(8,128)S(1)}, f32[152,128]{1,0:T(8,128)S(1)}, u32[]{:S(2)}, u32[]{:S(2)}) collective-permute-start(f32[152,128]{1,0:T(8,128)S(1)} %shard_map.69.refs_0_), channel_id=1, source_target_pairs={{0,4},{4,0},{8,12},{12,8},{1,5},{5,1},{9,13},{13,9},{2,6},{6,2},{1... | collective-permute-start | bytes 233480 | tf_op jit(solution)/shard_map/ppermute | solution.py:337
  26.8 6.9 %collective-permute-start.7 = (f32[152,128]{1,0:T(8,128)S(1)}, f32[152,128]{1,0:T(8,128)S(1)}, u32[]{:S(2)}, u32[]{:S(2)}) collective-permute-start(f32[152,128]{1,0:T(8,128)S(1)} %shard_map.69.refs_0_), channel_id=1, source_target_pairs={{0,16},{16,0},{32,48},{48,32},{64,80},{80,64},{96,112},{112,96},{1... | collective-permute-start | bytes 233480 | tf_op jit(solution)/shard_map/ppermute | solution.py:337
  28.9 4.8 %collective-permute-start.13 = (f32[152,128]{1,0:T(8,128)S(1)}, f32[152,128]{1,0:T(8,128)S(1)}, u32[]{:S(2)}, u32[]{:S(2)}) collective-permute-start(f32[152,128]{1,0:T(8,128)S(1)} %collective-permute-done.12.refs_6_), channel_id=1, source_target_pairs={{0,16},{16,0},{32,48},{48,32},{64,80},{80,64},{96,112},{112,96},{1... | collective-permute-start | bytes 233480 | tf_op jit(solution)/shard_map/ppermute | solution.py:337
  30.9 3.8 %collective-permute-start.11 = (f32[152,128]{1,0:T(8,128)S(1)}, f32[152,128]{1,0:T(8,128)S(1)}, u32[]{:S(2)}, u32[]{:S(2)}) collective-permute-start(f32[152,128]{1,0:T(8,128)S(1)} %collective-permute-done.10.refs_4_), channel_id=1, source_target_pairs={{0,16},{16,0},{32,48},{48,32},{64,80},{80,64},{96,112},{112,96},{1... | collective-permute-start | bytes 233480 | tf_op jit(solution)/shard_map/ppermute | solution.py:337
  33.7 1.3 %collective-permute-start.9 = (f32[152,128]{1,0:T(8,128)S(1)}, f32[152,128]{1,0:T(8,128)S(1)}, u32[]{:S(2)}, u32[]{:S(2)}) collective-permute-start(f32[152,128]{1,0:T(8,128)S(1)} %collective-permute-done.8.refs_2_), channel_id=1, source_target_pairs={{0,16},{16,0},{32,48},{48,32},{64,80},{80,64},{96,112},{112,96},{1... | collective-permute-start | bytes 233480 | tf_op jit(solution)/shard_map/ppermute | solution.py:337
  46.4 5.7 %collective-permute-start.14 = (bf16[656,128]{1,0:T(8,128)(2,1)S(1)}, bf16[656,128]{1,0:T(8,128)(2,1)S(1)}, u32[]{:S(2)}, u32[]{:S(2)}) collective-permute-start(bf16[656,128]{1,0:T(8,128)(2,1)S(1)} %get-tuple-element.29.first_ref), channel_id=1, source_target_pairs={{0,1},{1,0},{2,3},{3,2},{16,19},{17,18},{18,17},{19,16},{32,33},{3... | collective-permute-start | bytes 503816 | tf_op jit(solution)/shard_map/ppermute | solution.py:358
  49.0 5.8 %collective-permute-start.16 = (bf16[656,128]{1,0:T(8,128)(2,1)S(1)}, bf16[656,128]{1,0:T(8,128)(2,1)S(1)}, u32[]{:S(2)}, u32[]{:S(2)}) collective-permute-start(bf16[656,128]{1,0:T(8,128)(2,1)S(1)} %get-tuple-element.30.second_ref), channel_id=1, source_target_pairs={{0,1},{1,0},{2,3},{3,2},{16,19},{17,18},{18,17},{19,16},{32,33},{3... | collective-permute-start | bytes 503816 | tf_op jit(solution)/shard_map/ppermute | solution.py:358
  50.6 9.0 %copy-start = (bf16[4,512,512]{2,1,0:T(8,128)(2,1)}, bf16[4,512,512]{2,1,0:T(8,128)(2,1)S(1)}, u32[]{:S(2)}) copy-start(bf16[4,512,512]{2,1,0:T(8,128)(2,1)S(1)} %add_convert_fusion.momentum_ref) | copy-start | bytes 6291460
  52.1 4.8 %collective-permute-start.15 = (bf16[656,128]{1,0:T(8,128)(2,1)S(1)}, bf16[656,128]{1,0:T(8,128)(2,1)S(1)}, u32[]{:S(2)}, u32[]{:S(2)}) collective-permute-start(bf16[656,128]{1,0:T(8,128)(2,1)S(1)} %collective-permute-done.14.first_ref), channel_id=1, source_target_pairs={{0,3},{1,2},{2,1},{3,0},{16,17},{17,16},{18,19},{19,18},{32,35},{3... | collective-permute-start | bytes 503816 | tf_op jit(solution)/shard_map/ppermute | solution.py:358
  52.4 6.2 %collective-permute-start.19 = (bf16[656,128]{1,0:T(8,128)(2,1)S(1)}, bf16[656,128]{1,0:T(8,128)(2,1)S(1)}, u32[]{:S(2)}, u32[]{:S(2)}) collective-permute-start(bf16[656,128]{1,0:T(8,128)(2,1)S(1)} %collective-permute-done.14.first_ref), channel_id=1, source_target_pairs={{0,16},{16,0},{32,48},{48,32},{64,80},{80,64},{96,112},{112,96},{1... | collective-permute-start | bytes 503816 | tf_op jit(solution)/shard_map/ppermute | solution.py:337
  54.8 3.8 %collective-permute-start.18 = (bf16[656,128]{1,0:T(8,128)(2,1)S(1)}, bf16[656,128]{1,0:T(8,128)(2,1)S(1)}, u32[]{:S(2)}, u32[]{:S(2)}) collective-permute-start(bf16[656,128]{1,0:T(8,128)(2,1)S(1)} %collective-permute-done.16.second_ref), channel_id=1, source_target_pairs={{0,16},{16,0},{32,48},{48,32},{64,80},{80,64},{96,112},{112,96},{1... | collective-permute-start | bytes 503816 | tf_op jit(solution)/shard_map/ppermute | solution.py:337
  56.9 2.7 %collective-permute-start.17 = (bf16[656,128]{1,0:T(8,128)(2,1)S(1)}, bf16[656,128]{1,0:T(8,128)(2,1)S(1)}, u32[]{:S(2)}, u32[]{:S(2)}) collective-permute-start(bf16[656,128]{1,0:T(8,128)(2,1)S(1)} %collective-permute-done.15.first_ref), channel_id=1, source_target_pairs={{0,16},{16,0},{32,48},{48,32},{64,80},{80,64},{96,112},{112,96},{1... | collective-permute-start | bytes 503816 | tf_op jit(solution)/shard_map/ppermute | solution.py:337
  (2 other events, 6.6 us)

commit v6 on v5

--- a/solution.py
+++ b/solution.py
@@ -385,7 +385,9 @@
     last = functools.partial(last_product, update_scale)
     peaks, late_momentum = lax.optimization_barrier((peaks, momentum))
     new_momentum = decayed(late_momentum, gradient)
-    near = tuple(by_core(piece, "ctx", (1, 3)) for piece in (first, second))
+    near_first = by_core(first, "ctx", (1, 3))
+    late_second, new_momentum = lax.optimization_barrier((second, new_momentum))
+    near = near_first, by_core(late_second, "ctx", (1, 3))
     new_weights = last((0, 0), weights, new_momentum, peaks, (first, second))
     near_first, new_weights = lax.optimization_barrier((near[0], new_weights))
     far = by_core(near_first, "ctx", (3, 1))

time: 61.4 us -> 61.4 us (level)
  local copies, waits for them, and re-layouts: 0.83 us -> 0.12 us
  starting transfers between devices: 31.5 us -> 32.2 us
    ppermute x13, starting transfers between devices: 21.2 us -> 22.1 us  [crossed(): lax.ppermute(value, axis, [(at, at ^ mask) for at in range(lax.axis_size(...]
    unnamed x12, local copies, waits for them, and re-layouts: 0.74 us -> 0.03 us
  transfers between devices with their start and end apart: 20 -> 20, of which waited for: 9 -> 10; matrix products, arithmetic and copies ran while one was open for 2% -> 1% of each run, Pallas kernels for 6% -> 5%
where the time goes in v6:
time: 61.4 us; the launch traced here: 61.3 us
  starting transfers between devices  32.2 us (52%)
  Pallas kernels  17.8 us (29%)
  waiting for transfers between devices  9.33 us (15%)
  between operations  0.95 us (2%)
  other arithmetic  0.85 us (1%)
    ppermute x13, starting transfers between devices, crossed(): lax.ppermute(value, axis, [(at, at ^ mask) for at in range(lax.axis_size(...  22.1 us
    pallas_call x1, Pallas kernels, newton(): pl.pallas_call(newton_kernel, out_shape=(piece, piece, jax.ShapeDtypeStru...  11.5 us
    ppermute x4, starting transfers between devices, along_z(): return lax.ppermute(value, 'fsdp', pairs)  7.27 us
    ppermute x13, waiting for transfers between devices, crossed(): lax.ppermute(value, axis, [(at, at ^ mask) for at in range(lax.axis_size(...  5.33 us
    pallas_call x4, Pallas kernels, last_product(): pl.pallas_call(functools.partial(last_kernel, update_scale, masks, waitin...  4.73 us
    ppermute x4, waiting for transfers between devices, along_z(): return lax.ppermute(value, 'fsdp', pairs)  2.98 us
    ppermute x3, starting transfers between devices, by_core(): return lax.ppermute(value, ('fsdp', axis), pairs)  2.87 us
    pallas_call x1, Pallas kernels, partial_gram(): pl.pallas_call(partial_gram_kernel, out_shape=(shape, shape), in_specs=[p...  1.62 us
  transfers between devices with their start and end apart: 20, of which 10 were waited for; matrix products, arithmetic and copies ran while one was open for 1% of the time, Pallas kernels for 5%

profile of v6, /device:TPU:1, one launch (start us, length us, event | category | flops | bytes accessed | tf_op | source)
XLA Modules:
  0.0 61.3 jit_solution(264143855978229906)
XLA Ops:
  0.6 1.6 %shard_map.68 = (f32[144,128]{1,0:T(8,128)S(1)}, f32[144,128]{1,0:T(8,128)S(1)}) custom-call(bf16[4,512,512]{2,1,0:T(8,128)(2,1)} %momentum_ref.1, bf16[4,512,512]{2,1,0:T(8,128)(2,1)} %gradient_ref.1), custom_call_target="tpu_custom_call" | custom-call | flops 37748736 | bytes 786432 | tf_op jit(solution)/shard_map/pallas_call | solution.py:84
  2.3 3.3 %collective-permute-start = (f32[144,128]{1,0:T(8,128)S(1)}, f32[144,128]{1,0:T(8,128)S(1)}, u32[]{:S(2)}, u32[]{:S(2)}) collective-permute-start(f32[144,128]{1,0:T(8,128)S(1)} %get-tuple-element.23), channel_id=1, source_target_pairs={{0,16},{16,0},{32,48},{48,32},{64,80},{80,64},{96,112},{112,96},{1... | collective-permute-start | bytes 221192 | tf_op jit(solution)/shard_map/ppermute | solution.py:337
  5.9 0.6 %collective-permute-done = f32[144,128]{1,0:T(8,128)S(1)} collective-permute-done((f32[144,128]{1,0:T(8,128)S(1)}, f32[144,128]{1,0:T(8,128)S(1)}, u32[]{:S(2)}, u32[]{:S(2)}) %collective-permute-start) | collective-permute-done | bytes 73760 | tf_op jit(solution)/shard_map/ppermute | solution.py:337
  6.5 3.9 %collective-permute-start.3 = (f32[144,128]{1,0:T(8,128)S(1)}, f32[144,128]{1,0:T(8,128)S(1)}, u32[]{:S(2)}, u32[]{:S(2)}) collective-permute-start(f32[144,128]{1,0:T(8,128)S(1)} %add.15), channel_id=1, source_target_pairs={{0,96},{16,240},{32,64},{48,208},{64,32},{80,176},{96,0},{112,144}... | collective-permute-start | bytes 221192 | tf_op jit(solution)/shard_map/ppermute | solution.py:348
  11.0 1.1 %collective-permute-start.1 = (f32[144,128]{1,0:T(8,128)S(1)}, f32[144,128]{1,0:T(8,128)S(1)}, u32[]{:S(2)}, u32[]{:S(2)}) collective-permute-start(f32[144,128]{1,0:T(8,128)S(1)} %add.15), channel_id=1, source_target_pairs={{0,32},{16,48},{32,0},{48,16},{64,96},{80,112},{96,64},{112,80},{1... | collective-permute-start | bytes 221192 | tf_op jit(solution)/shard_map/ppermute | solution.py:348
  12.1 1.2 %collective-permute-start.4 = (f32[8,128]{1,0:T(8,128)S(1)}, f32[8,128]{1,0:T(8,128)S(1)}, u32[]{:S(2)}, u32[]{:S(2)}) collective-permute-start(f32[8,128]{1,0:T(8,128)S(1)} %broadcast_in_dim.37), channel_id=1, source_target_pairs={{0,1},{1,0},{2,3},{3,2},{4,5},{5,4},{6,7},{7,6},{8,9},{9,8},{10,11... | collective-permute-start | bytes 12296 | tf_op jit(solution)/shard_map/ppermute | solution.py:337
  13.3 1.5 %collective-permute-done.4 = f32[8,128]{1,0:T(8,128)S(1)} collective-permute-done((f32[8,128]{1,0:T(8,128)S(1)}, f32[8,128]{1,0:T(8,128)S(1)}, u32[]{:S(2)}, u32[]{:S(2)}) %collective-permute-start.4) | collective-permute-done | bytes 4128 | tf_op jit(solution)/shard_map/ppermute | solution.py:337
  14.9 3.0 %collective-permute-done.2 = f32[144,128]{1,0:T(8,128)S(1)} collective-permute-done((f32[144,128]{1,0:T(8,128)S(1)}, f32[144,128]{1,0:T(8,128)S(1)}, u32[]{:S(2)}, u32[]{:S(2)}) %collective-permute-start.2) | collective-permute-done | bytes 73760 | tf_op jit(solution)/shard_map/ppermute | solution.py:348
  17.9 1.7 %collective-permute-start.5 = (f32[144,128]{1,0:T(8,128)S(1)}, f32[144,128]{1,0:T(8,128)S(1)}, u32[]{:S(2)}, u32[]{:S(2)}) collective-permute-start(f32[144,128]{1,0:T(8,128)S(1)} %add_add_fusion.total_ref), channel_id=1, source_target_pairs={{0,224},{16,112},{32,192},{48,80},{64,160},{80,48},{96,128},{112,1... | collective-permute-start | bytes 221192 | tf_op jit(solution)/shard_map/ppermute | solution.py:348
  19.6 2.5 %collective-permute-start.6 = (f32[8,128]{1,0:T(8,128)S(1)}, f32[8,128]{1,0:T(8,128)S(1)}, u32[]{:S(2)}, u32[]{:S(2)}) collective-permute-start(f32[8,128]{1,0:T(8,128)S(1)} %max.3.peaks_ref), channel_id=1, source_target_pairs={{0,3},{1,2},{2,1},{3,0},{4,7},{5,6},{6,5},{7,4},{8,11},{9,10},{10,... | collective-permute-start | bytes 12296 | tf_op jit(solution)/shard_map/ppermute | solution.py:337
  22.0 1.2 %collective-permute-done.6.peaks_arrived_ref = f32[8,128]{1,0:T(8,128)S(1)} collective-permute-done((f32[8,128]{1,0:T(8,128)S(1)}, f32[8,128]{1,0:T(8,128)S(1)}, u32[]{:S(2)}, u32[]{:S(2)}) %collective-permute-start.6) | collective-permute-done | bytes 4128 | tf_op jit(solution)/shard_map/ppermute | solution.py:337
  23.3 2.8 %collective-permute-start.12 = (f32[152,128]{1,0:T(8,128)S(1)}, f32[152,128]{1,0:T(8,128)S(1)}, u32[]{:S(2)}, u32[]{:S(2)}) collective-permute-start(f32[152,128]{1,0:T(8,128)S(1)} %shard_map.69.refs_0_), channel_id=1, source_target_pairs={{0,12},{4,8},{8,4},{12,0},{1,13},{5,9},{9,5},{13,1},{2,14},{6,10},... | collective-permute-start | bytes 233480 | tf_op jit(solution)/shard_map/ppermute | solution.py:337
  26.8 2.1 %collective-permute-start.7 = (f32[152,128]{1,0:T(8,128)S(1)}, f32[152,128]{1,0:T(8,128)S(1)}, u32[]{:S(2)}, u32[]{:S(2)}) collective-permute-start(f32[152,128]{1,0:T(8,128)S(1)} %shard_map.69.refs_0_), channel_id=1, source_target_pairs={{0,16},{16,0},{32,48},{48,32},{64,80},{80,64},{96,112},{112,96},{1... | collective-permute-start | bytes 233480 | tf_op jit(solution)/shard_map/ppermute | solution.py:337
  28.9 1.7 %collective-permute-start.13 = (f32[152,128]{1,0:T(8,128)S(1)}, f32[152,128]{1,0:T(8,128)S(1)}, u32[]{:S(2)}, u32[]{:S(2)}) collective-permute-start(f32[152,128]{1,0:T(8,128)S(1)} %collective-permute-done.12.refs_6_), channel_id=1, source_target_pairs={{0,16},{16,0},{32,48},{48,32},{64,80},{80,64},{96,112},{112,96},{1... | collective-permute-start | bytes 233480 | tf_op jit(solution)/shard_map/ppermute | solution.py:337
  30.9 2.8 %collective-permute-start.11 = (f32[152,128]{1,0:T(8,128)S(1)}, f32[152,128]{1,0:T(8,128)S(1)}, u32[]{:S(2)}, u32[]{:S(2)}) collective-permute-start(f32[152,128]{1,0:T(8,128)S(1)} %collective-permute-done.10.refs_4_), channel_id=1, source_target_pairs={{0,16},{16,0},{32,48},{48,32},{64,80},{80,64},{96,112},{112,96},{1... | collective-permute-start | bytes 233480 | tf_op jit(solution)/shard_map/ppermute | solution.py:337
  33.7 0.9 %collective-permute-done.11.refs_5_ = f32[152,128]{1,0:T(8,128)S(1)} collective-permute-done((f32[152,128]{1,0:T(8,128)S(1)}, f32[152,128]{1,0:T(8,128)S(1)}, u32[]{:S(2)}, u32[]{:S(2)}) %collective-permute-start.11) | collective-permute-done | bytes 77856 | tf_op jit(solution)/shard_map/ppermute | solution.py:337
  35.0 11.5 %shard_map.70 = (bf16[656,128]{1,0:T(8,128)(2,1)S(1)}, bf16[656,128]{1,0:T(8,128)(2,1)S(1)}, f32[8,128]{1,0:T(8,128)S(1)}) custom-call(f32[152,128]{1,0:T(8,128)S(1)} %shard_map.69.refs_0_, f32[152,128]{1,0:T(8,128)S(1)} %collective-permute-done.7.refs_1_, f32[152,128]{1,0:T(8,128)S(1)} %collective-permute-done.8.refs_2_, ...), custom_call_target="tpu_custom_call" | custom-call | flops 13690208256 | bytes 1572864 | tf_op jit(solution)/shard_map/pallas_call | solution.py:229
  46.4 2.6 %collective-permute-start.14 = (bf16[656,128]{1,0:T(8,128)(2,1)S(1)}, bf16[656,128]{1,0:T(8,128)(2,1)S(1)}, u32[]{:S(2)}, u32[]{:S(2)}) collective-permute-start(bf16[656,128]{1,0:T(8,128)(2,1)S(1)} %get-tuple-element.33.first_ref), channel_id=1, source_target_pairs={{0,1},{1,0},{2,3},{3,2},{16,19},{17,18},{18,17},{19,16},{32,33},{3... | collective-permute-start | bytes 503816 | tf_op jit(solution)/shard_map/ppermute | solution.py:358
  49.0 0.6 %add_convert_fusion.momentum_ref = bf16[4,512,512]{2,1,0:T(8,128)(2,1)S(1)} fusion(bf16[4,512,512]{2,1,0:T(8,128)(2,1)S(1)} %copy-done.2, bf16[4,512,512]{2,1,0:T(8,128)(2,1)S(1)} %copy-done.3), kind=kLoop, calls=%fused_computation | loop fusion | flops 5242880 | bytes 6291456 | tf_op jit(solution)/shard_map/convert_element_type | solution.py:36
  50.0 1.3 %shard_map.71.refs_0_ = bf16[4,512,512]{2,1,0:T(8,128)(2,1)} custom-call(bf16[4,512,512]{2,1,0:T(8,128)(2,1)S(1)} %copy-done.1, bf16[4,512,512]{2,1,0:T(8,128)(2,1)S(1)} %add_convert_fusion.momentum_ref, f32[8,128]{1,0:T(8,128)S(1)} %get-tuple-element.32.peaks_ref, bf16[656,128]{1,0:T(8,128)(2,1)S(1)} %get-tuple-element.33.first_ref, ...), custom_call_target="tpu_custom_call" | custom-call | flops 268435456 | bytes 1572864 | tf_op jit(solution)/shard_map/pallas_call | solution.py:307
  52.0 2.8 %collective-permute-start.19 = (bf16[656,128]{1,0:T(8,128)(2,1)S(1)}, bf16[656,128]{1,0:T(8,128)(2,1)S(1)}, u32[]{:S(2)}, u32[]{:S(2)}) collective-permute-start(bf16[656,128]{1,0:T(8,128)(2,1)S(1)} %collective-permute-done.14.first_ref), channel_id=1, source_target_pairs={{0,16},{16,0},{32,48},{48,32},{64,80},{80,64},{96,112},{112,96},{1... | collective-permute-start | bytes 503816 | tf_op jit(solution)/shard_map/ppermute | solution.py:337
  55.2 1.3 %shard_map.72.refs_1_ = bf16[4,512,512]{2,1,0:T(8,128)(2,1)} custom-call(bf16[4,512,512]{2,1,0:T(8,128)(2,1)S(1)} %copy-done.1, bf16[4,512,512]{2,1,0:T(8,128)(2,1)S(1)} %add_convert_fusion.momentum_ref, f32[8,128]{1,0:T(8,128)S(1)} %get-tuple-element.32.peaks_ref, ...), custom_call_target="tpu_custom_call", output_to_operand_aliasing={{}: (5, {})} | custom-call | flops 268435456 | bytes 1572864 | tf_op jit(solution)/shard_map/pallas_call | solution.py:307
  56.6 2.1 %collective-permute-start.17 = (bf16[656,128]{1,0:T(8,128)(2,1)S(1)}, bf16[656,128]{1,0:T(8,128)(2,1)S(1)}, u32[]{:S(2)}, u32[]{:S(2)}) collective-permute-start(bf16[656,128]{1,0:T(8,128)(2,1)S(1)} %collective-permute-done.15.first_ref), channel_id=1, source_target_pairs={{0,16},{16,0},{32,48},{48,32},{64,80},{80,64},{96,112},{112,96},{1... | collective-permute-start | bytes 503816 | tf_op jit(solution)/shard_map/ppermute | solution.py:337
  59.6 1.4 %shard_map.74 = bf16[4,512,512]{2,1,0:T(8,128)(2,1)} custom-call(bf16[4,512,512]{2,1,0:T(8,128)(2,1)S(1)} %copy-done.1, bf16[4,512,512]{2,1,0:T(8,128)(2,1)S(1)} %add_convert_fusion.momentum_ref, f32[8,128]{1,0:T(8,128)S(1)} %get-tuple-element.32.peaks_ref, bf16[656,128]{1,0:T(8,128)(2,1)S(1)} %collective-permute-done.15.first_ref, ...), custom_call_target="tpu_custom_call", output_to_operand_aliasing={{}: (6, {})} | custom-call | flops 268435456 | bytes 1572864 | tf_op jit(solution)/shard_map/pallas_call | solution.py:307
  (43 shorter events, 4.6 us)
Async XLA Ops:
  0.6 5.0 %copy-start.4 = (f32[1,1,61,32]{2,3,1,0:T(8,128)S(1)}, f32[1,1,61,32]{2,3,1,0:T(8,128)}, u32[]{:S(2)}) copy-start(f32[1,1,61,32]{2,3,1,0:T(8,128)} %param.8) | copy-start | bytes 23428
  2.3 4.2 %collective-permute-start = (f32[144,128]{1,0:T(8,128)S(1)}, f32[144,128]{1,0:T(8,128)S(1)}, u32[]{:S(2)}, u32[]{:S(2)}) collective-permute-start(f32[144,128]{1,0:T(8,128)S(1)} %get-tuple-element.23), channel_id=1, source_target_pairs={{0,16},{16,0},{32,48},{48,32},{64,80},{80,64},{96,112},{112,96},{1... | collective-permute-start | bytes 221192 | tf_op jit(solution)/shard_map/ppermute | solution.py:337
  6.5 8.3 %collective-permute-start.3 = (f32[144,128]{1,0:T(8,128)S(1)}, f32[144,128]{1,0:T(8,128)S(1)}, u32[]{:S(2)}, u32[]{:S(2)}) collective-permute-start(f32[144,128]{1,0:T(8,128)S(1)} %add.15), channel_id=1, source_target_pairs={{0,96},{16,240},{32,64},{48,208},{64,32},{80,176},{96,0},{112,144}... | collective-permute-start | bytes 221192 | tf_op jit(solution)/shard_map/ppermute | solution.py:348
  10.5 7.4 %collective-permute-start.2 = (f32[144,128]{1,0:T(8,128)S(1)}, f32[144,128]{1,0:T(8,128)S(1)}, u32[]{:S(2)}, u32[]{:S(2)}) collective-permute-start(f32[144,128]{1,0:T(8,128)S(1)} %add.15), channel_id=1, source_target_pairs={{0,64},{16,208},{32,96},{48,240},{64,0},{80,144},{96,32},{112,176}... | collective-permute-start | bytes 221192 | tf_op jit(solution)/shard_map/ppermute | solution.py:348
  11.0 6.8 %collective-permute-start.1 = (f32[144,128]{1,0:T(8,128)S(1)}, f32[144,128]{1,0:T(8,128)S(1)}, u32[]{:S(2)}, u32[]{:S(2)}) collective-permute-start(f32[144,128]{1,0:T(8,128)S(1)} %add.15), channel_id=1, source_target_pairs={{0,32},{16,48},{32,0},{48,16},{64,96},{80,112},{96,64},{112,80},{1... | collective-permute-start | bytes 221192 | tf_op jit(solution)/shard_map/ppermute | solution.py:348
  12.1 2.8 %collective-permute-start.4 = (f32[8,128]{1,0:T(8,128)S(1)}, f32[8,128]{1,0:T(8,128)S(1)}, u32[]{:S(2)}, u32[]{:S(2)}) collective-permute-start(f32[8,128]{1,0:T(8,128)S(1)} %broadcast_in_dim.37), channel_id=1, source_target_pairs={{0,1},{1,0},{2,3},{3,2},{4,5},{5,4},{6,7},{7,6},{8,9},{9,8},{10,11... | collective-permute-start | bytes 12296 | tf_op jit(solution)/shard_map/ppermute | solution.py:337
  17.9 5.4 %collective-permute-start.5 = (f32[144,128]{1,0:T(8,128)S(1)}, f32[144,128]{1,0:T(8,128)S(1)}, u32[]{:S(2)}, u32[]{:S(2)}) collective-permute-start(f32[144,128]{1,0:T(8,128)S(1)} %add_add_fusion.total_ref), channel_id=1, source_target_pairs={{0,224},{16,112},{32,192},{48,80},{64,160},{80,48},{96,128},{112,1... | collective-permute-start | bytes 221192 | tf_op jit(solution)/shard_map/ppermute | solution.py:348
  19.6 3.7 %collective-permute-start.6 = (f32[8,128]{1,0:T(8,128)S(1)}, f32[8,128]{1,0:T(8,128)S(1)}, u32[]{:S(2)}, u32[]{:S(2)}) collective-permute-start(f32[8,128]{1,0:T(8,128)S(1)} %max.3.peaks_ref), channel_id=1, source_target_pairs={{0,3},{1,2},{2,1},{3,0},{4,7},{5,6},{6,5},{7,4},{8,11},{9,10},{10,... | collective-permute-start | bytes 12296 | tf_op jit(solution)/shard_map/ppermute | solution.py:337
  23.3 25.8 %copy-start.2 = (bf16[4,512,512]{2,1,0:T(8,128)(2,1)S(1)}, bf16[4,512,512]{2,1,0:T(8,128)(2,1)}, u32[]{:S(2)}) copy-start(bf16[4,512,512]{2,1,0:T(8,128)(2,1)} %gradient_ref.1) | copy-start | bytes 6291460
  23.3 25.7 %copy-start.3 = (bf16[4,512,512]{2,1,0:T(8,128)(2,1)S(1)}, bf16[4,512,512]{2,1,0:T(8,128)(2,1)}, u32[]{:S(2)}) copy-start(bf16[4,512,512]{2,1,0:T(8,128)(2,1)} %momentum_ref.1) | copy-start | bytes 6291460
  23.3 5.6 %collective-permute-start.12 = (f32[152,128]{1,0:T(8,128)S(1)}, f32[152,128]{1,0:T(8,128)S(1)}, u32[]{:S(2)}, u32[]{:S(2)}) collective-permute-start(f32[152,128]{1,0:T(8,128)S(1)} %shard_map.69.refs_0_), channel_id=1, source_target_pairs={{0,12},{4,8},{8,4},{12,0},{1,13},{5,9},{9,5},{13,1},{2,14},{6,10},... | collective-permute-start | bytes 233480 | tf_op jit(solution)/shard_map/ppermute | solution.py:337
  26.1 4.8 %collective-permute-start.10 = (f32[152,128]{1,0:T(8,128)S(1)}, f32[152,128]{1,0:T(8,128)S(1)}, u32[]{:S(2)}, u32[]{:S(2)}) collective-permute-start(f32[152,128]{1,0:T(8,128)S(1)} %shard_map.69.refs_0_), channel_id=1, source_target_pairs={{0,8},{4,12},{8,0},{12,4},{1,9},{5,13},{9,1},{13,5},{2,10},{6,14},... | collective-permute-start | bytes 233480 | tf_op jit(solution)/shard_map/ppermute | solution.py:337
  26.4 7.2 %collective-permute-start.8 = (f32[152,128]{1,0:T(8,128)S(1)}, f32[152,128]{1,0:T(8,128)S(1)}, u32[]{:S(2)}, u32[]{:S(2)}) collective-permute-start(f32[152,128]{1,0:T(8,128)S(1)} %shard_map.69.refs_0_), channel_id=1, source_target_pairs={{0,4},{4,0},{8,12},{12,8},{1,5},{5,1},{9,13},{13,9},{2,6},{6,2},{1... | collective-permute-start | bytes 233480 | tf_op jit(solution)/shard_map/ppermute | solution.py:337
  26.8 6.9 %collective-permute-start.7 = (f32[152,128]{1,0:T(8,128)S(1)}, f32[152,128]{1,0:T(8,128)S(1)}, u32[]{:S(2)}, u32[]{:S(2)}) collective-permute-start(f32[152,128]{1,0:T(8,128)S(1)} %shard_map.69.refs_0_), channel_id=1, source_target_pairs={{0,16},{16,0},{32,48},{48,32},{64,80},{80,64},{96,112},{112,96},{1... | collective-permute-start | bytes 233480 | tf_op jit(solution)/shard_map/ppermute | solution.py:337
  28.9 4.8 %collective-permute-start.13 = (f32[152,128]{1,0:T(8,128)S(1)}, f32[152,128]{1,0:T(8,128)S(1)}, u32[]{:S(2)}, u32[]{:S(2)}) collective-permute-start(f32[152,128]{1,0:T(8,128)S(1)} %collective-permute-done.12.refs_6_), channel_id=1, source_target_pairs={{0,16},{16,0},{32,48},{48,32},{64,80},{80,64},{96,112},{112,96},{1... | collective-permute-start | bytes 233480 | tf_op jit(solution)/shard_map/ppermute | solution.py:337
  30.9 3.8 %collective-permute-start.11 = (f32[152,128]{1,0:T(8,128)S(1)}, f32[152,128]{1,0:T(8,128)S(1)}, u32[]{:S(2)}, u32[]{:S(2)}) collective-permute-start(f32[152,128]{1,0:T(8,128)S(1)} %collective-permute-done.10.refs_4_), channel_id=1, source_target_pairs={{0,16},{16,0},{32,48},{48,32},{64,80},{80,64},{96,112},{112,96},{1... | collective-permute-start | bytes 233480 | tf_op jit(solution)/shard_map/ppermute | solution.py:337
  33.7 1.3 %collective-permute-start.9 = (f32[152,128]{1,0:T(8,128)S(1)}, f32[152,128]{1,0:T(8,128)S(1)}, u32[]{:S(2)}, u32[]{:S(2)}) collective-permute-start(f32[152,128]{1,0:T(8,128)S(1)} %collective-permute-done.8.refs_2_), channel_id=1, source_target_pairs={{0,16},{16,0},{32,48},{48,32},{64,80},{80,64},{96,112},{112,96},{1... | collective-permute-start | bytes 233480 | tf_op jit(solution)/shard_map/ppermute | solution.py:337
  46.4 5.5 %collective-permute-start.14 = (bf16[656,128]{1,0:T(8,128)(2,1)S(1)}, bf16[656,128]{1,0:T(8,128)(2,1)S(1)}, u32[]{:S(2)}, u32[]{:S(2)}) collective-permute-start(bf16[656,128]{1,0:T(8,128)(2,1)S(1)} %get-tuple-element.33.first_ref), channel_id=1, source_target_pairs={{0,1},{1,0},{2,3},{3,2},{16,19},{17,18},{18,17},{19,16},{32,33},{3... | collective-permute-start | bytes 503816 | tf_op jit(solution)/shard_map/ppermute | solution.py:358
  49.7 10.0 %copy-start = (bf16[4,512,512]{2,1,0:T(8,128)(2,1)}, bf16[4,512,512]{2,1,0:T(8,128)(2,1)S(1)}, u32[]{:S(2)}) copy-start(bf16[4,512,512]{2,1,0:T(8,128)(2,1)S(1)} %add_convert_fusion.momentum_ref) | copy-start | bytes 6291460
  49.7 5.5 %collective-permute-start.16 = (bf16[656,128]{1,0:T(8,128)(2,1)S(1)}, bf16[656,128]{1,0:T(8,128)(2,1)S(1)}, u32[]{:S(2)}, u32[]{:S(2)}) collective-permute-start(bf16[656,128]{1,0:T(8,128)(2,1)S(1)} %get-tuple-element.35.second_ref), channel_id=1, source_target_pairs={{0,1},{1,0},{2,3},{3,2},{16,19},{17,18},{18,17},{19,16},{32,33},{3... | collective-permute-start | bytes 503816 | tf_op jit(solution)/shard_map/ppermute | solution.py:358
  52.0 4.6 %collective-permute-start.15 = (bf16[656,128]{1,0:T(8,128)(2,1)S(1)}, bf16[656,128]{1,0:T(8,128)(2,1)S(1)}, u32[]{:S(2)}, u32[]{:S(2)}) collective-permute-start(bf16[656,128]{1,0:T(8,128)(2,1)S(1)} %collective-permute-done.14.first_ref), channel_id=1, source_target_pairs={{0,3},{1,2},{2,1},{3,0},{16,17},{17,16},{18,19},{19,18},{32,35},{3... | collective-permute-start | bytes 503816 | tf_op jit(solution)/shard_map/ppermute | solution.py:358
  52.0 6.7 %collective-permute-start.19 = (bf16[656,128]{1,0:T(8,128)(2,1)S(1)}, bf16[656,128]{1,0:T(8,128)(2,1)S(1)}, u32[]{:S(2)}, u32[]{:S(2)}) collective-permute-start(bf16[656,128]{1,0:T(8,128)(2,1)S(1)} %collective-permute-done.14.first_ref), channel_id=1, source_target_pairs={{0,16},{16,0},{32,48},{48,32},{64,80},{80,64},{96,112},{112,96},{1... | collective-permute-start | bytes 503816 | tf_op jit(solution)/shard_map/ppermute | solution.py:337
  55.2 3.4 %collective-permute-start.18 = (bf16[656,128]{1,0:T(8,128)(2,1)S(1)}, bf16[656,128]{1,0:T(8,128)(2,1)S(1)}, u32[]{:S(2)}, u32[]{:S(2)}) collective-permute-start(bf16[656,128]{1,0:T(8,128)(2,1)S(1)} %collective-permute-done.16.second_ref), channel_id=1, source_target_pairs={{0,16},{16,0},{32,48},{48,32},{64,80},{80,64},{96,112},{112,96},{1... | collective-permute-start | bytes 503816 | tf_op jit(solution)/shard_map/ppermute | solution.py:337
  56.6 3.1 %collective-permute-start.17 = (bf16[656,128]{1,0:T(8,128)(2,1)S(1)}, bf16[656,128]{1,0:T(8,128)(2,1)S(1)}, u32[]{:S(2)}, u32[]{:S(2)}) collective-permute-start(bf16[656,128]{1,0:T(8,128)(2,1)S(1)} %collective-permute-done.15.first_ref), channel_id=1, source_target_pairs={{0,16},{16,0},{32,48},{48,32},{64,80},{80,64},{96,112},{112,96},{1... | collective-permute-start | bytes 503816 | tf_op jit(solution)/shard_map/ppermute | solution.py:337
  (2 other events, 8.5 us)

commit v7 on v5

--- a/solution.py
+++ b/solution.py
@@ -251,19 +251,8 @@
     return lax.axis_index("ctx") ^ (masks[0] + (masks[1] - masks[0]) * core)
 
 
-def last_kernel(update_scale, masks, waiting_masks, keeps, weights_ref, momentum_ref, peaks_ref, first_ref, second_ref, *refs):
-    stores = []
-    if keeps:
-        fresh, factors = refs[-2:]
-    else:
-        out_ref, factors, fresh, left = refs[-4:]
-    if waiting_masks is not None:
-        stores.append(pltpu.make_async_copy(refs[0], out_ref.at[matrix_at(waiting_masks)], left.at[2]))
-        stores[0].start()
-    rank, cols = fresh.shape
-    shard = lax.axis_index("fsdp")
-    core = lax.rem(shard, 2)
-    matrix = matrix_at(masks)
+def fill(factors, first_ref, second_ref):
+    core = lax.rem(lax.axis_index("fsdp"), 2)
     for side, kept in enumerate(KEPT):
         for at, (row, column) in enumerate(kept):
             rows = slice(at * BLOCK, (at + 1) * BLOCK)
@@ -271,8 +260,16 @@
             factors[row * BLOCK : (row + 1) * BLOCK, column * BLOCK : (column + 1) * BLOCK] = block
             if row != column:
                 factors[column * BLOCK : (column + 1) * BLOCK, row * BLOCK : (row + 1) * BLOCK] = block.T
-    end = first_ref[HALF:, :].astype(jnp.float32)
+
+
+def start_of(momentum, half_ref):
+    end = half_ref[HALF:, :].astype(jnp.float32)
     inverse = 1.0 / ((end[0:1, 0:1] + end[1:2, 0:1]) + end[2:3, 0:1])
+    return (momentum.astype(jnp.float32) * inverse).astype(jnp.bfloat16)
+
+
+def scale_of(matrix, peaks_ref, cols):
+    shard = lax.axis_index("fsdp")
     heads = cols // (KNOPE + VDIM)
     column = lax.broadcasted_iota(jnp.int32, (1, cols), 1)
     lane = lax.broadcasted_iota(jnp.int32, (1, BLOCK), 1)
@@ -280,40 +277,75 @@
     for head in range(heads):
         place = matrix * (BLOCK // BLOCKS) + shard * heads + head
         peak = jnp.max(jnp.where(lane == place, peaks_ref[0:1, :], 0.0), axis=1, keepdims=True)
-        first = head * (KNOPE + VDIM)
-        column_peaks = jnp.where((column >= first) & (column < first + KNOPE), peak, column_peaks)
-    scale = jnp.sqrt(jnp.minimum(1.0, clip_limit / column_peaks))
-    start = (momentum_ref[matrix].astype(jnp.float32) * inverse).astype(jnp.bfloat16)
+        begin = head * (KNOPE + VDIM)
+        column_peaks = jnp.where((column >= begin) & (column < begin + KNOPE), peak, column_peaks)
+    return jnp.sqrt(jnp.minimum(1.0, clip_limit / column_peaks))
+
+
+def fresh_rows(update_scale, weights, factors, start, scale):
+    orthogonal = jnp.dot(factors, start, preferred_element_type=jnp.float32)
+    value = weights.astype(jnp.float32) - step_size * (update_scale * orthogonal)
+    return (value * scale).astype(jnp.bfloat16)
+
+
+def last_kernel(update_scale, masks, weights_ref, momentum_ref, peaks_ref, first_ref, second_ref, *refs):
+    out_ref, factors, fresh, left = refs[-4:]
+    rank, cols = fresh.shape
+    matrix = matrix_at(masks)
+    fill(factors, first_ref, second_ref)
+    start, scale = start_of(momentum_ref[matrix], first_ref), scale_of(matrix, peaks_ref, cols)
+    stores = []
     for at in range(rank // STRIP):
         rows = slice(at * STRIP, (at + 1) * STRIP)
-        orthogonal = jnp.dot(factors[rows, :], start, preferred_element_type=jnp.float32)
-        value = weights_ref[matrix, rows, :].astype(jnp.float32) - step_size * (update_scale * orthogonal)
-        fresh[rows, :] = (value * scale).astype(jnp.bfloat16)
-        if not keeps:
-            stores.append(pltpu.make_async_copy(fresh.at[rows], out_ref.at[matrix, rows], left.at[at]))
-            stores[-1].start()
+        fresh[rows, :] = fresh_rows(update_scale, weights_ref[matrix, rows, :], factors[rows, :], start, scale)
+        stores.append(pltpu.make_async_copy(fresh.at[rows], out_ref.at[matrix, rows], left.at[at]))
+        stores[-1].start()
     for store in stores:
         store.wait()
 
 
-def last_product(update_scale, masks, weights, momentum, peaks, pair, before=None, waiting=None, keeps=False):
+def waiting_kernel(update_scale, masks, next_masks, weights_ref, momentum_ref, peaks_ref, first_ref, second_ref, next_ref, out_ref, start_ref, scale_ref, factors):
+    rank, cols = out_ref.shape
+    matrix, following = matrix_at(masks), matrix_at(next_masks)
+    fill(factors, first_ref, second_ref)
+    start, scale = start_of(momentum_ref[matrix], first_ref), scale_of(matrix, peaks_ref, cols)
+    for at in range(rank // STRIP):
+        rows = slice(at * STRIP, (at + 1) * STRIP)
+        out_ref[rows, :] = fresh_rows(update_scale, weights_ref[matrix, rows, :], factors[rows, :], start, scale)
+    start_ref[...] = start_of(momentum_ref[following], next_ref)
+    scale_ref[...] = jnp.broadcast_to(scale_of(following, peaks_ref, cols), scale_ref.shape)
+
+
+def closing_kernel(update_scale, masks, waiting_masks, weights_ref, first_ref, second_ref, waiting_ref, start_ref, scale_ref, before_ref, out_ref, factors, fresh, left):
+    rank = fresh.shape[0]
+    matrix = matrix_at(masks)
+    stores = [pltpu.make_async_copy(waiting_ref, out_ref.at[matrix_at(waiting_masks)], left.at[2])]
+    stores[0].start()
+    fill(factors, first_ref, second_ref)
+    for at in range(rank // STRIP):
+        rows = slice(at * STRIP, (at + 1) * STRIP)
+        fresh[rows, :] = fresh_rows(update_scale, weights_ref[matrix, rows, :], factors[rows, :], start_ref[...], scale_ref[0:1, :])
+        stores.append(pltpu.make_async_copy(fresh.at[rows], out_ref.at[matrix, rows], left.at[at]))
+        stores[-1].start()
+    for store in stores:
+        store.wait()
+
+
+def last_call(kernel, weights, inside, before, outs=None):
     rank, cols = weights.shape[1:]
     whole, outside = pl.BlockSpec(memory_space=pltpu.VMEM), pl.BlockSpec(memory_space=pl.ANY)
-    waiting_masks, waiting_block = waiting or (None, None)
-    extra = [] if waiting is None else [waiting_block]
     earlier = [] if before is None else [before]
-    block = jax.ShapeDtypeStruct((rank, cols), weights.dtype)
     staging = [pltpu.VMEM((rank, cols), jnp.bfloat16), pltpu.SemaphoreType.DMA((3,))]
     return pl.pallas_call(
-        functools.partial(last_kernel, update_scale, masks, waiting_masks, keeps),
-        out_shape=block if keeps else jax.ShapeDtypeStruct(weights.shape, weights.dtype),
-        in_specs=[whole] * (5 + len(extra)) + [outside] * len(earlier),
-        out_specs=whole if keeps else outside,
-        scratch_shapes=[pltpu.VMEM((rank, rank), jnp.bfloat16)] + ([] if keeps else staging),
-        input_output_aliases={5 + len(extra): 0} if earlier else {},
+        kernel,
+        out_shape=outs or jax.ShapeDtypeStruct(weights.shape, weights.dtype),
+        in_specs=[whole] * (1 + len(inside)) + [outside] * len(earlier),
+        out_specs=(whole,) * len(outs) if outs else outside,
+        scratch_shapes=[pltpu.VMEM((rank, rank), jnp.bfloat16)] + ([] if outs else staging),
+        input_output_aliases={1 + len(inside): 0} if earlier else {},
         compiler_params=pltpu.CompilerParams(vmem_limit_bytes=24 * 2**20),
         cost_estimate=pl.CostEstimate(flops=2 * rank * rank * cols, bytes_accessed=6 * rank * cols, transcendentals=0),
-    )(weights, momentum, peaks, *pair, *extra, *earlier)
+    )(weights, *inside, *earlier)
 
 
 def join_kernel(total_ref, arrived_ref, peaks_ref, peaks_arrived_ref, out_ref):
@@ -382,20 +414,32 @@
     halves = [mine] + [crossed(mine, "dp", mask) for mask in (1, 2, 3)]
     first, second, peaks = newton([piece for one in halves for piece in (one, swapped(one))], rank)
     update_scale = rms_factor * math.sqrt(max(rank, cols * fsdp))
-    last = functools.partial(last_product, update_scale)
     peaks, late_momentum = lax.optimization_barrier((peaks, momentum))
     new_momentum = decayed(late_momentum, gradient)
+
+    def last(masks, pair, before=None):
+        kernel = functools.partial(last_kernel, update_scale, masks)
+        return last_call(kernel, weights, [new_momentum, peaks, *pair], before)
+
     near = tuple(by_core(piece, "ctx", (1, 3)) for piece in (first, second))
-    new_weights = last((0, 0), weights, new_momentum, peaks, (first, second))
+    new_weights = last((0, 0), (first, second))
     near_first, new_weights = lax.optimization_barrier((near[0], new_weights))
     far = by_core(near_first, "ctx", (3, 1))
     cross = swapped(near[1]), swapped(near_first)
-    new_weights = last((1, 3), weights, new_momentum, peaks, (near_first, near[1]), new_weights)
+    new_weights = last((1, 3), (near_first, near[1]), new_weights)
     far, new_weights = lax.optimization_barrier((far, new_weights))
-    far = far, swapped(far)
-    waiting = last((3, 1), weights, new_momentum, peaks, cross, keeps=True)
-    far, waiting = lax.optimization_barrier((far, waiting))
-    new_weights = last((2, 2), weights, new_momentum, peaks, far, new_weights, ((3, 1), waiting))
+    far_too = swapped(far)
+    block = jax.ShapeDtypeStruct((rank, cols), jnp.bfloat16)
+    waiting = last_call(
+        functools.partial(waiting_kernel, update_scale, (3, 1), (2, 2)),
+        weights,
+        [new_momentum, peaks, *cross, far],
+        None,
+        (block, block, jax.ShapeDtypeStruct((8, cols), jnp.float32)),
+    )
+    far_too, waiting = lax.optimization_barrier((far_too, waiting))
+    closing = functools.partial(closing_kernel, update_scale, (2, 2), (3, 1))
+    new_weights = last_call(closing, weights, [far, far_too, *waiting], new_weights)
     return (new_weights, new_momentum)
 
 

time: 61.4 us -> 61.2 us (level)
  no operation moved by 1% of the time
where the time goes in v7:
time: 61.2 us; the launch traced here: 61.1 us
  starting transfers between devices  31.5 us (51%)
  Pallas kernels  18 us (29%)
  waiting for transfers between devices  8.96 us (15%)
  between operations  0.95 us (2%)
  other arithmetic  0.87 us (1%)
  local copies, waits for them, and re-layouts  0.83 us (1%)
    ppermute x13, starting transfers between devices, crossed(): lax.ppermute(value, axis, [(at, at ^ mask) for at in range(lax.axis_size(...  21.2 us
    pallas_call x1, Pallas kernels, newton(): pl.pallas_call(newton_kernel, out_shape=(piece, piece, jax.ShapeDtypeStru...  11.5 us
    ppermute x4, starting transfers between devices, along_z(): return lax.ppermute(value, 'fsdp', pairs)  7.27 us
    ppermute x13, waiting for transfers between devices, crossed(): lax.ppermute(value, axis, [(at, at ^ mask) for at in range(lax.axis_size(...  5.19 us
    pallas_call x4, Pallas kernels, last_call(): pl.pallas_call(kernel, out_shape=outs or jax.ShapeDtypeStruct(weights.sha...  4.86 us
    ppermute x3, starting transfers between devices, by_core(): return lax.ppermute(value, ('fsdp', axis), pairs)  3.06 us
    ppermute x4, waiting for transfers between devices, along_z(): return lax.ppermute(value, 'fsdp', pairs)  2.98 us
    pallas_call x1, Pallas kernels, partial_gram(): pl.pallas_call(partial_gram_kernel, out_shape=(shape, shape), in_specs=[p...  1.62 us
  transfers between devices with their start and end apart: 20, of which 9 were waited for; matrix products, arithmetic and copies ran while one was open for 2% of the time, Pallas kernels for 6%

profile of v7, /device:TPU:1, one launch (start us, length us, event | category | flops | bytes accessed | tf_op | source)
XLA Modules:
  0.0 61.1 jit_solution(6428701824502647730)
XLA Ops:
  0.6 1.6 %shard_map.68 = (f32[144,128]{1,0:T(8,128)S(1)}, f32[144,128]{1,0:T(8,128)S(1)}) custom-call(bf16[4,512,512]{2,1,0:T(8,128)(2,1)} %momentum_ref.1, bf16[4,512,512]{2,1,0:T(8,128)(2,1)} %gradient_ref.1), custom_call_target="tpu_custom_call" | custom-call | flops 37748736 | bytes 786432 | tf_op jit(solution)/shard_map/pallas_call | solution.py:84
  2.3 3.3 %collective-permute-start = (f32[144,128]{1,0:T(8,128)S(1)}, f32[144,128]{1,0:T(8,128)S(1)}, u32[]{:S(2)}, u32[]{:S(2)}) collective-permute-start(f32[144,128]{1,0:T(8,128)S(1)} %get-tuple-element.25), channel_id=1, source_target_pairs={{0,16},{16,0},{32,48},{48,32},{64,80},{80,64},{96,112},{112,96},{1... | collective-permute-start | bytes 221192 | tf_op jit(solution)/shard_map/ppermute | solution.py:369
  6.5 3.9 %collective-permute-start.3 = (f32[144,128]{1,0:T(8,128)S(1)}, f32[144,128]{1,0:T(8,128)S(1)}, u32[]{:S(2)}, u32[]{:S(2)}) collective-permute-start(f32[144,128]{1,0:T(8,128)S(1)} %add.15), channel_id=1, source_target_pairs={{0,96},{16,240},{32,64},{48,208},{64,32},{80,176},{96,0},{112,144}... | collective-permute-start | bytes 221192 | tf_op jit(solution)/shard_map/ppermute | solution.py:380
  11.0 1.1 %collective-permute-start.1 = (f32[144,128]{1,0:T(8,128)S(1)}, f32[144,128]{1,0:T(8,128)S(1)}, u32[]{:S(2)}, u32[]{:S(2)}) collective-permute-start(f32[144,128]{1,0:T(8,128)S(1)} %add.15), channel_id=1, source_target_pairs={{0,32},{16,48},{32,0},{48,16},{64,96},{80,112},{96,64},{112,80},{1... | collective-permute-start | bytes 221192 | tf_op jit(solution)/shard_map/ppermute | solution.py:380
  12.1 1.2 %collective-permute-start.4 = (f32[8,128]{1,0:T(8,128)S(1)}, f32[8,128]{1,0:T(8,128)S(1)}, u32[]{:S(2)}, u32[]{:S(2)}) collective-permute-start(f32[8,128]{1,0:T(8,128)S(1)} %broadcast_in_dim.37), channel_id=1, source_target_pairs={{0,1},{1,0},{2,3},{3,2},{4,5},{5,4},{6,7},{7,6},{8,9},{9,8},{10,11... | collective-permute-start | bytes 12296 | tf_op jit(solution)/shard_map/ppermute | solution.py:369
  13.3 1.5 %collective-permute-done.4 = f32[8,128]{1,0:T(8,128)S(1)} collective-permute-done((f32[8,128]{1,0:T(8,128)S(1)}, f32[8,128]{1,0:T(8,128)S(1)}, u32[]{:S(2)}, u32[]{:S(2)}) %collective-permute-start.4) | collective-permute-done | bytes 4128 | tf_op jit(solution)/shard_map/ppermute | solution.py:369
  14.9 3.0 %collective-permute-done.2 = f32[144,128]{1,0:T(8,128)S(1)} collective-permute-done((f32[144,128]{1,0:T(8,128)S(1)}, f32[144,128]{1,0:T(8,128)S(1)}, u32[]{:S(2)}, u32[]{:S(2)}) %collective-permute-start.2) | collective-permute-done | bytes 73760 | tf_op jit(solution)/shard_map/ppermute | solution.py:380
  17.9 1.7 %collective-permute-start.5 = (f32[144,128]{1,0:T(8,128)S(1)}, f32[144,128]{1,0:T(8,128)S(1)}, u32[]{:S(2)}, u32[]{:S(2)}) collective-permute-start(f32[144,128]{1,0:T(8,128)S(1)} %add_add_fusion.total_ref), channel_id=1, source_target_pairs={{0,224},{16,112},{32,192},{48,80},{64,160},{80,48},{96,128},{112,1... | collective-permute-start | bytes 221192 | tf_op jit(solution)/shard_map/ppermute | solution.py:380
  19.6 2.5 %collective-permute-start.6 = (f32[8,128]{1,0:T(8,128)S(1)}, f32[8,128]{1,0:T(8,128)S(1)}, u32[]{:S(2)}, u32[]{:S(2)}) collective-permute-start(f32[8,128]{1,0:T(8,128)S(1)} %max.3.peaks_ref), channel_id=1, source_target_pairs={{0,3},{1,2},{2,1},{3,0},{4,7},{5,6},{6,5},{7,4},{8,11},{9,10},{10,... | collective-permute-start | bytes 12296 | tf_op jit(solution)/shard_map/ppermute | solution.py:369
  22.0 1.2 %collective-permute-done.6.peaks_arrived_ref = f32[8,128]{1,0:T(8,128)S(1)} collective-permute-done((f32[8,128]{1,0:T(8,128)S(1)}, f32[8,128]{1,0:T(8,128)S(1)}, u32[]{:S(2)}, u32[]{:S(2)}) %collective-permute-start.6) | collective-permute-done | bytes 4128 | tf_op jit(solution)/shard_map/ppermute | solution.py:369
  23.3 2.8 %collective-permute-start.12 = (f32[152,128]{1,0:T(8,128)S(1)}, f32[152,128]{1,0:T(8,128)S(1)}, u32[]{:S(2)}, u32[]{:S(2)}) collective-permute-start(f32[152,128]{1,0:T(8,128)S(1)} %shard_map.69.refs_0_), channel_id=1, source_target_pairs={{0,12},{4,8},{8,4},{12,0},{1,13},{5,9},{9,5},{13,1},{2,14},{6,10},... | collective-permute-start | bytes 233480 | tf_op jit(solution)/shard_map/ppermute | solution.py:369
  26.8 2.1 %collective-permute-start.7 = (f32[152,128]{1,0:T(8,128)S(1)}, f32[152,128]{1,0:T(8,128)S(1)}, u32[]{:S(2)}, u32[]{:S(2)}) collective-permute-start(f32[152,128]{1,0:T(8,128)S(1)} %shard_map.69.refs_0_), channel_id=1, source_target_pairs={{0,16},{16,0},{32,48},{48,32},{64,80},{80,64},{96,112},{112,96},{1... | collective-permute-start | bytes 233480 | tf_op jit(solution)/shard_map/ppermute | solution.py:369
  28.9 1.7 %collective-permute-start.13 = (f32[152,128]{1,0:T(8,128)S(1)}, f32[152,128]{1,0:T(8,128)S(1)}, u32[]{:S(2)}, u32[]{:S(2)}) collective-permute-start(f32[152,128]{1,0:T(8,128)S(1)} %collective-permute-done.12.refs_6_), channel_id=1, source_target_pairs={{0,16},{16,0},{32,48},{48,32},{64,80},{80,64},{96,112},{112,96},{1... | collective-permute-start | bytes 233480 | tf_op jit(solution)/shard_map/ppermute | solution.py:369
  30.9 2.8 %collective-permute-start.11 = (f32[152,128]{1,0:T(8,128)S(1)}, f32[152,128]{1,0:T(8,128)S(1)}, u32[]{:S(2)}, u32[]{:S(2)}) collective-permute-start(f32[152,128]{1,0:T(8,128)S(1)} %collective-permute-done.10.refs_4_), channel_id=1, source_target_pairs={{0,16},{16,0},{32,48},{48,32},{64,80},{80,64},{96,112},{112,96},{1... | collective-permute-start | bytes 233480 | tf_op jit(solution)/shard_map/ppermute | solution.py:369
  33.7 0.9 %collective-permute-done.11.refs_5_ = f32[152,128]{1,0:T(8,128)S(1)} collective-permute-done((f32[152,128]{1,0:T(8,128)S(1)}, f32[152,128]{1,0:T(8,128)S(1)}, u32[]{:S(2)}, u32[]{:S(2)}) %collective-permute-start.11) | collective-permute-done | bytes 77856 | tf_op jit(solution)/shard_map/ppermute | solution.py:369
  35.0 11.5 %shard_map.70 = (bf16[656,128]{1,0:T(8,128)(2,1)S(1)}, bf16[656,128]{1,0:T(8,128)(2,1)S(1)}, f32[8,128]{1,0:T(8,128)S(1)}) custom-call(f32[152,128]{1,0:T(8,128)S(1)} %shard_map.69.refs_0_, f32[152,128]{1,0:T(8,128)S(1)} %collective-permute-done.7.refs_1_, f32[152,128]{1,0:T(8,128)S(1)} %collective-permute-done.8.refs_2_, ...), custom_call_target="tpu_custom_call" | custom-call | flops 13690208256 | bytes 1572864 | tf_op jit(solution)/shard_map/pallas_call | solution.py:229
  46.4 2.6 %collective-permute-start.14 = (bf16[656,128]{1,0:T(8,128)(2,1)S(1)}, bf16[656,128]{1,0:T(8,128)(2,1)S(1)}, u32[]{:S(2)}, u32[]{:S(2)}) collective-permute-start(bf16[656,128]{1,0:T(8,128)(2,1)S(1)} %get-tuple-element.30.first_ref), channel_id=1, source_target_pairs={{0,1},{1,0},{2,3},{3,2},{16,19},{17,18},{18,17},{19,16},{32,33},{3... | collective-permute-start | bytes 503816 | tf_op jit(solution)/shard_map/ppermute | solution.py:390
  50.6 1.5 %shard_map.71.refs_0_ = bf16[4,512,512]{2,1,0:T(8,128)(2,1)} custom-call(bf16[4,512,512]{2,1,0:T(8,128)(2,1)S(1)} %copy-done, bf16[4,512,512]{2,1,0:T(8,128)(2,1)S(1)} %add_convert_fusion.momentum_ref, f32[8,128]{1,0:T(8,128)S(1)} %get-tuple-element.33.peaks_ref, bf16[656,128]{1,0:T(8,128)(2,1)S(1)} %get-tuple-element.30.first_ref, ...), custom_call_target="tpu_custom_call" | custom-call | flops 268435456 | bytes 1572864 | tf_op jit(solution)/shard_map/pallas_call | solution.py:339
  52.4 2.4 %collective-permute-start.19 = (bf16[656,128]{1,0:T(8,128)(2,1)S(1)}, bf16[656,128]{1,0:T(8,128)(2,1)S(1)}, u32[]{:S(2)}, u32[]{:S(2)}) collective-permute-start(bf16[656,128]{1,0:T(8,128)(2,1)S(1)} %collective-permute-done.14.first_ref), channel_id=1, source_target_pairs={{0,16},{16,0},{32,48},{48,32},{64,80},{80,64},{96,112},{112,96},{1... | collective-permute-start | bytes 503816 | tf_op jit(solution)/shard_map/ppermute | solution.py:369
  54.8 1.3 %shard_map.72.before_ref = bf16[4,512,512]{2,1,0:T(8,128)(2,1)} custom-call(bf16[4,512,512]{2,1,0:T(8,128)(2,1)S(1)} %copy-done, bf16[4,512,512]{2,1,0:T(8,128)(2,1)S(1)} %add_convert_fusion.momentum_ref, f32[8,128]{1,0:T(8,128)S(1)} %get-tuple-element.33.peaks_ref, ...), custom_call_target="tpu_custom_call", output_to_operand_aliasing={{}: (5, {})} | custom-call | flops 268435456 | bytes 1572864 | tf_op jit(solution)/shard_map/pallas_call | solution.py:339
  56.1 0.8 %collective-permute-done.15.next_ref.first_ref = bf16[656,128]{1,0:T(8,128)(2,1)S(1)} collective-permute-done((bf16[656,128]{1,0:T(8,128)(2,1)S(1)}, bf16[656,128]{1,0:T(8,128)(2,1)S(1)}, u32[]{:S(2)}, u32[]{:S(2)}) %collective-permute-start.15) | collective-permute-done | bytes 167968 | tf_op jit(solution)/shard_map/ppermute | solution.py:390
  56.9 1.7 %collective-permute-start.17 = (bf16[656,128]{1,0:T(8,128)(2,1)S(1)}, bf16[656,128]{1,0:T(8,128)(2,1)S(1)}, u32[]{:S(2)}, u32[]{:S(2)}) collective-permute-start(bf16[656,128]{1,0:T(8,128)(2,1)S(1)} %collective-permute-done.15.next_ref.first_ref), channel_id=1, source_target_pairs={{0,16},{16,0},{32,48},{48,32},{64,80},{80,64},{96,112},{112,96},{1... | collective-permute-start | bytes 503816 | tf_op jit(solution)/shard_map/ppermute | solution.py:369
  58.6 0.8 %shard_map.73 = (bf16[512,512]{1,0:T(8,128)(2,1)S(1)}, bf16[512,512]{1,0:T(8,128)(2,1)S(1)}, f32[8,512]{1,0:T(8,128)S(1)}) custom-call(bf16[4,512,512]{2,1,0:T(8,128)(2,1)S(1)} %copy-done, bf16[4,512,512]{2,1,0:T(8,128)(2,1)S(1)} %add_convert_fusion.momentum_ref, f32[8,128]{1,0:T(8,128)S(1)} %get-tuple-element.33.peaks_ref, ...), custom_call_target="tpu_custom_call" | custom-call | flops 268435456 | bytes 1572864 | tf_op jit(solution)/shard_map/pallas_call | solution.py:339
  59.6 1.3 %shard_map.74 = bf16[4,512,512]{2,1,0:T(8,128)(2,1)} custom-call(bf16[4,512,512]{2,1,0:T(8,128)(2,1)S(1)} %copy-done, bf16[656,128]{1,0:T(8,128)(2,1)S(1)} %collective-permute-done.15.next_ref.first_ref, bf16[656,128]{1,0:T(8,128)(2,1)S(1)} %collective-permute-done.17.second_ref, ...), custom_call_target="tpu_custom_call", output_to_operand_aliasing={{}: (6, {})} | custom-call | flops 268435456 | bytes 1572864 | tf_op jit(solution)/shard_map/pallas_call | solution.py:339
  (43 shorter events, 5.0 us)
Async XLA Ops:
  0.6 5.0 %copy-start.4 = (f32[1,1,61,32]{2,3,1,0:T(8,128)S(1)}, f32[1,1,61,32]{2,3,1,0:T(8,128)}, u32[]{:S(2)}) copy-start(f32[1,1,61,32]{2,3,1,0:T(8,128)} %param.8) | copy-start | bytes 23428
  2.3 4.2 %collective-permute-start = (f32[144,128]{1,0:T(8,128)S(1)}, f32[144,128]{1,0:T(8,128)S(1)}, u32[]{:S(2)}, u32[]{:S(2)}) collective-permute-start(f32[144,128]{1,0:T(8,128)S(1)} %get-tuple-element.25), channel_id=1, source_target_pairs={{0,16},{16,0},{32,48},{48,32},{64,80},{80,64},{96,112},{112,96},{1... | collective-permute-start | bytes 221192 | tf_op jit(solution)/shard_map/ppermute | solution.py:369
  6.5 8.3 %collective-permute-start.3 = (f32[144,128]{1,0:T(8,128)S(1)}, f32[144,128]{1,0:T(8,128)S(1)}, u32[]{:S(2)}, u32[]{:S(2)}) collective-permute-start(f32[144,128]{1,0:T(8,128)S(1)} %add.15), channel_id=1, source_target_pairs={{0,96},{16,240},{32,64},{48,208},{64,32},{80,176},{96,0},{112,144}... | collective-permute-start | bytes 221192 | tf_op jit(solution)/shard_map/ppermute | solution.py:380
  10.5 7.4 %collective-permute-start.2 = (f32[144,128]{1,0:T(8,128)S(1)}, f32[144,128]{1,0:T(8,128)S(1)}, u32[]{:S(2)}, u32[]{:S(2)}) collective-permute-start(f32[144,128]{1,0:T(8,128)S(1)} %add.15), channel_id=1, source_target_pairs={{0,64},{16,208},{32,96},{48,240},{64,0},{80,144},{96,32},{112,176}... | collective-permute-start | bytes 221192 | tf_op jit(solution)/shard_map/ppermute | solution.py:380
  11.0 6.8 %collective-permute-start.1 = (f32[144,128]{1,0:T(8,128)S(1)}, f32[144,128]{1,0:T(8,128)S(1)}, u32[]{:S(2)}, u32[]{:S(2)}) collective-permute-start(f32[144,128]{1,0:T(8,128)S(1)} %add.15), channel_id=1, source_target_pairs={{0,32},{16,48},{32,0},{48,16},{64,96},{80,112},{96,64},{112,80},{1... | collective-permute-start | bytes 221192 | tf_op jit(solution)/shard_map/ppermute | solution.py:380
  12.1 2.8 %collective-permute-start.4 = (f32[8,128]{1,0:T(8,128)S(1)}, f32[8,128]{1,0:T(8,128)S(1)}, u32[]{:S(2)}, u32[]{:S(2)}) collective-permute-start(f32[8,128]{1,0:T(8,128)S(1)} %broadcast_in_dim.37), channel_id=1, source_target_pairs={{0,1},{1,0},{2,3},{3,2},{4,5},{5,4},{6,7},{7,6},{8,9},{9,8},{10,11... | collective-permute-start | bytes 12296 | tf_op jit(solution)/shard_map/ppermute | solution.py:369
  17.9 5.4 %collective-permute-start.5 = (f32[144,128]{1,0:T(8,128)S(1)}, f32[144,128]{1,0:T(8,128)S(1)}, u32[]{:S(2)}, u32[]{:S(2)}) collective-permute-start(f32[144,128]{1,0:T(8,128)S(1)} %add_add_fusion.total_ref), channel_id=1, source_target_pairs={{0,224},{16,112},{32,192},{48,80},{64,160},{80,48},{96,128},{112,1... | collective-permute-start | bytes 221192 | tf_op jit(solution)/shard_map/ppermute | solution.py:380
  19.6 3.7 %collective-permute-start.6 = (f32[8,128]{1,0:T(8,128)S(1)}, f32[8,128]{1,0:T(8,128)S(1)}, u32[]{:S(2)}, u32[]{:S(2)}) collective-permute-start(f32[8,128]{1,0:T(8,128)S(1)} %max.3.peaks_ref), channel_id=1, source_target_pairs={{0,3},{1,2},{2,1},{3,0},{4,7},{5,6},{6,5},{7,4},{8,11},{9,10},{10,... | collective-permute-start | bytes 12296 | tf_op jit(solution)/shard_map/ppermute | solution.py:369
  23.3 25.9 %copy-start.2 = (bf16[4,512,512]{2,1,0:T(8,128)(2,1)S(1)}, bf16[4,512,512]{2,1,0:T(8,128)(2,1)}, u32[]{:S(2)}) copy-start(bf16[4,512,512]{2,1,0:T(8,128)(2,1)} %momentum_ref.1) | copy-start | bytes 6291460
  23.3 25.9 %copy-start.3 = (bf16[4,512,512]{2,1,0:T(8,128)(2,1)S(1)}, bf16[4,512,512]{2,1,0:T(8,128)(2,1)}, u32[]{:S(2)}) copy-start(bf16[4,512,512]{2,1,0:T(8,128)(2,1)} %gradient_ref.1) | copy-start | bytes 6291460
  23.3 5.6 %collective-permute-start.12 = (f32[152,128]{1,0:T(8,128)S(1)}, f32[152,128]{1,0:T(8,128)S(1)}, u32[]{:S(2)}, u32[]{:S(2)}) collective-permute-start(f32[152,128]{1,0:T(8,128)S(1)} %shard_map.69.refs_0_), channel_id=1, source_target_pairs={{0,12},{4,8},{8,4},{12,0},{1,13},{5,9},{9,5},{13,1},{2,14},{6,10},... | collective-permute-start | bytes 233480 | tf_op jit(solution)/shard_map/ppermute | solution.py:369
  26.1 4.8 %collective-permute-start.10 = (f32[152,128]{1,0:T(8,128)S(1)}, f32[152,128]{1,0:T(8,128)S(1)}, u32[]{:S(2)}, u32[]{:S(2)}) collective-permute-start(f32[152,128]{1,0:T(8,128)S(1)} %shard_map.69.refs_0_), channel_id=1, source_target_pairs={{0,8},{4,12},{8,0},{12,4},{1,9},{5,13},{9,1},{13,5},{2,10},{6,14},... | collective-permute-start | bytes 233480 | tf_op jit(solution)/shard_map/ppermute | solution.py:369
  26.4 7.2 %collective-permute-start.8 = (f32[152,128]{1,0:T(8,128)S(1)}, f32[152,128]{1,0:T(8,128)S(1)}, u32[]{:S(2)}, u32[]{:S(2)}) collective-permute-start(f32[152,128]{1,0:T(8,128)S(1)} %shard_map.69.refs_0_), channel_id=1, source_target_pairs={{0,4},{4,0},{8,12},{12,8},{1,5},{5,1},{9,13},{13,9},{2,6},{6,2},{1... | collective-permute-start | bytes 233480 | tf_op jit(solution)/shard_map/ppermute | solution.py:369
  26.8 6.9 %collective-permute-start.7 = (f32[152,128]{1,0:T(8,128)S(1)}, f32[152,128]{1,0:T(8,128)S(1)}, u32[]{:S(2)}, u32[]{:S(2)}) collective-permute-start(f32[152,128]{1,0:T(8,128)S(1)} %shard_map.69.refs_0_), channel_id=1, source_target_pairs={{0,16},{16,0},{32,48},{48,32},{64,80},{80,64},{96,112},{112,96},{1... | collective-permute-start | bytes 233480 | tf_op jit(solution)/shard_map/ppermute | solution.py:369
  28.9 4.8 %collective-permute-start.13 = (f32[152,128]{1,0:T(8,128)S(1)}, f32[152,128]{1,0:T(8,128)S(1)}, u32[]{:S(2)}, u32[]{:S(2)}) collective-permute-start(f32[152,128]{1,0:T(8,128)S(1)} %collective-permute-done.12.refs_6_), channel_id=1, source_target_pairs={{0,16},{16,0},{32,48},{48,32},{64,80},{80,64},{96,112},{112,96},{1... | collective-permute-start | bytes 233480 | tf_op jit(solution)/shard_map/ppermute | solution.py:369
  30.9 3.8 %collective-permute-start.11 = (f32[152,128]{1,0:T(8,128)S(1)}, f32[152,128]{1,0:T(8,128)S(1)}, u32[]{:S(2)}, u32[]{:S(2)}) collective-permute-start(f32[152,128]{1,0:T(8,128)S(1)} %collective-permute-done.10.refs_4_), channel_id=1, source_target_pairs={{0,16},{16,0},{32,48},{48,32},{64,80},{80,64},{96,112},{112,96},{1... | collective-permute-start | bytes 233480 | tf_op jit(solution)/shard_map/ppermute | solution.py:369
  33.7 1.3 %collective-permute-start.9 = (f32[152,128]{1,0:T(8,128)S(1)}, f32[152,128]{1,0:T(8,128)S(1)}, u32[]{:S(2)}, u32[]{:S(2)}) collective-permute-start(f32[152,128]{1,0:T(8,128)S(1)} %collective-permute-done.8.refs_2_), channel_id=1, source_target_pairs={{0,16},{16,0},{32,48},{48,32},{64,80},{80,64},{96,112},{112,96},{1... | collective-permute-start | bytes 233480 | tf_op jit(solution)/shard_map/ppermute | solution.py:369
  46.4 5.7 %collective-permute-start.14 = (bf16[656,128]{1,0:T(8,128)(2,1)S(1)}, bf16[656,128]{1,0:T(8,128)(2,1)S(1)}, u32[]{:S(2)}, u32[]{:S(2)}) collective-permute-start(bf16[656,128]{1,0:T(8,128)(2,1)S(1)} %get-tuple-element.30.first_ref), channel_id=1, source_target_pairs={{0,1},{1,0},{2,3},{3,2},{16,19},{17,18},{18,17},{19,16},{32,33},{3... | collective-permute-start | bytes 503816 | tf_op jit(solution)/shard_map/ppermute | solution.py:390
  49.0 5.8 %collective-permute-start.16 = (bf16[656,128]{1,0:T(8,128)(2,1)S(1)}, bf16[656,128]{1,0:T(8,128)(2,1)S(1)}, u32[]{:S(2)}, u32[]{:S(2)}) collective-permute-start(bf16[656,128]{1,0:T(8,128)(2,1)S(1)} %get-tuple-element.34.second_ref), channel_id=1, source_target_pairs={{0,1},{1,0},{2,3},{3,2},{16,19},{17,18},{18,17},{19,16},{32,33},{3... | collective-permute-start | bytes 503816 | tf_op jit(solution)/shard_map/ppermute | solution.py:390
  50.6 8.0 %copy-start.1 = (bf16[4,512,512]{2,1,0:T(8,128)(2,1)}, bf16[4,512,512]{2,1,0:T(8,128)(2,1)S(1)}, u32[]{:S(2)}) copy-start(bf16[4,512,512]{2,1,0:T(8,128)(2,1)S(1)} %add_convert_fusion.momentum_ref) | copy-start | bytes 6291460
  52.1 4.8 %collective-permute-start.15 = (bf16[656,128]{1,0:T(8,128)(2,1)S(1)}, bf16[656,128]{1,0:T(8,128)(2,1)S(1)}, u32[]{:S(2)}, u32[]{:S(2)}) collective-permute-start(bf16[656,128]{1,0:T(8,128)(2,1)S(1)} %collective-permute-done.14.first_ref), channel_id=1, source_target_pairs={{0,3},{1,2},{2,1},{3,0},{16,17},{17,16},{18,19},{19,18},{32,35},{3... | collective-permute-start | bytes 503816 | tf_op jit(solution)/shard_map/ppermute | solution.py:390
  52.4 6.2 %collective-permute-start.19 = (bf16[656,128]{1,0:T(8,128)(2,1)S(1)}, bf16[656,128]{1,0:T(8,128)(2,1)S(1)}, u32[]{:S(2)}, u32[]{:S(2)}) collective-permute-start(bf16[656,128]{1,0:T(8,128)(2,1)S(1)} %collective-permute-done.14.first_ref), channel_id=1, source_target_pairs={{0,16},{16,0},{32,48},{48,32},{64,80},{80,64},{96,112},{112,96},{1... | collective-permute-start | bytes 503816 | tf_op jit(solution)/shard_map/ppermute | solution.py:369
  54.8 3.8 %collective-permute-start.18 = (bf16[656,128]{1,0:T(8,128)(2,1)S(1)}, bf16[656,128]{1,0:T(8,128)(2,1)S(1)}, u32[]{:S(2)}, u32[]{:S(2)}) collective-permute-start(bf16[656,128]{1,0:T(8,128)(2,1)S(1)} %collective-permute-done.16.second_ref), channel_id=1, source_target_pairs={{0,16},{16,0},{32,48},{48,32},{64,80},{80,64},{96,112},{112,96},{1... | collective-permute-start | bytes 503816 | tf_op jit(solution)/shard_map/ppermute | solution.py:369
  56.9 2.7 %collective-permute-start.17 = (bf16[656,128]{1,0:T(8,128)(2,1)S(1)}, bf16[656,128]{1,0:T(8,128)(2,1)S(1)}, u32[]{:S(2)}, u32[]{:S(2)}) collective-permute-start(bf16[656,128]{1,0:T(8,128)(2,1)S(1)} %collective-permute-done.15.next_ref.first_ref), channel_id=1, source_target_pairs={{0,16},{16,0},{32,48},{48,32},{64,80},{80,64},{96,112},{112,96},{1... | collective-permute-start | bytes 503816 | tf_op jit(solution)/shard_map/ppermute | solution.py:369
  (2 other events, 6.6 us)

commit v8 on v7

--- a/solution.py
+++ b/solution.py
@@ -29,6 +29,7 @@
 HALF = 640
 END = 16
 STRIP = 256
+TURNS = (0, 1, 3, 2)
 KEPT = [[(0, 0), (0, 1), (0, 2), (0, 3), (1, 1)], [(1, 2), (1, 3), (2, 2), (2, 3), (3, 3)]]
 
 
@@ -116,7 +117,7 @@
     rank = a_now.shape[0]
     mid = rank // 2
     dp_at, core = lax.axis_index("dp"), lax.rem(lax.axis_index("fsdp"), 2)
-    for turn, pair in enumerate(parts):
+    for turn, pair in zip(TURNS, parts):
         for side, piece in enumerate(pair):
             half = core + side - 2 * core * side
             stacks[dp_at ^ turn, pl.ds(aligned(half, PART), PART), :] = piece[0:PART, :]
@@ -411,7 +412,7 @@
     peaks = jnp.maximum(peaks, crossed(peaks, "ctx", 1))
     total, peaks = lax.optimization_barrier((total, peaks))
     mine = join(total, along_z(total, 7), peaks, crossed(peaks, "ctx", 3))
-    halves = [mine] + [crossed(mine, "dp", mask) for mask in (1, 2, 3)]
+    halves = [mine] + [crossed(mine, "dp", mask) for mask in TURNS[1:]]
     first, second, peaks = newton([piece for one in halves for piece in (one, swapped(one))], rank)
     update_scale = rms_factor * math.sqrt(max(rank, cols * fsdp))
     peaks, late_momentum = lax.optimization_barrier((peaks, momentum))

time: 61.2 us -> 61.1 us (level)
  no operation moved by 1% of the time
where the time goes in v8:
time: 61.1 us; the launch traced here: 61 us
  starting transfers between devices  31.5 us (52%)
  Pallas kernels  18 us (29%)
  waiting for transfers between devices  8.81 us (14%)
  between operations  0.95 us (2%)
  other arithmetic  0.87 us (1%)
  local copies, waits for them, and re-layouts  0.83 us (1%)
    ppermute x13, starting transfers between devices, crossed(): lax.ppermute(value, axis, [(at, at ^ mask) for at in range(lax.axis_size(...  21.2 us
    pallas_call x1, Pallas kernels, newton(): pl.pallas_call(newton_kernel, out_shape=(piece, piece, jax.ShapeDtypeStru...  11.5 us
    ppermute x4, starting transfers between devices, along_z(): return lax.ppermute(value, 'fsdp', pairs)  7.27 us
    ppermute x13, waiting for transfers between devices, crossed(): lax.ppermute(value, axis, [(at, at ^ mask) for at in range(lax.axis_size(...  5.04 us
    pallas_call x4, Pallas kernels, last_call(): pl.pallas_call(kernel, out_shape=outs or jax.ShapeDtypeStruct(weights.sha...  4.87 us
    ppermute x3, starting transfers between devices, by_core(): return lax.ppermute(value, ('fsdp', axis), pairs)  3.06 us
    ppermute x4, waiting for transfers between devices, along_z(): return lax.ppermute(value, 'fsdp', pairs)  2.98 us
    pallas_call x1, Pallas kernels, partial_gram(): pl.pallas_call(partial_gram_kernel, out_shape=(shape, shape), in_specs=[p...  1.62 us
  transfers between devices with their start and end apart: 20, of which 9 were waited for; matrix products, arithmetic and copies ran while one was open for 2% of the time, Pallas kernels for 6%

profile of v8, /device:TPU:1, one launch (start us, length us, event | category | flops | bytes accessed | tf_op | source)
XLA Modules:
  0.0 61.0 jit_solution(17782307587506780855)
XLA Ops:
  0.6 1.6 %shard_map.68 = (f32[144,128]{1,0:T(8,128)S(1)}, f32[144,128]{1,0:T(8,128)S(1)}) custom-call(bf16[4,512,512]{2,1,0:T(8,128)(2,1)} %momentum_ref.1, bf16[4,512,512]{2,1,0:T(8,128)(2,1)} %gradient_ref.1), custom_call_target="tpu_custom_call" | custom-call | flops 37748736 | bytes 786432 | tf_op jit(solution)/shard_map/pallas_call | solution.py:85
  2.3 3.3 %collective-permute-start = (f32[144,128]{1,0:T(8,128)S(1)}, f32[144,128]{1,0:T(8,128)S(1)}, u32[]{:S(2)}, u32[]{:S(2)}) collective-permute-start(f32[144,128]{1,0:T(8,128)S(1)} %get-tuple-element.25), channel_id=1, source_target_pairs={{0,16},{16,0},{32,48},{48,32},{64,80},{80,64},{96,112},{112,96},{1... | collective-permute-start | bytes 221192 | tf_op jit(solution)/shard_map/ppermute | solution.py:370
  6.5 3.9 %collective-permute-start.3 = (f32[144,128]{1,0:T(8,128)S(1)}, f32[144,128]{1,0:T(8,128)S(1)}, u32[]{:S(2)}, u32[]{:S(2)}) collective-permute-start(f32[144,128]{1,0:T(8,128)S(1)} %add.15), channel_id=1, source_target_pairs={{0,96},{16,240},{32,64},{48,208},{64,32},{80,176},{96,0},{112,144}... | collective-permute-start | bytes 221192 | tf_op jit(solution)/shard_map/ppermute | solution.py:381
  11.0 1.1 %collective-permute-start.1 = (f32[144,128]{1,0:T(8,128)S(1)}, f32[144,128]{1,0:T(8,128)S(1)}, u32[]{:S(2)}, u32[]{:S(2)}) collective-permute-start(f32[144,128]{1,0:T(8,128)S(1)} %add.15), channel_id=1, source_target_pairs={{0,32},{16,48},{32,0},{48,16},{64,96},{80,112},{96,64},{112,80},{1... | collective-permute-start | bytes 221192 | tf_op jit(solution)/shard_map/ppermute | solution.py:381
  12.1 1.2 %collective-permute-start.4 = (f32[8,128]{1,0:T(8,128)S(1)}, f32[8,128]{1,0:T(8,128)S(1)}, u32[]{:S(2)}, u32[]{:S(2)}) collective-permute-start(f32[8,128]{1,0:T(8,128)S(1)} %broadcast_in_dim.37), channel_id=1, source_target_pairs={{0,1},{1,0},{2,3},{3,2},{4,5},{5,4},{6,7},{7,6},{8,9},{9,8},{10,11... | collective-permute-start | bytes 12296 | tf_op jit(solution)/shard_map/ppermute | solution.py:370
  13.3 1.5 %collective-permute-done.4 = f32[8,128]{1,0:T(8,128)S(1)} collective-permute-done((f32[8,128]{1,0:T(8,128)S(1)}, f32[8,128]{1,0:T(8,128)S(1)}, u32[]{:S(2)}, u32[]{:S(2)}) %collective-permute-start.4) | collective-permute-done | bytes 4128 | tf_op jit(solution)/shard_map/ppermute | solution.py:370
  14.9 3.0 %collective-permute-done.2 = f32[144,128]{1,0:T(8,128)S(1)} collective-permute-done((f32[144,128]{1,0:T(8,128)S(1)}, f32[144,128]{1,0:T(8,128)S(1)}, u32[]{:S(2)}, u32[]{:S(2)}) %collective-permute-start.2) | collective-permute-done | bytes 73760 | tf_op jit(solution)/shard_map/ppermute | solution.py:381
  17.9 1.7 %collective-permute-start.5 = (f32[144,128]{1,0:T(8,128)S(1)}, f32[144,128]{1,0:T(8,128)S(1)}, u32[]{:S(2)}, u32[]{:S(2)}) collective-permute-start(f32[144,128]{1,0:T(8,128)S(1)} %add_add_fusion.total_ref), channel_id=1, source_target_pairs={{0,224},{16,112},{32,192},{48,80},{64,160},{80,48},{96,128},{112,1... | collective-permute-start | bytes 221192 | tf_op jit(solution)/shard_map/ppermute | solution.py:381
  19.6 2.5 %collective-permute-start.6 = (f32[8,128]{1,0:T(8,128)S(1)}, f32[8,128]{1,0:T(8,128)S(1)}, u32[]{:S(2)}, u32[]{:S(2)}) collective-permute-start(f32[8,128]{1,0:T(8,128)S(1)} %max.3.peaks_ref), channel_id=1, source_target_pairs={{0,3},{1,2},{2,1},{3,0},{4,7},{5,6},{6,5},{7,4},{8,11},{9,10},{10,... | collective-permute-start | bytes 12296 | tf_op jit(solution)/shard_map/ppermute | solution.py:370
  22.0 1.2 %collective-permute-done.6.peaks_arrived_ref = f32[8,128]{1,0:T(8,128)S(1)} collective-permute-done((f32[8,128]{1,0:T(8,128)S(1)}, f32[8,128]{1,0:T(8,128)S(1)}, u32[]{:S(2)}, u32[]{:S(2)}) %collective-permute-start.6) | collective-permute-done | bytes 4128 | tf_op jit(solution)/shard_map/ppermute | solution.py:370
  23.3 3.0 %collective-permute-start.12 = (f32[152,128]{1,0:T(8,128)S(1)}, f32[152,128]{1,0:T(8,128)S(1)}, u32[]{:S(2)}, u32[]{:S(2)}) collective-permute-start(f32[152,128]{1,0:T(8,128)S(1)} %shard_map.69.refs_0_), channel_id=1, source_target_pairs={{0,8},{4,12},{8,0},{12,4},{1,9},{5,13},{9,1},{13,5},{2,10},{6,14},... | collective-permute-start | bytes 233480 | tf_op jit(solution)/shard_map/ppermute | solution.py:370
  26.3 0.8 %collective-permute-start.10 = (f32[152,128]{1,0:T(8,128)S(1)}, f32[152,128]{1,0:T(8,128)S(1)}, u32[]{:S(2)}, u32[]{:S(2)}) collective-permute-start(f32[152,128]{1,0:T(8,128)S(1)} %shard_map.69.refs_0_), channel_id=1, source_target_pairs={{0,12},{4,8},{8,4},{12,0},{1,13},{5,9},{9,5},{13,1},{2,14},{6,10},... | collective-permute-start | bytes 233480 | tf_op jit(solution)/shard_map/ppermute | solution.py:370
  27.1 2.0 %collective-permute-start.7 = (f32[152,128]{1,0:T(8,128)S(1)}, f32[152,128]{1,0:T(8,128)S(1)}, u32[]{:S(2)}, u32[]{:S(2)}) collective-permute-start(f32[152,128]{1,0:T(8,128)S(1)} %shard_map.69.refs_0_), channel_id=1, source_target_pairs={{0,16},{16,0},{32,48},{48,32},{64,80},{80,64},{96,112},{112,96},{1... | collective-permute-start | bytes 233480 | tf_op jit(solution)/shard_map/ppermute | solution.py:370
  29.0 1.6 %collective-permute-start.13 = (f32[152,128]{1,0:T(8,128)S(1)}, f32[152,128]{1,0:T(8,128)S(1)}, u32[]{:S(2)}, u32[]{:S(2)}) collective-permute-start(f32[152,128]{1,0:T(8,128)S(1)} %collective-permute-done.12.refs_6_), channel_id=1, source_target_pairs={{0,16},{16,0},{32,48},{48,32},{64,80},{80,64},{96,112},{112,96},{1... | collective-permute-start | bytes 233480 | tf_op jit(solution)/shard_map/ppermute | solution.py:370
  30.8 2.8 %collective-permute-start.11 = (f32[152,128]{1,0:T(8,128)S(1)}, f32[152,128]{1,0:T(8,128)S(1)}, u32[]{:S(2)}, u32[]{:S(2)}) collective-permute-start(f32[152,128]{1,0:T(8,128)S(1)} %collective-permute-done.10.refs_4_), channel_id=1, source_target_pairs={{0,16},{16,0},{32,48},{48,32},{64,80},{80,64},{96,112},{112,96},{1... | collective-permute-start | bytes 233480 | tf_op jit(solution)/shard_map/ppermute | solution.py:370
  33.6 0.9 %collective-permute-done.11.refs_5_ = f32[152,128]{1,0:T(8,128)S(1)} collective-permute-done((f32[152,128]{1,0:T(8,128)S(1)}, f32[152,128]{1,0:T(8,128)S(1)}, u32[]{:S(2)}, u32[]{:S(2)}) %collective-permute-start.11) | collective-permute-done | bytes 77856 | tf_op jit(solution)/shard_map/ppermute | solution.py:370
  34.9 11.5 %shard_map.70 = (bf16[656,128]{1,0:T(8,128)(2,1)S(1)}, bf16[656,128]{1,0:T(8,128)(2,1)S(1)}, f32[8,128]{1,0:T(8,128)S(1)}) custom-call(f32[152,128]{1,0:T(8,128)S(1)} %shard_map.69.refs_0_, f32[152,128]{1,0:T(8,128)S(1)} %collective-permute-done.7.refs_1_, f32[152,128]{1,0:T(8,128)S(1)} %collective-permute-done.8.refs_2_, ...), custom_call_target="tpu_custom_call" | custom-call | flops 13690208256 | bytes 1572864 | tf_op jit(solution)/shard_map/pallas_call | solution.py:230
  46.3 2.6 %collective-permute-start.14 = (bf16[656,128]{1,0:T(8,128)(2,1)S(1)}, bf16[656,128]{1,0:T(8,128)(2,1)S(1)}, u32[]{:S(2)}, u32[]{:S(2)}) collective-permute-start(bf16[656,128]{1,0:T(8,128)(2,1)S(1)} %get-tuple-element.30.first_ref), channel_id=1, source_target_pairs={{0,1},{1,0},{2,3},{3,2},{16,19},{17,18},{18,17},{19,16},{32,33},{3... | collective-permute-start | bytes 503816 | tf_op jit(solution)/shard_map/ppermute | solution.py:391
  50.5 1.5 %shard_map.71.refs_0_ = bf16[4,512,512]{2,1,0:T(8,128)(2,1)} custom-call(bf16[4,512,512]{2,1,0:T(8,128)(2,1)S(1)} %copy-done, bf16[4,512,512]{2,1,0:T(8,128)(2,1)S(1)} %add_convert_fusion.momentum_ref, f32[8,128]{1,0:T(8,128)S(1)} %get-tuple-element.33.peaks_ref, bf16[656,128]{1,0:T(8,128)(2,1)S(1)} %get-tuple-element.30.first_ref, ...), custom_call_target="tpu_custom_call" | custom-call | flops 268435456 | bytes 1572864 | tf_op jit(solution)/shard_map/pallas_call | solution.py:340
  52.3 2.4 %collective-permute-start.19 = (bf16[656,128]{1,0:T(8,128)(2,1)S(1)}, bf16[656,128]{1,0:T(8,128)(2,1)S(1)}, u32[]{:S(2)}, u32[]{:S(2)}) collective-permute-start(bf16[656,128]{1,0:T(8,128)(2,1)S(1)} %collective-permute-done.14.first_ref), channel_id=1, source_target_pairs={{0,16},{16,0},{32,48},{48,32},{64,80},{80,64},{96,112},{112,96},{1... | collective-permute-start | bytes 503816 | tf_op jit(solution)/shard_map/ppermute | solution.py:370
  54.7 1.3 %shard_map.72.before_ref = bf16[4,512,512]{2,1,0:T(8,128)(2,1)} custom-call(bf16[4,512,512]{2,1,0:T(8,128)(2,1)S(1)} %copy-done, bf16[4,512,512]{2,1,0:T(8,128)(2,1)S(1)} %add_convert_fusion.momentum_ref, f32[8,128]{1,0:T(8,128)S(1)} %get-tuple-element.33.peaks_ref, ...), custom_call_target="tpu_custom_call", output_to_operand_aliasing={{}: (5, {})} | custom-call | flops 268435456 | bytes 1572864 | tf_op jit(solution)/shard_map/pallas_call | solution.py:340
  56.0 0.8 %collective-permute-done.15.next_ref.first_ref = bf16[656,128]{1,0:T(8,128)(2,1)S(1)} collective-permute-done((bf16[656,128]{1,0:T(8,128)(2,1)S(1)}, bf16[656,128]{1,0:T(8,128)(2,1)S(1)}, u32[]{:S(2)}, u32[]{:S(2)}) %collective-permute-start.15) | collective-permute-done | bytes 167968 | tf_op jit(solution)/shard_map/ppermute | solution.py:391
  56.8 1.7 %collective-permute-start.17 = (bf16[656,128]{1,0:T(8,128)(2,1)S(1)}, bf16[656,128]{1,0:T(8,128)(2,1)S(1)}, u32[]{:S(2)}, u32[]{:S(2)}) collective-permute-start(bf16[656,128]{1,0:T(8,128)(2,1)S(1)} %collective-permute-done.15.next_ref.first_ref), channel_id=1, source_target_pairs={{0,16},{16,0},{32,48},{48,32},{64,80},{80,64},{96,112},{112,96},{1... | collective-permute-start | bytes 503816 | tf_op jit(solution)/shard_map/ppermute | solution.py:370
  59.5 1.3 %shard_map.74 = bf16[4,512,512]{2,1,0:T(8,128)(2,1)} custom-call(bf16[4,512,512]{2,1,0:T(8,128)(2,1)S(1)} %copy-done, bf16[656,128]{1,0:T(8,128)(2,1)S(1)} %collective-permute-done.15.next_ref.first_ref, bf16[656,128]{1,0:T(8,128)(2,1)S(1)} %collective-permute-done.17.second_ref, ...), custom_call_target="tpu_custom_call", output_to_operand_aliasing={{}: (6, {})} | custom-call | flops 268435456 | bytes 1572864 | tf_op jit(solution)/shard_map/pallas_call | solution.py:340
  (43 shorter events, 5.0 us)
Async XLA Ops:
  0.6 5.0 %copy-start.4 = (f32[1,1,61,32]{2,3,1,0:T(8,128)S(1)}, f32[1,1,61,32]{2,3,1,0:T(8,128)}, u32[]{:S(2)}) copy-start(f32[1,1,61,32]{2,3,1,0:T(8,128)} %param.8) | copy-start | bytes 23428
  2.3 4.2 %collective-permute-start = (f32[144,128]{1,0:T(8,128)S(1)}, f32[144,128]{1,0:T(8,128)S(1)}, u32[]{:S(2)}, u32[]{:S(2)}) collective-permute-start(f32[144,128]{1,0:T(8,128)S(1)} %get-tuple-element.25), channel_id=1, source_target_pairs={{0,16},{16,0},{32,48},{48,32},{64,80},{80,64},{96,112},{112,96},{1... | collective-permute-start | bytes 221192 | tf_op jit(solution)/shard_map/ppermute | solution.py:370
  6.5 8.3 %collective-permute-start.3 = (f32[144,128]{1,0:T(8,128)S(1)}, f32[144,128]{1,0:T(8,128)S(1)}, u32[]{:S(2)}, u32[]{:S(2)}) collective-permute-start(f32[144,128]{1,0:T(8,128)S(1)} %add.15), channel_id=1, source_target_pairs={{0,96},{16,240},{32,64},{48,208},{64,32},{80,176},{96,0},{112,144}... | collective-permute-start | bytes 221192 | tf_op jit(solution)/shard_map/ppermute | solution.py:381
  10.5 7.4 %collective-permute-start.2 = (f32[144,128]{1,0:T(8,128)S(1)}, f32[144,128]{1,0:T(8,128)S(1)}, u32[]{:S(2)}, u32[]{:S(2)}) collective-permute-start(f32[144,128]{1,0:T(8,128)S(1)} %add.15), channel_id=1, source_target_pairs={{0,64},{16,208},{32,96},{48,240},{64,0},{80,144},{96,32},{112,176}... | collective-permute-start | bytes 221192 | tf_op jit(solution)/shard_map/ppermute | solution.py:381
  11.0 6.8 %collective-permute-start.1 = (f32[144,128]{1,0:T(8,128)S(1)}, f32[144,128]{1,0:T(8,128)S(1)}, u32[]{:S(2)}, u32[]{:S(2)}) collective-permute-start(f32[144,128]{1,0:T(8,128)S(1)} %add.15), channel_id=1, source_target_pairs={{0,32},{16,48},{32,0},{48,16},{64,96},{80,112},{96,64},{112,80},{1... | collective-permute-start | bytes 221192 | tf_op jit(solution)/shard_map/ppermute | solution.py:381
  12.1 2.8 %collective-permute-start.4 = (f32[8,128]{1,0:T(8,128)S(1)}, f32[8,128]{1,0:T(8,128)S(1)}, u32[]{:S(2)}, u32[]{:S(2)}) collective-permute-start(f32[8,128]{1,0:T(8,128)S(1)} %broadcast_in_dim.37), channel_id=1, source_target_pairs={{0,1},{1,0},{2,3},{3,2},{4,5},{5,4},{6,7},{7,6},{8,9},{9,8},{10,11... | collective-permute-start | bytes 12296 | tf_op jit(solution)/shard_map/ppermute | solution.py:370
  17.9 5.4 %collective-permute-start.5 = (f32[144,128]{1,0:T(8,128)S(1)}, f32[144,128]{1,0:T(8,128)S(1)}, u32[]{:S(2)}, u32[]{:S(2)}) collective-permute-start(f32[144,128]{1,0:T(8,128)S(1)} %add_add_fusion.total_ref), channel_id=1, source_target_pairs={{0,224},{16,112},{32,192},{48,80},{64,160},{80,48},{96,128},{112,1... | collective-permute-start | bytes 221192 | tf_op jit(solution)/shard_map/ppermute | solution.py:381
  19.6 3.7 %collective-permute-start.6 = (f32[8,128]{1,0:T(8,128)S(1)}, f32[8,128]{1,0:T(8,128)S(1)}, u32[]{:S(2)}, u32[]{:S(2)}) collective-permute-start(f32[8,128]{1,0:T(8,128)S(1)} %max.3.peaks_ref), channel_id=1, source_target_pairs={{0,3},{1,2},{2,1},{3,0},{4,7},{5,6},{6,5},{7,4},{8,11},{9,10},{10,... | collective-permute-start | bytes 12296 | tf_op jit(solution)/shard_map/ppermute | solution.py:370
  23.3 25.8 %copy-start.2 = (bf16[4,512,512]{2,1,0:T(8,128)(2,1)S(1)}, bf16[4,512,512]{2,1,0:T(8,128)(2,1)}, u32[]{:S(2)}) copy-start(bf16[4,512,512]{2,1,0:T(8,128)(2,1)} %momentum_ref.1) | copy-start | bytes 6291460
  23.3 25.8 %copy-start.3 = (bf16[4,512,512]{2,1,0:T(8,128)(2,1)S(1)}, bf16[4,512,512]{2,1,0:T(8,128)(2,1)}, u32[]{:S(2)}) copy-start(bf16[4,512,512]{2,1,0:T(8,128)(2,1)} %gradient_ref.1) | copy-start | bytes 6291460
  23.3 5.8 %collective-permute-start.12 = (f32[152,128]{1,0:T(8,128)S(1)}, f32[152,128]{1,0:T(8,128)S(1)}, u32[]{:S(2)}, u32[]{:S(2)}) collective-permute-start(f32[152,128]{1,0:T(8,128)S(1)} %shard_map.69.refs_0_), channel_id=1, source_target_pairs={{0,8},{4,12},{8,0},{12,4},{1,9},{5,13},{9,1},{13,5},{2,10},{6,14},... | collective-permute-start | bytes 233480 | tf_op jit(solution)/shard_map/ppermute | solution.py:370
  26.3 4.5 %collective-permute-start.10 = (f32[152,128]{1,0:T(8,128)S(1)}, f32[152,128]{1,0:T(8,128)S(1)}, u32[]{:S(2)}, u32[]{:S(2)}) collective-permute-start(f32[152,128]{1,0:T(8,128)S(1)} %shard_map.69.refs_0_), channel_id=1, source_target_pairs={{0,12},{4,8},{8,4},{12,0},{1,13},{5,9},{9,5},{13,1},{2,14},{6,10},... | collective-permute-start | bytes 233480 | tf_op jit(solution)/shard_map/ppermute | solution.py:370
  27.1 6.5 %collective-permute-start.8 = (f32[152,128]{1,0:T(8,128)S(1)}, f32[152,128]{1,0:T(8,128)S(1)}, u32[]{:S(2)}, u32[]{:S(2)}) collective-permute-start(f32[152,128]{1,0:T(8,128)S(1)} %shard_map.69.refs_0_), channel_id=1, source_target_pairs={{0,4},{4,0},{8,12},{12,8},{1,5},{5,1},{9,13},{13,9},{2,6},{6,2},{1... | collective-permute-start | bytes 233480 | tf_op jit(solution)/shard_map/ppermute | solution.py:370
  27.1 6.5 %collective-permute-start.7 = (f32[152,128]{1,0:T(8,128)S(1)}, f32[152,128]{1,0:T(8,128)S(1)}, u32[]{:S(2)}, u32[]{:S(2)}) collective-permute-start(f32[152,128]{1,0:T(8,128)S(1)} %shard_map.69.refs_0_), channel_id=1, source_target_pairs={{0,16},{16,0},{32,48},{48,32},{64,80},{80,64},{96,112},{112,96},{1... | collective-permute-start | bytes 233480 | tf_op jit(solution)/shard_map/ppermute | solution.py:370
  29.0 4.6 %collective-permute-start.13 = (f32[152,128]{1,0:T(8,128)S(1)}, f32[152,128]{1,0:T(8,128)S(1)}, u32[]{:S(2)}, u32[]{:S(2)}) collective-permute-start(f32[152,128]{1,0:T(8,128)S(1)} %collective-permute-done.12.refs_6_), channel_id=1, source_target_pairs={{0,16},{16,0},{32,48},{48,32},{64,80},{80,64},{96,112},{112,96},{1... | collective-permute-start | bytes 233480 | tf_op jit(solution)/shard_map/ppermute | solution.py:370
  30.8 3.7 %collective-permute-start.11 = (f32[152,128]{1,0:T(8,128)S(1)}, f32[152,128]{1,0:T(8,128)S(1)}, u32[]{:S(2)}, u32[]{:S(2)}) collective-permute-start(f32[152,128]{1,0:T(8,128)S(1)} %collective-permute-done.10.refs_4_), channel_id=1, source_target_pairs={{0,16},{16,0},{32,48},{48,32},{64,80},{80,64},{96,112},{112,96},{1... | collective-permute-start | bytes 233480 | tf_op jit(solution)/shard_map/ppermute | solution.py:370
  33.6 1.3 %collective-permute-start.9 = (f32[152,128]{1,0:T(8,128)S(1)}, f32[152,128]{1,0:T(8,128)S(1)}, u32[]{:S(2)}, u32[]{:S(2)}) collective-permute-start(f32[152,128]{1,0:T(8,128)S(1)} %collective-permute-done.8.refs_2_), channel_id=1, source_target_pairs={{0,16},{16,0},{32,48},{48,32},{64,80},{80,64},{96,112},{112,96},{1... | collective-permute-start | bytes 233480 | tf_op jit(solution)/shard_map/ppermute | solution.py:370
  46.3 5.7 %collective-permute-start.14 = (bf16[656,128]{1,0:T(8,128)(2,1)S(1)}, bf16[656,128]{1,0:T(8,128)(2,1)S(1)}, u32[]{:S(2)}, u32[]{:S(2)}) collective-permute-start(bf16[656,128]{1,0:T(8,128)(2,1)S(1)} %get-tuple-element.30.first_ref), channel_id=1, source_target_pairs={{0,1},{1,0},{2,3},{3,2},{16,19},{17,18},{18,17},{19,16},{32,33},{3... | collective-permute-start | bytes 503816 | tf_op jit(solution)/shard_map/ppermute | solution.py:391
  48.9 5.8 %collective-permute-start.16 = (bf16[656,128]{1,0:T(8,128)(2,1)S(1)}, bf16[656,128]{1,0:T(8,128)(2,1)S(1)}, u32[]{:S(2)}, u32[]{:S(2)}) collective-permute-start(bf16[656,128]{1,0:T(8,128)(2,1)S(1)} %get-tuple-element.34.second_ref), channel_id=1, source_target_pairs={{0,1},{1,0},{2,3},{3,2},{16,19},{17,18},{18,17},{19,16},{32,33},{3... | collective-permute-start | bytes 503816 | tf_op jit(solution)/shard_map/ppermute | solution.py:391
  50.5 8.0 %copy-start.1 = (bf16[4,512,512]{2,1,0:T(8,128)(2,1)}, bf16[4,512,512]{2,1,0:T(8,128)(2,1)S(1)}, u32[]{:S(2)}) copy-start(bf16[4,512,512]{2,1,0:T(8,128)(2,1)S(1)} %add_convert_fusion.momentum_ref) | copy-start | bytes 6291460
  52.0 4.8 %collective-permute-start.15 = (bf16[656,128]{1,0:T(8,128)(2,1)S(1)}, bf16[656,128]{1,0:T(8,128)(2,1)S(1)}, u32[]{:S(2)}, u32[]{:S(2)}) collective-permute-start(bf16[656,128]{1,0:T(8,128)(2,1)S(1)} %collective-permute-done.14.first_ref), channel_id=1, source_target_pairs={{0,3},{1,2},{2,1},{3,0},{16,17},{17,16},{18,19},{19,18},{32,35},{3... | collective-permute-start | bytes 503816 | tf_op jit(solution)/shard_map/ppermute | solution.py:391
  52.3 6.2 %collective-permute-start.19 = (bf16[656,128]{1,0:T(8,128)(2,1)S(1)}, bf16[656,128]{1,0:T(8,128)(2,1)S(1)}, u32[]{:S(2)}, u32[]{:S(2)}) collective-permute-start(bf16[656,128]{1,0:T(8,128)(2,1)S(1)} %collective-permute-done.14.first_ref), channel_id=1, source_target_pairs={{0,16},{16,0},{32,48},{48,32},{64,80},{80,64},{96,112},{112,96},{1... | collective-permute-start | bytes 503816 | tf_op jit(solution)/shard_map/ppermute | solution.py:370
  54.7 3.8 %collective-permute-start.18 = (bf16[656,128]{1,0:T(8,128)(2,1)S(1)}, bf16[656,128]{1,0:T(8,128)(2,1)S(1)}, u32[]{:S(2)}, u32[]{:S(2)}) collective-permute-start(bf16[656,128]{1,0:T(8,128)(2,1)S(1)} %collective-permute-done.16.second_ref), channel_id=1, source_target_pairs={{0,16},{16,0},{32,48},{48,32},{64,80},{80,64},{96,112},{112,96},{1... | collective-permute-start | bytes 503816 | tf_op jit(solution)/shard_map/ppermute | solution.py:370
  56.8 2.7 %collective-permute-start.17 = (bf16[656,128]{1,0:T(8,128)(2,1)S(1)}, bf16[656,128]{1,0:T(8,128)(2,1)S(1)}, u32[]{:S(2)}, u32[]{:S(2)}) collective-permute-start(bf16[656,128]{1,0:T(8,128)(2,1)S(1)} %collective-permute-done.15.next_ref.first_ref), channel_id=1, source_target_pairs={{0,16},{16,0},{32,48},{48,32},{64,80},{80,64},{96,112},{112,96},{1... | collective-permute-start | bytes 503816 | tf_op jit(solution)/shard_map/ppermute | solution.py:370
  (2 other events, 6.6 us)
